TPU v7x, 32 devices: a whole 2x2x4 slice. The times are simulated.
32 devices in a mesh: grp: 4 (over y, x), dev: 8 (over z, core).
Axes of the slice: x: 2, y: 2, z: 4, core: 2. Of those that a mesh axis runs over, the one named last changes fastest.
Arguments:
- spectrum: float32 [1152, 8, 128], P(None, 'dev'), may hold values from 0.05 to 2
- sea_mask: int32 [8, 128], P('dev'), may hold values 0 or 1
- wind: float32 [2, 8, 128], P(None, 'dev'), may hold values from -24 to 24
- currents: float32 [4, 2, 4096], P('grp', None, 'dev'), may hold values from -6 to 6
- coupling: int32 [4, 4096], P('grp', 'dev'), may hold values from 0 to 1023, as said below
Outputs:
- updated: float32 [1152, 8, 128], P(None, 'dev')
- cell_drift: float32 [4, 2, 4096], P('grp', None, 'dev')
Inputs may be any that keep to these rules, and one draw needn't show every extreme that they name: `coupling`: an ocean cell's entry names the wave point i * 128 + j that it is averaged into and reads its drift from; cell c lies in grid column i with i equal to c // 512 - 1, c // 512 or c // 512 + 1, periodic over 8 columns. `sea_mask`: 1 marks a sea point.
All inputs are finite; a program needn't handle non-finite values. No bound on the sum of `sea_mask` on one device may be relied on, other than what follows from the above.
Results may differ from a plain program's by a relative error of at most 0.00014.
Values sent between devices are 32-bit elements; how exact they have to be, the bound alone decides.
No kernel may reach another device: no remote copies, remote signals or barrier semaphores. Data moves between devices by JAX's collectives and lax.ppermute only.
A program may use at most 64 MiB of HBM per device.

v0:
```python
import math

import jax
import jax.numpy as jnp
from jax import lax
from jax.sharding import PartitionSpec as P

NDIR = 32


FIRST_FREQ = 0.04
GROWTH = 1.1
SPEED_TOP = 0.45
CURRENT_TOP = 0.2
WIND_GAIN = 0.03
WHITECAP = 0.3
STEEP_SCALE = 0.4
STOKES_GAIN = 3.0


def from_behind(value, axis, steps):
    count = lax.axis_size(axis)
    pairs = [(source, (source + steps) % count) for source in range(count)]
    return lax.ppermute(value, axis, pairs)


def with_halo(cells, sides, width):
    for axis, dim in sides:
        count = lax.axis_size(axis)
        head = lax.slice_in_dim(cells, 0, width, axis=dim)
        tail = lax.slice_in_dim(cells, cells.shape[dim] - width, cells.shape[dim], axis=dim)
        cells = jnp.concatenate(
            [
                lax.ppermute(tail, axis, [(i, (i + 1) % count) for i in range(count)]),
                cells,
                lax.ppermute(head, axis, [((i + 1) % count, i) for i in range(count)]),
            ],
            axis=dim,
        )
    return cells


def bin_tables(bin_index):
    freq_level = (bin_index // NDIR).astype(jnp.float32)
    heading = (bin_index % NDIR).astype(jnp.float32) * (2.0 * math.pi / NDIR)
    frequency = FIRST_FREQ * GROWTH**freq_level
    group_speed = SPEED_TOP * FIRST_FREQ / frequency
    return (frequency, jnp.cos(heading), jnp.sin(heading), group_speed)


def column(values):
    return values[:, None, None]


def sources(energy, sea_frac, wind, mean_current, frequency, cosine_dir, sine_dir):
    energy = energy * sea_frac
    spacing = 0.1 * frequency
    total_energy = jnp.sum(energy * column(spacing), axis=0)
    moment = jnp.sum(energy * column(spacing * frequency), axis=0)
    is_sea = sea_frac > 0.5
    safe_total = jnp.where(is_sea, total_energy, 1.0)
    mean_freq = jnp.where(is_sea, moment / safe_total, 1.0)
    steepness = STEEP_SCALE * total_energy * mean_freq**4
    damping = WHITECAP * (column(frequency) / mean_freq) ** 2 * steepness**2
    along_wind = column(cosine_dir) * (wind[0] - mean_current[0]) + column(sine_dir) * (
        wind[1] - mean_current[1]
    )
    growth = WIND_GAIN * jnp.maximum(0.64 * column(frequency) * along_wind - 1.0, 0.0)
    return energy * (1.0 + growth) / (1.0 + damping)


def transport(
    west_energy,
    centre,
    east_energy,
    west_flow,
    centre_flow,
    east_flow,
    group_speed,
    cosine_dir,
    sine_dir,
    sea_frac,
):
    speed_x = column(group_speed * cosine_dir)
    speed_y = column(group_speed * sine_dir)
    face_east = 0.5 * (speed_x + centre_flow[0] + (speed_x + east_flow[0]))
    face_west = 0.5 * (speed_x + west_flow[0] + (speed_x + centre_flow[0]))
    flux_east = jnp.maximum(face_east, 0.0) * centre + jnp.minimum(face_east, 0.0) * east_energy
    flux_west = jnp.maximum(face_west, 0.0) * west_energy + jnp.minimum(face_west, 0.0) * centre
    speed_north = speed_y + centre_flow[1]
    face_north = 0.5 * (speed_north[:, :, :-1] + speed_north[:, :, 1:])
    flux_north = (
        jnp.maximum(face_north, 0.0) * centre[:, :, :-1]
        + jnp.minimum(face_north, 0.0) * centre[:, :, 1:]
    )
    flux_north = jnp.pad(flux_north, ((0, 0), (0, 0), (1, 1)))
    return sea_frac * (
        centre - (flux_east - flux_west) - (flux_north[:, :, 1:] - flux_north[:, :, :-1])
    )


def stokes_table(frequency, cosine_dir, sine_dir):
    weight = STOKES_GAIN * 0.1 * frequency**4
    return jnp.stack([weight * cosine_dir, weight * sine_dir])


def body(spectrum, sea_mask, wind, currents, coupling):
    bin_count = spectrum.shape[0]
    width_y = spectrum.shape[2]
    devices = lax.axis_size("dev")
    device_index = lax.axis_index("dev")
    is_ocean = lax.axis_index("grp") > 0
    cell_values = jnp.concatenate([currents[0], jnp.ones_like(currents[0, :1])], axis=0)
    cell_values = jnp.where(is_ocean, cell_values, 0.0)
    target_col = coupling[0] // width_y
    target_row = coupling[0] % width_y
    band_slot = (target_col - device_index + devices + 1) % devices
    band_index = band_slot * width_y + target_row
    partial_value = jax.ops.segment_sum(cell_values.T, band_index, num_segments=3 * width_y)
    partial_value = partial_value.T.reshape(3, 3, width_y)
    from_west = from_behind(partial_value[:, 2], "dev", 1)
    from_east = from_behind(partial_value[:, 0], "dev", -1)
    owned_sums = (partial_value[:, 1] + from_west + from_east)[:, None, :]
    group_sums = lax.psum(owned_sums, "grp")
    mean_current = group_sums[:2] / jnp.maximum(group_sums[2], 1.0)
    flow_local = CURRENT_TOP * jnp.tanh(mean_current)
    sea_frac = sea_mask.astype(jnp.float32)
    frequency, cosine_dir, sine_dir, group_speed = bin_tables(
        jnp.arange(bin_count, dtype=jnp.int32)
    )
    forced = sources(spectrum, sea_frac, wind, mean_current, frequency, cosine_dir, sine_dir)
    widened = with_halo(jnp.concatenate([forced, flow_local], axis=0), (("dev", 1),), 1)
    updated = transport(
        widened[:bin_count, 0:1],
        forced,
        widened[:bin_count, 2:3],
        widened[bin_count:, 0:1],
        flow_local,
        widened[bin_count:, 2:3],
        group_speed,
        cosine_dir,
        sine_dir,
        sea_frac,
    )
    stokes_weights = stokes_table(frequency, cosine_dir, sine_dir)
    local_drift = jnp.dot(
        stokes_weights, updated.reshape(bin_count, -1), precision=lax.Precision.HIGHEST
    ).reshape(2, 1, width_y)
    band_drift = with_halo(local_drift, (("dev", 1),), 1)
    cell_drift = band_drift.reshape(2, -1)[:, band_index]
    cell_drift = jnp.where(is_ocean, cell_drift, 0.0)[None]
    return (updated, cell_drift)


def solution(mesh):
    return jax.shard_map(
        body,
        mesh=mesh,
        in_specs=(
            P(None, "dev", None),
            P("dev", None),
            P(None, "dev", None),
            P("grp", None, "dev"),
            P("grp", "dev"),
        ),
        out_specs=(P(None, "dev", None), P("grp", None, "dev")),
        check_vma=False,
    )
```

profile of v0, /device:TPU:0, one launch (start us, length us, event | category | flops | bytes accessed | tf_op | source)
XLA Modules:
  0.0 65.5 jit_solution(131562197040564361)
XLA Ops:
  0.6 0.0 copy-start.3
  0.6 0.0 copy-start
  0.7 0.8 %select_bitcast_fusion.1 = f32[512,3]{0,1:T(4,128)S(1)} fusion(f32[2,512]{1,0:T(2,128)} %bitcast.75, pred[]{:T(512)S(6)} %gt.9), kind=kLoop, calls=%fused_computation.65 | loop fusion | flops 1536 | bytes 10241 | tf_op jit(solution)/shard_map/transpose | solution.py:119
  1.4 0.1 copy.12
  1.6 0.7 %compare_select_fusion = (s32[512,1]{0,1:T(1,128)S(1)}, s32[512,1]{0,1:T(1,128)S(1)}) fusion(s32[]{:T(128)S(6)} %axis_index.22, s32[1,512]{1,0:T(1,128)} %param.9), kind=kLoop, calls=%fused_computation.44 | loop fusion | flops 18944 | bytes 6148 | tf_op jit(solution)/shard_map/select_n | solution.py:150
  2.3 2.3 %scatter_custom_fusion = f32[384,3]{1,0:T(8,128)S(1)} fusion(s32[512]{0:T(512)S(1)} %bitcast.78, f32[512,3]{1,0:T(8,128)S(1)} %copy.12, f32[]{:T(128)} %constant.121.clone.1), kind=kCustom, calls=%fused_computation.32 | custom fusion | flops 1536 | bytes 4612 | tf_op jit(solution)/shard_map/scatter-add | solution.py:119
  4.6 0.0 copy-start.2
  4.6 0.1 copy.20
  4.7 4.5 %collective-permute-start.1 = (f32[3,128]{1,0:T(4,128)S(1)}, f32[3,128]{1,0:T(4,128)S(1)}, u32[]{:S(2)}, u32[]{:S(2)}) collective-permute-start(f32[3,128]{1,0:T(4,128)S(1)} %bitcast.76), channel_id=1, source_target_pairs={{0,7},{1,0},{2,1},{3,2},{4,3},{5,4},{6,5},{7,6},{8,15},{9,8},{10,9... | collective-permute-start | bytes 4616 | tf_op jit(solution)/shard_map/ppermute | solution.py:24
  9.2 0.1 copy.19
  9.3 0.0 collective-permute-start
  9.3 0.1 fusion.28
  9.4 0.1 fusion.43
  9.4 0.2 sine_multiply_fusion
  9.6 0.0 copy-done.3
  9.6 0.0 copy-done
  9.6 4.3 %multiply_reduce_fusion.1 = (f32[128]{0:T(128)S(1)}, f32[128]{0:T(128)S(1)}) fusion(f32[1152]{0:T(1024)S(1)} %get-tuple-element.22, f32[1152,1,128]{2,1,0:T(1,128)S(1)} %copy-done, f32[128]{0:T(128)S(1)} %convert_bitcast_fusion, f32[1152]{0:T(1024)S(1)} %get-tuple-element.21), kind=kLoop, calls=%fused_computation.27 | loop fusion | flops 737024 | bytes 600576 | tf_op jit(solution)/shard_map/reduce_sum | solution.py:59
  14.0 0.1 fusion.44
  14.0 0.1 copy.18
  14.1 0.0 collective-permute-done.1
  14.1 0.0 collective-permute-done
  14.1 9.9 %psum.7 = f32[3,1,128]{2,1,0:T(1,128)S(1)} all-reduce(f32[3,1,128]{2,1,0:T(1,128)S(1)} %broadcast_in_dim.16), channel_id=1, replica_groups=mesh['grp'=4,'dev'=8] {'grp'}, use_global_device_ids=true, to_apply=%region_1.2 | all-reduce | flops 384 | bytes 3072 | tf_op jit(solution)/shard_map/psum | solution.py:124
  24.1 0.0 copy-done.2
  24.1 6.3 %fusion.2 = f32[1152,1,128]{2,1,0:T(1,128)S(1)} fusion(f32[1152]{0:T(1024)S(1)} %get-tuple-element.26, f32[128]{0:T(128)S(1)} %get-tuple-element.12, f32[128]{0:T(128)S(1)} %bitcast.73, f32[128]{0:T(128)S(1)} %get-tuple-element.18, f32[128]{0:T(128)S(1)} %get-tuple-element.17, f32[1152]{0:T(1024)S(1)} %get-tuple-element.25, f32[1152]{0:T(1024)S(1)} %get-tuple-element.23, ...), kind=kLoop, calls=%fused_computation.11 | loop fusion | flops 2211840 | bytes 1200640 | tf_op jit(solution)/shard_map/div | solution.py:69
  30.4 1.9 %pad_maximum_fusion = f32[1154,1,128]{2,1,0:T(1,128)S(1)} fusion(f32[2,1,128]{2,1,0:T(1,128)S(1)} %get-tuple-element.10, f32[1152,1,128]{2,1,0:T(1,128)S(1)} %fusion.2), kind=kLoop, calls=%fused_computation.7 | loop fusion | flops 147712 | bytes 1181696 | tf_op jit(solution)/shard_map/concatenate | solution.py:132
  32.3 0.1 collective-permute-start.3
  32.4 3.5 %collective-permute-start.2 = (f32[1154,1,128]{2,1,0:T(1,128)S(1)}, f32[1154,1,128]{2,1,0:T(1,128)S(1)}, u32[]{:S(2)}, u32[]{:S(2)}) collective-permute-start(f32[1154,1,128]{2,1,0:T(1,128)S(1)} %pad_maximum_fusion), channel_id=1, source_target_pairs={{1,0},{2,1},{3,2},{4,3},{5,4},{6,5},{7,6},{0,7},{9,8},{10,9},{11,1... | collective-permute-start | bytes 1772552 | tf_op jit(solution)/shard_map/ppermute | solution.py:36
  35.9 3.2 %broadcast_add_fusion = f32[1152,1,128]{2,1,0:T(1,128)S(1)} fusion(f32[128]{0:T(128)S(1)} %get-tuple-element.20, f32[1152]{0:T(1024)S(1)} %fusion.43), kind=kLoop, calls=%fused_computation.29 | loop fusion | flops 147456 | bytes 594944 | tf_op jit(solution)/shard_map/add | solution.py:90
  39.1 2.6 %fusion.7 = f32[1152,1,127]{2,1,0:T(1,128)S(1)} fusion(f32[1152,1,128]{2,1,0:T(1,128)S(1)} %fusion.2, f32[1152,1,128]{2,1,0:T(1,128)S(1)} %broadcast_add_fusion), kind=kLoop, calls=%fused_computation.17 | loop fusion | flops 1024128 | bytes 2926080 | tf_op jit(solution)/shard_map/add | solution.py:93
  41.7 7.6 %collective-permute-done.3 = f32[1154,1,128]{2,1,0:T(1,128)S(1)} collective-permute-done((f32[1154,1,128]{2,1,0:T(1,128)S(1)}, f32[1154,1,128]{2,1,0:T(1,128)S(1)}, u32[]{:S(2)}, u32[]{:S(2)}) %collective-permute-start.3) | collective-permute-done | bytes 590880 | tf_op jit(solution)/shard_map/ppermute | solution.py:34
  49.4 0.0 collective-permute-done.2
  49.4 8.9 %fusion.12 = f32[1152,1,128]{2,1,0:T(1,128)S(1)} fusion(f32[1152,1,127]{2,1,0:T(1,128)S(1)} %fusion.7, f32[1154,1,128]{2,1,0:T(1,128)S(1)} %collective-permute-done.3, f32[1154,1,128]{2,1,0:T(1,128)S(1)} %collective-permute-done.2, f32[128]{0:T(128)S(1)} %slice_bitcast_fusion.1, f32[128]{0:T(128)S(1)} %slice_bitcast_fusion.2, f32[128]{0:T(128)S(1)} %get-tuple-element.19, ...), kind=kLoop, calls=%fused_computation.28 | loop fusion | flops 5455872 | bytes 2971648 | tf_op jit(solution)/shard_map/mul | solution.py:97
  58.2 0.0 copy-start.1
  58.2 0.4 convolution_bitcast_fusion
  58.6 0.0 collective-permute-start.5
  58.7 0.5 collective-permute-start.4
  59.2 0.8 %collective-permute-done.5 = f32[2,1,128]{2,0,1:T(2,128)S(1)} collective-permute-done((f32[2,1,128]{2,0,1:T(2,128)S(1)}, f32[2,1,128]{2,0,1:T(2,128)S(1)}, u32[]{:S(2)}, u32[]{:S(2)}) %collective-permute-start.5) | collective-permute-done | bytes 1056 | tf_op jit(solution)/shard_map/ppermute | solution.py:36
  60.0 3.6 %collective-permute-done.4 = f32[2,1,128]{2,0,1:T(2,128)S(1)} collective-permute-done((f32[2,1,128]{2,0,1:T(2,128)S(1)}, f32[2,1,128]{2,0,1:T(2,128)S(1)}, u32[]{:S(2)}, u32[]{:S(2)}) %collective-permute-start.4) | collective-permute-done | bytes 1056 | tf_op jit(solution)/shard_map/ppermute | solution.py:34
  63.6 0.1 copy.16
  63.7 1.0 %gather_fusion = f32[512,2]{1,0:T(8,128)S(1)} fusion(f32[2,384]{0,1:T(8,128)S(1)} %copy.16, s32[1024]{0:T(1024)S(1)} %pad_clamp_fusion), kind=kCustom, calls=%fused_computation | custom fusion | bytes 10240 | tf_op jit(solution)/shard_map/gather | solution.py:150
  64.8 0.0 copy-done.1
  64.8 0.7 %copy.17 = f32[1,2,512]{2,1,0:T(2,128)} copy(f32[1,2,512]{1,2,0:T(8,128)S(1)} %select_bitcast_fusion) | data formatting | bytes 8192
  (16 shorter events, 0.1 us)
Async XLA Ops:
  0.6 9.0 %copy-start.3 = (s32[1,128]{1,0:T(1,128)S(1)}, s32[1,128]{1,0:T(1,128)}, u32[]{:S(2)}) copy-start(s32[1,128]{1,0:T(1,128)} %param.6) | copy-start | bytes 1540
  0.6 9.0 %copy-start = (f32[1152,1,128]{2,1,0:T(1,128)S(1)}, f32[1152,1,128]{2,1,0:T(1,128)}, u32[]{:S(2)}) copy-start(f32[1152,1,128]{2,1,0:T(1,128)} %param.5) | copy-start | bytes 1769476
  4.6 19.5 %copy-start.2 = (f32[2,1,128]{2,1,0:T(1,128)S(1)}, f32[2,1,128]{2,1,0:T(1,128)}, u32[]{:S(2)}) copy-start(f32[2,1,128]{2,1,0:T(1,128)} %param.7) | copy-start | bytes 3076
  4.7 9.4 %collective-permute-start.1 = (f32[3,128]{1,0:T(4,128)S(1)}, f32[3,128]{1,0:T(4,128)S(1)}, u32[]{:S(2)}, u32[]{:S(2)}) collective-permute-start(f32[3,128]{1,0:T(4,128)S(1)} %bitcast.76), channel_id=1, source_target_pairs={{0,7},{1,0},{2,1},{3,2},{4,3},{5,4},{6,5},{7,6},{8,15},{9,8},{10,9... | collective-permute-start | bytes 4616 | tf_op jit(solution)/shard_map/ppermute | solution.py:24
  9.3 4.8 %collective-permute-start = (f32[3,128]{1,0:T(4,128)S(1)}, f32[3,128]{1,0:T(4,128)S(1)}, u32[]{:S(2)}, u32[]{:S(2)}) collective-permute-start(f32[3,128]{1,0:T(4,128)S(1)} %bitcast.77), channel_id=1, source_target_pairs={{0,1},{1,2},{2,3},{3,4},{4,5},{5,6},{6,7},{7,0},{8,9},{9,10},{10,1... | collective-permute-start | bytes 4616 | tf_op jit(solution)/shard_map/ppermute | solution.py:24
  32.3 17.1 %collective-permute-start.3 = (f32[1154,1,128]{2,1,0:T(1,128)S(1)}, f32[1154,1,128]{2,1,0:T(1,128)S(1)}, u32[]{:S(2)}, u32[]{:S(2)}) collective-permute-start(f32[1154,1,128]{2,1,0:T(1,128)S(1)} %pad_maximum_fusion), channel_id=1, source_target_pairs={{0,1},{1,2},{2,3},{3,4},{4,5},{5,6},{6,7},{7,0},{8,9},{9,10},{10,1... | collective-permute-start | bytes 1772552 | tf_op jit(solution)/shard_map/ppermute | solution.py:34
  32.4 17.0 %collective-permute-start.2 = (f32[1154,1,128]{2,1,0:T(1,128)S(1)}, f32[1154,1,128]{2,1,0:T(1,128)S(1)}, u32[]{:S(2)}, u32[]{:S(2)}) collective-permute-start(f32[1154,1,128]{2,1,0:T(1,128)S(1)} %pad_maximum_fusion), channel_id=1, source_target_pairs={{1,0},{2,1},{3,2},{4,3},{5,4},{6,5},{7,6},{0,7},{9,8},{10,9},{11,1... | collective-permute-start | bytes 1772552 | tf_op jit(solution)/shard_map/ppermute | solution.py:36
  58.2 6.5 %copy-start.1 = (f32[1152,1,128]{2,1,0:T(1,128)}, f32[1152,1,128]{2,1,0:T(1,128)S(1)}, u32[]{:S(2)}) copy-start(f32[1152,1,128]{2,1,0:T(1,128)S(1)} %fusion.12) | copy-start | bytes 1769476
  58.6 1.3 %collective-permute-start.5 = (f32[2,1,128]{2,0,1:T(2,128)S(1)}, f32[2,1,128]{2,0,1:T(2,128)S(1)}, u32[]{:S(2)}, u32[]{:S(2)}) collective-permute-start(f32[2,1,128]{2,0,1:T(2,128)S(1)} %convolution_bitcast_fusion), channel_id=1, source_target_pairs={{1,0},{2,1},{3,2},{4,3},{5,4},{6,5},{7,6},{0,7},{9,8},{10,9},{11,1... | collective-permute-start | bytes 3080 | tf_op jit(solution)/shard_map/ppermute | solution.py:36
  58.7 4.8 %collective-permute-start.4 = (f32[2,1,128]{2,0,1:T(2,128)S(1)}, f32[2,1,128]{2,0,1:T(2,128)S(1)}, u32[]{:S(2)}, u32[]{:S(2)}) collective-permute-start(f32[2,1,128]{2,0,1:T(2,128)S(1)} %convolution_bitcast_fusion), channel_id=1, source_target_pairs={{0,1},{1,2},{2,3},{3,4},{4,5},{5,6},{6,7},{7,0},{8,9},{9,10},{10,1... | collective-permute-start | bytes 3080 | tf_op jit(solution)/shard_map/ppermute | solution.py:34
where the time goes:
time: 65.7 us; the launch traced here: 65.5 us
  other arithmetic  31.4 us (48%)
  waiting for transfers between devices  12 us (18%)
  blocking collectives  9.91 us (15%)
  starting transfers between devices  8.66 us (13%)
  local copies, waits for them, and re-layouts  2.25 us (3%)
  between operations  0.89 us (1%)
    ppermute x2, waiting for transfers between devices, with_halo(): lax.ppermute(tail, axis, [(i, (i + 1) % count) for i in range(count)])  11.2 us
    psum x1, blocking collectives, body(): group_sums = lax.psum(owned_sums, 'grp')  9.91 us
    mul x2, other arithmetic, transport(): sea_frac * (centre - (flux_east - flux_west) - (flux_north[:, :, 1:] - fl...  8.86 us
    div x1, other arithmetic, sources(): return energy * (1.0 + growth) / (1.0 + damping)  6.29 us
    ppermute x2, starting transfers between devices, from_behind(): return lax.ppermute(value, axis, pairs)  4.53 us
    reduce_sum x1, other arithmetic, sources(): moment = jnp.sum(energy * column(spacing * frequency), axis=0)  4.33 us
    ppermute x2, starting transfers between devices, with_halo(): lax.ppermute(head, axis, [((i + 1) % count, i) for i in range(count)])  3.58 us
    add x1, other arithmetic, transport(): speed_north = speed_y + centre_flow[1]  3.24 us
  transfers between devices with their start and end apart: 6, of which 3 were waited for; matrix products, arithmetic and copies ran while one was open for 16% of the time, Pallas kernels for 0%

commit v1 on v0

v1 whole, which is shorter than its diff:
```python
import functools
import math

import jax
import jax.numpy as jnp
import numpy as np
from jax import lax
from jax.experimental import pallas as pl
from jax.experimental.pallas import tpu as pltpu
from jax.sharding import PartitionSpec as P

NDIR = 32
FIRST_FREQ = 0.04
GROWTH = 1.1
SPEED_TOP = 0.45
CURRENT_TOP = 0.2
WIND_GAIN = 0.03
WHITECAP = 0.3
STEEP_SCALE = 0.4
STOKES_GAIN = 3.0

SLOTS = 4
FIELDS = 8
SUM_X, SUM_Y, COUNT, SEA, WIND_X, WIND_Y, DAMP = range(7)
VMEM = pl.BlockSpec(memory_space=pltpu.VMEM)
SMEM = pl.BlockSpec(memory_space=pltpu.SMEM)


def level_groups(levels):
    for size in (4, 3, 2):
        if levels % size == 0:
            return levels // size, size
    return levels, 1


def slots_of(coupling, width, shape_ref, columns):
    col = lax.div(coupling, jnp.int32(width))
    row = coupling - col * width
    slot = col - shape_ref[0]
    slot = jnp.where(slot < 0, slot + columns, slot)
    slot = jnp.where(slot >= columns, slot - columns, slot)
    return row, slot


def band_kernel(columns, where_ref, coupling_ref, currents_ref, spectrum_ref, sea_ref, wind_ref, band_ref):
    width = spectrum_ref.shape[1]
    bins = spectrum_ref.shape[0]
    is_ocean = where_ref[2] > 0

    @pl.when(is_ocean)
    def _():
        row, slot = slots_of(coupling_ref[...], width, where_ref, columns)
        cells = row.shape[1]
        parts_x, parts_y = [], []
        for comp, parts in ((0, parts_x), (1, parts_y)):
            rest = currents_ref[comp : comp + 1, :]
            for _ in range(3):
                part = rest.astype(jnp.bfloat16).astype(jnp.float32)
                parts.append(part)
                rest = rest - part
        slot_id = lax.broadcasted_iota(jnp.int32, (SLOTS, cells), 0)
        here = jnp.where(slot_id == slot, 1.0, 0.0)
        rows = []
        for part in range(3):
            rows += [here * parts_x[part], here * parts_y[part]]
        rows += [here, jnp.zeros_like(here)]
        values = jnp.concatenate(rows, axis=0).astype(jnp.bfloat16)
        row_id = lax.broadcasted_iota(jnp.int32, (width, cells), 0)
        hot = jnp.where(row_id == row, 1.0, 0.0).astype(jnp.bfloat16)
        sums = lax.dot_general(
            values, hot, (((1,), (1,)), ((), ())), preferred_element_type=jnp.float32
        )
        step = 2 * SLOTS
        band_ref[0:step, :] = sums[0:step] + sums[step : 2 * step] + sums[2 * step : 3 * step]
        band_ref[step : 2 * step, :] = sums[3 * step : 4 * step]
        band_ref[2 * step : 4 * step, :] = jnp.zeros((2 * step, width), jnp.float32)

    @pl.when(jnp.logical_not(is_ocean))
    def _():
        band_ref[...] = jnp.zeros_like(band_ref)
        total = jnp.zeros((8, width), jnp.float32)
        moment = jnp.zeros((8, width), jnp.float32)
        for level in range(bins // NDIR):
            frequency = FIRST_FREQ * GROWTH**level
            block = spectrum_ref[level * NDIR : (level + 1) * NDIR, :]
            block = block[0:8] + block[8:16] + (block[16:24] + block[24:32])
            total += (0.1 * frequency) * block
            moment += (0.1 * frequency * frequency) * block
        sea = sea_ref[...].astype(jnp.float32)
        total = jnp.sum(total, axis=0, keepdims=True) * sea
        moment = jnp.sum(moment, axis=0, keepdims=True) * sea
        is_sea = sea > 0.5
        mean_freq = jnp.where(is_sea, moment / jnp.where(is_sea, total, 1.0), 1.0)
        square = mean_freq * mean_freq
        steep = STEEP_SCALE * total * (square * square)
        damp = WHITECAP * (steep * steep) / square
        own = where_ref[1] + 1
        band_ref[pl.ds(SEA * SLOTS + own, 1), :] = sea
        band_ref[pl.ds(WIND_X * SLOTS + own, 1), :] = wind_ref[0:1, :]
        band_ref[pl.ds(WIND_Y * SLOTS + own, 1), :] = wind_ref[1:2, :]
        band_ref[pl.ds(DAMP * SLOTS + own, 1), :] = damp


def step_kernel(
    where_ref, table_ref, own_ref, mate_ref, other_ref, band_ref, before_ref, after_ref, updated_ref, drift_ref
):
    bins, width = own_ref.shape
    lanes = 8
    odd = where_ref[1]
    slot_own, slot_mate, slot_other = 1 + odd, 2 - odd, 3 * odd

    def field(index, slot):
        base = index * SLOTS
        value = band_ref[pl.ds(base + slot, 1), :]
        low = before_ref[pl.ds(base + jnp.minimum(slot, 1) + 2, 1), :]
        high = after_ref[pl.ds(base + jnp.maximum(slot, 2) - 2, 1), :]
        return value + jnp.where(slot < 2, low, high)

    cosine = [table_ref[8 * k : 8 * k + 8, :] for k in range(4)]
    sine = [table_ref[NDIR + 8 * k : NDIR + 8 * k + 8, :] for k in range(4)]

    def column_state(slot):
        count = jnp.maximum(field(COUNT, slot), 1.0)
        mean_x = field(SUM_X, slot) / count
        mean_y = field(SUM_Y, slot) / count
        rel_x = field(WIND_X, slot) - mean_x
        rel_y = field(WIND_Y, slot) - mean_y
        gain = WIND_GAIN * 0.64
        along = [(gain * rel_x) * cosine[k] + (gain * rel_y) * sine[k] for k in range(4)]
        sea = jnp.broadcast_to(field(SEA, slot), (lanes, width))
        damp = jnp.broadcast_to(field(DAMP, slot), (lanes, width))
        return mean_x, mean_y, along, sea, damp

    own_x, own_y, along_own, sea_own, damp_own = column_state(slot_own)
    mate_x, _, along_mate, sea_mate, damp_mate = column_state(slot_mate)
    other_x, _, along_other, sea_other, damp_other = column_state(slot_other)
    flow_x = CURRENT_TOP * jnp.tanh(own_x)
    flow_y = CURRENT_TOP * jnp.tanh(own_y)
    sign = jnp.where(odd > 0, 1.0, -1.0)
    face_mate = jnp.broadcast_to(
        (0.5 * sign) * (flow_x + CURRENT_TOP * jnp.tanh(mate_x)), (lanes, width)
    )
    face_other = jnp.broadcast_to(
        (-0.5 * sign) * (flow_x + CURRENT_TOP * jnp.tanh(other_x)), (lanes, width)
    )
    flow_y = jnp.broadcast_to(flow_y, (lanes, width))
    face_north = 0.5 * (flow_y + pltpu.roll(flow_y, width - 1, 1))
    inner = jnp.where(
        lax.broadcasted_iota(jnp.int32, (lanes, width), 1) < width - 1, 1.0, 0.0
    )
    signed_cosine = [sign * cosine[k] for k in range(4)]
    outer_count, inner_count = level_groups(bins // NDIR)

    def level_step(index, carry):
        frequency, speed, sums = carry
        sums = list(sums)
        for sub in range(inner_count):
            square = frequency * frequency
            scale_own = sea_own / (1.0 + square * damp_own)
            scale_mate = sea_mate / (1.0 + square * damp_mate)
            scale_other = sea_other / (1.0 + square * damp_other)
            weight = (STOKES_GAIN * 0.1) * (square * square)
            base = (index * inner_count + sub) * NDIR
            for k in range(4):
                rows = pl.ds(pl.multiple_of(base + 8 * k, 8), 8)

                def forced_of(ref, scale, along):
                    grown = jnp.maximum(frequency * along[k] + (1.0 - WIND_GAIN), 1.0)
                    return (ref[rows, :] * scale) * grown

                forced = forced_of(own_ref, scale_own, along_own)
                forced_mate = forced_of(mate_ref, scale_mate, along_mate)
                forced_other = forced_of(other_ref, scale_other, along_other)
                speed_x = speed * signed_cosine[k]
                q_mate = face_mate + speed_x
                q_other = face_other - speed_x
                in_mate = jnp.maximum(q_mate, 0.0)
                in_other = jnp.maximum(q_other, 0.0)
                out = (in_mate - q_mate) + (in_other - q_other)
                north = speed * sine[k] + face_north
                flux = (
                    jnp.maximum(north, 0.0) * forced
                    + jnp.minimum(north, 0.0) * pltpu.roll(forced, width - 1, 1)
                ) * inner
                new = forced - out * forced + (in_mate * forced_mate + in_other * forced_other)
                new = (new - (flux - pltpu.roll(flux, 1, 1))) * sea_own
                updated_ref[rows, :] = new
                sums[k] = sums[k] + weight * new
            frequency = frequency * GROWTH
            speed = speed * (1.0 / GROWTH)
        return frequency, speed, tuple(sums)

    zero = jnp.zeros((lanes, width), jnp.float32)
    start = (jnp.float32(FIRST_FREQ), jnp.float32(SPEED_TOP), (zero,) * 4)
    _, _, sums = lax.fori_loop(0, outer_count, level_step, start)
    drift_x = sums[0] * cosine[0]
    drift_y = sums[0] * sine[0]
    for k in range(1, 4):
        drift_x = drift_x + sums[k] * cosine[k]
        drift_y = drift_y + sums[k] * sine[k]
    drift_ref[0:1, :] = jnp.sum(drift_x, axis=0, keepdims=True)
    drift_ref[1:2, :] = jnp.sum(drift_y, axis=0, keepdims=True)
    drift_ref[2:8, :] = jnp.zeros((6, width), jnp.float32)


def pick_kernel(columns, where_ref, coupling_ref, own_ref, mate_ref, other_ref, cells_ref):
    width = own_ref.shape[1]
    odd = where_ref[1]
    ocean = jnp.where(where_ref[2] > 0, 1.0, 0.0)
    for start in range(0, coupling_ref.shape[1], width):
        part = pl.ds(start, width)
        row, slot = slots_of(coupling_ref[:, part], width, where_ref, columns)
        row = jnp.broadcast_to(row, (8, width))
        own = jnp.take_along_axis(own_ref[...], row, axis=1)[0:2]
        mate = jnp.take_along_axis(mate_ref[...], row, axis=1)[0:2]
        other = jnp.take_along_axis(other_ref[...], row, axis=1)[0:2]
        value = jnp.where(slot == 1 + odd, own, jnp.where(slot == 2 - odd, mate, other))
        cells_ref[:, part] = value * ocean


def direction_table(width):
    heading = np.arange(NDIR) * (2.0 * math.pi / NDIR)
    table = np.concatenate([np.cos(heading), np.sin(heading)]).astype(np.float32)
    return jnp.asarray(np.repeat(table[:, None], width, axis=1))


def body(spectrum, sea_mask, wind, currents, coupling):
    bins, _, width = spectrum.shape
    devices = lax.axis_size("dev")
    groups = lax.axis_size("grp")
    me = lax.axis_index("dev")
    odd = me % 2
    first = me - odd - 1
    where = jnp.stack([first, odd, lax.axis_index("grp")]).astype(jnp.int32)
    mates = [(i, i ^ 1) for i in range(devices)]
    others = [(i, (i + (1 if i % 2 else -1)) % devices) for i in range(devices)]

    def shifted(value, steps):
        return lax.ppermute(value, "dev", [(i, (i + steps) % devices) for i in range(devices)])

    own = spectrum.reshape(bins, width)
    other = lax.ppermute(own, "dev", others)
    mate = lax.ppermute(own, "dev", mates)

    band = pl.pallas_call(
        functools.partial(band_kernel, devices),
        out_shape=jax.ShapeDtypeStruct((FIELDS * SLOTS, width), jnp.float32),
        in_specs=[SMEM] + [VMEM] * 5,
        out_specs=VMEM,
    )(where, coupling, currents[0], own, sea_mask, wind[:, 0])
    band = band + lax.ppermute(band, "dev", mates)
    reach = 1
    while reach < groups:
        band = band + lax.ppermute(band, "grp", [(i, i ^ reach) for i in range(groups)])
        reach *= 2
    before = shifted(band, 2)
    after = shifted(band, -2)

    updated, drift = pl.pallas_call(
        step_kernel,
        out_shape=(
            jax.ShapeDtypeStruct((bins, width), jnp.float32),
            jax.ShapeDtypeStruct((8, width), jnp.float32),
        ),
        in_specs=[SMEM] + [VMEM] * 7,
        out_specs=(VMEM, VMEM),
    )(where, direction_table(width), own, mate, other, band, before, after)

    drift_other = lax.ppermute(drift, "dev", others)
    drift_mate = lax.ppermute(drift, "dev", mates)
    cells = pl.pallas_call(
        functools.partial(pick_kernel, devices),
        out_shape=jax.ShapeDtypeStruct(currents.shape[1:], jnp.float32),
        in_specs=[SMEM] + [VMEM] * 4,
        out_specs=VMEM,
    )(where, coupling, drift, drift_mate, drift_other)
    return updated.reshape(spectrum.shape), cells[None]


def solution(mesh):
    return jax.shard_map(
        body,
        mesh=mesh,
        in_specs=(
            P(None, "dev", None),
            P("dev", None),
            P(None, "dev", None),
            P("grp", None, "dev"),
            P("grp", "dev"),
        ),
        out_specs=(P(None, "dev", None), P("grp", None, "dev")),
        check_vma=False,
    )
```

time: 65.7 us -> 37.2 us (0.57)
  other arithmetic: 31.4 us -> 1.35 us
  blocking collectives: 9.91 us -> 0 us
  Pallas kernels: 0 us -> 7.25 us
  waiting for transfers between devices: 12 us -> 14.5 us
  starting transfers between devices: 8.66 us -> 10.3 us
    psum x1 -> x0, blocking collectives: 9.91 us -> none  [body(): group_sums = lax.psum(owned_sums, 'grp')]
    mul x10 -> x0, other arithmetic: 9.19 us -> none  [the longest x2 8.86 us: transport(): sea_frac * (centre - (flux_east - flux_west) - (flux_north[:, :, 1:] - fl...]
    pallas_call x0 -> x3, Pallas kernels: none -> 7.25 us  [the longest x1 3.94 us: body(): pl.pallas_call(step_kernel, out_shape=(jax.ShapeDtypeStruct((bins, width)...]
    div x2 -> x0, other arithmetic: 6.29 us -> none  [the longest x1 6.29 us: sources(): return energy * (1.0 + growth) / (1.0 + damping)]
    add x3, other arithmetic: 5.85 us -> 0.73 us  [the longest x1 0.72 us: body(): band = band + lax.ppermute(band, 'dev', mates)]
    reduce_sum x1 -> x0, other arithmetic: 4.33 us -> none  [sources(): moment = jnp.sum(energy * column(spacing * frequency), axis=0)]
    ppermute x6 -> x9, waiting for transfers between devices: 12 us -> 14.5 us  [the longest x1 5.03 us: body(): drift_other = lax.ppermute(drift, 'dev', others)]
    scatter-add x1 -> x0, other arithmetic: 2.3 us -> none  [body(): jax.ops.segment_sum(cell_values.T, band_index, num_segments=3 * width_y)]
  transfers between devices with their start and end apart: 6 -> 9, of which waited for: 3 -> 6; matrix products, arithmetic and copies ran while one was open for 16% -> 4% of each run, Pallas kernels for 0% -> 5%
where the time goes in v1:
time: 37.2 us; the launch traced here: 36.9 us
  waiting for transfers between devices  14.5 us (39%)
  starting transfers between devices  10.3 us (28%)
  Pallas kernels  7.25 us (19%)
  local copies, waits for them, and re-layouts  2.81 us (8%)
  other arithmetic  1.35 us (4%)
  between operations  0.67 us (2%)
    ppermute x1, waiting for transfers between devices, body(): drift_other = lax.ppermute(drift, 'dev', others)  5.03 us
    ppermute x1, starting transfers between devices, body(): other = lax.ppermute(own, 'dev', others)  4.55 us
    ppermute x2, waiting for transfers between devices, body(): lax.ppermute(band, 'grp', [(i, i ^ reach) for i in range(groups)])  4.3 us
    ppermute x2, waiting for transfers between devices, shifted(): lax.ppermute(value, 'dev', [(i, (i + steps) % devices) for i in range(dev...  4.15 us
    pallas_call x1, Pallas kernels, body(): pl.pallas_call(step_kernel, out_shape=(jax.ShapeDtypeStruct((bins, width)...  3.94 us
    ppermute x2, starting transfers between devices, body(): lax.ppermute(band, 'grp', [(i, i ^ reach) for i in range(groups)])  3.18 us
    unnamed x14, local copies, waits for them, and re-layouts  2.81 us
    ppermute x2, starting transfers between devices, shifted(): lax.ppermute(value, 'dev', [(i, (i + steps) % devices) for i in range(dev...  2.03 us
  transfers between devices with their start and end apart: 9, of which 6 were waited for; matrix products, arithmetic and copies ran while one was open for 4% of the time, Pallas kernels for 5%

profile of v1, /device:TPU:0, one launch (start us, length us, event | category | flops | bytes accessed | tf_op | source)
XLA Modules:
  0.0 36.9 jit_solution(16882738355195548422)
XLA Ops:
  0.6 4.6 %collective-permute-start.1 = (f32[1152,128]{1,0:T(8,128)}, f32[1152,128]{1,0:T(8,128)S(1)}, u32[]{:S(2)}, u32[]{:S(2)}) collective-permute-start(f32[1152,128]{1,0:T(8,128)} %bitcast.10), channel_id=1, source_target_pairs={{0,7},{1,2},{2,1},{3,4},{4,3},{5,6},{6,5},{7,0},{8,15},{9,10},{10,... | collective-permute-start | bytes 1769480 | tf_op jit(solution)/shard_map/ppermute | solution.py:242
  5.2 0.0 collective-permute-start
  5.2 0.6 %pad_add_fusion.where_ref = s32[3]{0:T(128)} fusion(s32[1]{0:T(128)} %bitcast.2, s32[1]{0:T(128)} %bitcast.1, s32[1]{0:T(128)} %bitcast), kind=kLoop, calls=%fused_computation | loop fusion | flops 6 | bytes 24 | tf_op jit(solution)/shard_map/stack | solution.py:234
  5.8 1.8 %shard_map.77 = f32[32,128]{1,0:T(8,128)} custom-call(s32[3]{0:T(128)} %pad_add_fusion.where_ref, s32[1,512]{1,0:T(1,128)} %coupling_ref.3, f32[2,512]{1,0:T(2,128)} %bitcast.14, f32[1152,128]{1,0:T(8,128)} %bitcast.12, s32[1,128]{1,0:T(1,128)} %sea_ref.1, f32[2,128]{1,0:T(2,128)} %bitcast.16), custom_call_target="tpu_custom_call" | custom-call | tf_op jit(solution)/shard_map/pallas_call | solution.py:245
  7.6 0.5 %collective-permute-start.2 = (f32[32,128]{1,0:T(8,128)}, f32[32,128]{1,0:T(8,128)S(1)}, u32[]{:S(2)}, u32[]{:S(2)}) collective-permute-start(f32[32,128]{1,0:T(8,128)} %shard_map.77), channel_id=1, source_target_pairs={{0,1},{1,0},{2,3},{3,2},{4,5},{5,4},{6,7},{7,6},{8,9},{9,8},{10,11... | collective-permute-start | bytes 49160 | tf_op jit(solution)/shard_map/ppermute | solution.py:251
  8.1 1.0 %collective-permute-done.2 = f32[32,128]{1,0:T(8,128)S(1)} collective-permute-done((f32[32,128]{1,0:T(8,128)}, f32[32,128]{1,0:T(8,128)S(1)}, u32[]{:S(2)}, u32[]{:S(2)}) %collective-permute-start.2) | collective-permute-done | bytes 16416 | tf_op jit(solution)/shard_map/ppermute | solution.py:251
  9.2 0.7 %add.15 = f32[32,128]{1,0:T(8,128)S(1)} add(f32[32,128]{1,0:T(8,128)} %shard_map.77, f32[32,128]{1,0:T(8,128)S(1)} %collective-permute-done.2) | non-fusion elementwise | flops 4096 | bytes 49152 | tf_op jit(solution)/shard_map/add | solution.py:251
  9.9 1.6 %collective-permute-start.3 = (f32[32,128]{1,0:T(8,128)S(1)}, f32[32,128]{1,0:T(8,128)S(1)}, u32[]{:S(2)}, u32[]{:S(2)}) collective-permute-start(f32[32,128]{1,0:T(8,128)S(1)} %add.15), channel_id=1, source_target_pairs={{0,8},{8,0},{16,24},{24,16},{1,9},{9,1},{17,25},{25,17},{2,10},{10... | collective-permute-start | bytes 49160 | tf_op jit(solution)/shard_map/ppermute | solution.py:254
  11.5 2.2 %collective-permute-done.3 = f32[32,128]{1,0:T(8,128)S(1)} collective-permute-done((f32[32,128]{1,0:T(8,128)S(1)}, f32[32,128]{1,0:T(8,128)S(1)}, u32[]{:S(2)}, u32[]{:S(2)}) %collective-permute-start.3) | collective-permute-done | bytes 16416 | tf_op jit(solution)/shard_map/ppermute | solution.py:254
  13.6 1.6 %collective-permute-start.4 = (f32[32,128]{1,0:T(8,128)S(1)}, f32[32,128]{1,0:T(8,128)S(1)}, u32[]{:S(2)}, u32[]{:S(2)}) collective-permute-start(f32[32,128]{1,0:T(8,128)S(1)} %add.16), channel_id=1, source_target_pairs={{0,16},{8,24},{16,0},{24,8},{1,17},{9,25},{17,1},{25,9},{2,18},{10... | collective-permute-start | bytes 49160 | tf_op jit(solution)/shard_map/ppermute | solution.py:254
  15.2 2.1 %collective-permute-done.4 = f32[32,128]{1,0:T(8,128)S(1)} collective-permute-done((f32[32,128]{1,0:T(8,128)S(1)}, f32[32,128]{1,0:T(8,128)S(1)}, u32[]{:S(2)}, u32[]{:S(2)}) %collective-permute-start.4) | collective-permute-done | bytes 16416 | tf_op jit(solution)/shard_map/ppermute | solution.py:254
  17.4 0.0 copy-start.2
  17.4 0.6 %collective-permute-start.6 = (f32[32,128]{1,0:T(8,128)S(1)}, f32[32,128]{1,0:T(8,128)S(1)}, u32[]{:S(2)}, u32[]{:S(2)}) collective-permute-start(f32[32,128]{1,0:T(8,128)S(1)} %add.17.band_ref), channel_id=1, source_target_pairs={{0,6},{1,7},{2,0},{3,1},{4,2},{5,3},{6,4},{7,5},{8,14},{9,15},{10,... | collective-permute-start | bytes 49160 | tf_op jit(solution)/shard_map/ppermute | solution.py:239
  18.0 1.4 %collective-permute-start.5 = (f32[32,128]{1,0:T(8,128)S(1)}, f32[32,128]{1,0:T(8,128)S(1)}, u32[]{:S(2)}, u32[]{:S(2)}) collective-permute-start(f32[32,128]{1,0:T(8,128)S(1)} %add.17.band_ref), channel_id=1, source_target_pairs={{0,2},{1,3},{2,4},{3,5},{4,6},{5,7},{6,0},{7,1},{8,10},{9,11},{10,... | collective-permute-start | bytes 49160 | tf_op jit(solution)/shard_map/ppermute | solution.py:239
  19.4 1.7 %collective-permute-done.6.after_ref = f32[32,128]{1,0:T(8,128)S(1)} collective-permute-done((f32[32,128]{1,0:T(8,128)S(1)}, f32[32,128]{1,0:T(8,128)S(1)}, u32[]{:S(2)}, u32[]{:S(2)}) %collective-permute-start.6) | collective-permute-done | bytes 16416 | tf_op jit(solution)/shard_map/ppermute | solution.py:239
  21.1 0.0 copy-start.3
  21.1 2.4 %collective-permute-done.5.before_ref = f32[32,128]{1,0:T(8,128)S(1)} collective-permute-done((f32[32,128]{1,0:T(8,128)S(1)}, f32[32,128]{1,0:T(8,128)S(1)}, u32[]{:S(2)}, u32[]{:S(2)}) %collective-permute-start.5) | collective-permute-done | bytes 16416 | tf_op jit(solution)/shard_map/ppermute | solution.py:239
  23.6 0.0 copy-start.4
  23.6 0.0 collective-permute-done.1.other_ref
  23.6 0.0 copy-start
  23.6 0.0 collective-permute-done.mate_ref
  23.6 0.0 copy-done.2
  23.6 0.0 copy-done.3
  23.6 0.6 %copy-done.4 = f32[32,128]{1,0:T(8,128)} copy-done((f32[32,128]{1,0:T(8,128)}, f32[32,128]{1,0:T(8,128)S(1)}, u32[]{:S(2)}) %copy-start.4) | copy-done | bytes 16408
  24.2 0.2 copy-done
  24.4 0.0 copy-start.1
  24.4 0.8 %copy-done.1 = f32[1152,128]{1,0:T(8,128)} copy-done((f32[1152,128]{1,0:T(8,128)}, f32[1152,128]{1,0:T(8,128)S(1)}, u32[]{:S(2)}) %copy-start.1) | copy-done | bytes 589848
  25.2 3.9 %shard_map.78 = (f32[1152,128]{1,0:T(8,128)}, f32[8,128]{1,0:T(8,128)}) custom-call(s32[3]{0:T(128)} %pad_add_fusion.where_ref, f32[64,128]{1,0:T(8,128)} %constant.26.clone.table_ref, f32[1152,128]{1,0:T(8,128)} %bitcast.13, f32[1152,128]{1,0:T(8,128)} %copy-done.1, f32[1152,128]{1,0:T(8,128)} %copy-done, f32[32,128]{1,0:T(8,128)} %copy-done.2, ...), custom_call_target="tpu_custom_call" | custom-call | tf_op jit(solution)/shard_map/pallas_call | solution.py:259
  29.2 0.0 collective-permute-start.8
  29.2 0.0 collective-permute-start.7
  29.2 5.0 %collective-permute-done.8.other_ref = f32[8,128]{1,0:T(8,128)S(1)} collective-permute-done((f32[8,128]{1,0:T(8,128)}, f32[8,128]{1,0:T(8,128)S(1)}, u32[]{:S(2)}, u32[]{:S(2)}) %collective-permute-start.8) | collective-permute-done | bytes 4128 | tf_op jit(solution)/shard_map/ppermute | solution.py:269
  34.2 0.0 copy-start.5
  34.2 0.0 collective-permute-done.7.mate_ref
  34.2 0.6 %copy-done.5 = f32[8,128]{1,0:T(8,128)} copy-done((f32[8,128]{1,0:T(8,128)}, f32[8,128]{1,0:T(8,128)S(1)}, u32[]{:S(2)}) %copy-start.5) | copy-done | bytes 4120
  34.8 0.0 copy-start.6
  34.8 0.6 %copy-done.6 = f32[8,128]{1,0:T(8,128)} copy-done((f32[8,128]{1,0:T(8,128)}, f32[8,128]{1,0:T(8,128)S(1)}, u32[]{:S(2)}) %copy-start.6) | copy-done | bytes 4120
  35.4 1.5 %shard_map.79 = f32[2,512]{1,0:T(2,128)} custom-call(s32[3]{0:T(128)} %pad_add_fusion.where_ref, s32[1,512]{1,0:T(1,128)} %coupling_ref.3, f32[8,128]{1,0:T(8,128)} %get-tuple-element.5.own_ref, f32[8,128]{1,0:T(8,128)} %copy-done.6, f32[8,128]{1,0:T(8,128)} %copy-done.5), custom_call_target="tpu_custom_call" | custom-call | tf_op jit(solution)/shard_map/pallas_call | solution.py:271
  (2 shorter events, 0.0 us)
Async XLA Ops:
  0.6 22.9 %collective-permute-start.1 = (f32[1152,128]{1,0:T(8,128)}, f32[1152,128]{1,0:T(8,128)S(1)}, u32[]{:S(2)}, u32[]{:S(2)}) collective-permute-start(f32[1152,128]{1,0:T(8,128)} %bitcast.10), channel_id=1, source_target_pairs={{0,7},{1,2},{2,1},{3,4},{4,3},{5,6},{6,5},{7,0},{8,15},{9,10},{10,... | collective-permute-start | bytes 1769480 | tf_op jit(solution)/shard_map/ppermute | solution.py:242
  5.2 18.4 %collective-permute-start = (f32[1152,128]{1,0:T(8,128)}, f32[1152,128]{1,0:T(8,128)S(1)}, u32[]{:S(2)}, u32[]{:S(2)}) collective-permute-start(f32[1152,128]{1,0:T(8,128)} %bitcast.11), channel_id=1, source_target_pairs={{0,1},{1,0},{2,3},{3,2},{4,5},{5,4},{6,7},{7,6},{8,9},{9,8},{10,11... | collective-permute-start | bytes 1769480 | tf_op jit(solution)/shard_map/ppermute | solution.py:243
  7.6 1.6 %collective-permute-start.2 = (f32[32,128]{1,0:T(8,128)}, f32[32,128]{1,0:T(8,128)S(1)}, u32[]{:S(2)}, u32[]{:S(2)}) collective-permute-start(f32[32,128]{1,0:T(8,128)} %shard_map.77), channel_id=1, source_target_pairs={{0,1},{1,0},{2,3},{3,2},{4,5},{5,4},{6,7},{7,6},{8,9},{9,8},{10,11... | collective-permute-start | bytes 49160 | tf_op jit(solution)/shard_map/ppermute | solution.py:251
  9.9 3.7 %collective-permute-start.3 = (f32[32,128]{1,0:T(8,128)S(1)}, f32[32,128]{1,0:T(8,128)S(1)}, u32[]{:S(2)}, u32[]{:S(2)}) collective-permute-start(f32[32,128]{1,0:T(8,128)S(1)} %add.15), channel_id=1, source_target_pairs={{0,8},{8,0},{16,24},{24,16},{1,9},{9,1},{17,25},{25,17},{2,10},{10... | collective-permute-start | bytes 49160 | tf_op jit(solution)/shard_map/ppermute | solution.py:254
  13.6 3.7 %collective-permute-start.4 = (f32[32,128]{1,0:T(8,128)S(1)}, f32[32,128]{1,0:T(8,128)S(1)}, u32[]{:S(2)}, u32[]{:S(2)}) collective-permute-start(f32[32,128]{1,0:T(8,128)S(1)} %add.16), channel_id=1, source_target_pairs={{0,16},{8,24},{16,0},{24,8},{1,17},{9,25},{17,1},{25,9},{2,18},{10... | collective-permute-start | bytes 49160 | tf_op jit(solution)/shard_map/ppermute | solution.py:254
  17.4 6.2 %copy-start.2 = (f32[32,128]{1,0:T(8,128)}, f32[32,128]{1,0:T(8,128)S(1)}, u32[]{:S(2)}) copy-start(f32[32,128]{1,0:T(8,128)S(1)} %add.17.band_ref) | copy-start | bytes 49156
  17.4 3.7 %collective-permute-start.6 = (f32[32,128]{1,0:T(8,128)S(1)}, f32[32,128]{1,0:T(8,128)S(1)}, u32[]{:S(2)}, u32[]{:S(2)}) collective-permute-start(f32[32,128]{1,0:T(8,128)S(1)} %add.17.band_ref), channel_id=1, source_target_pairs={{0,6},{1,7},{2,0},{3,1},{4,2},{5,3},{6,4},{7,5},{8,14},{9,15},{10,... | collective-permute-start | bytes 49160 | tf_op jit(solution)/shard_map/ppermute | solution.py:239
  18.0 5.5 %collective-permute-start.5 = (f32[32,128]{1,0:T(8,128)S(1)}, f32[32,128]{1,0:T(8,128)S(1)}, u32[]{:S(2)}, u32[]{:S(2)}) collective-permute-start(f32[32,128]{1,0:T(8,128)S(1)} %add.17.band_ref), channel_id=1, source_target_pairs={{0,2},{1,3},{2,4},{3,5},{4,6},{5,7},{6,0},{7,1},{8,10},{9,11},{10,... | collective-permute-start | bytes 49160 | tf_op jit(solution)/shard_map/ppermute | solution.py:239
  21.1 2.5 %copy-start.3 = (f32[32,128]{1,0:T(8,128)}, f32[32,128]{1,0:T(8,128)S(1)}, u32[]{:S(2)}) copy-start(f32[32,128]{1,0:T(8,128)S(1)} %collective-permute-done.6.after_ref) | copy-start | bytes 49156
  23.6 0.6 %copy-start.4 = (f32[32,128]{1,0:T(8,128)}, f32[32,128]{1,0:T(8,128)S(1)}, u32[]{:S(2)}) copy-start(f32[32,128]{1,0:T(8,128)S(1)} %collective-permute-done.5.before_ref) | copy-start | bytes 49156
  23.6 0.8 %copy-start = (f32[1152,128]{1,0:T(8,128)}, f32[1152,128]{1,0:T(8,128)S(1)}, u32[]{:S(2)}) copy-start(f32[1152,128]{1,0:T(8,128)S(1)} %collective-permute-done.1.other_ref) | copy-start | bytes 1769476
  24.4 0.8 %copy-start.1 = (f32[1152,128]{1,0:T(8,128)}, f32[1152,128]{1,0:T(8,128)S(1)}, u32[]{:S(2)}) copy-start(f32[1152,128]{1,0:T(8,128)S(1)} %collective-permute-done.mate_ref) | copy-start | bytes 1769476
  29.2 5.0 %collective-permute-start.8 = (f32[8,128]{1,0:T(8,128)}, f32[8,128]{1,0:T(8,128)S(1)}, u32[]{:S(2)}, u32[]{:S(2)}) collective-permute-start(f32[8,128]{1,0:T(8,128)} %get-tuple-element.5.own_ref), channel_id=1, source_target_pairs={{0,7},{1,2},{2,1},{3,4},{4,3},{5,6},{6,5},{7,0},{8,15},{9,10},{10,... | collective-permute-start | bytes 12296 | tf_op jit(solution)/shard_map/ppermute | solution.py:269
  29.2 5.0 %collective-permute-start.7 = (f32[8,128]{1,0:T(8,128)}, f32[8,128]{1,0:T(8,128)S(1)}, u32[]{:S(2)}, u32[]{:S(2)}) collective-permute-start(f32[8,128]{1,0:T(8,128)} %get-tuple-element.5.own_ref), channel_id=1, source_target_pairs={{0,1},{1,0},{2,3},{3,2},{4,5},{5,4},{6,7},{7,6},{8,9},{9,8},{10,11... | collective-permute-start | bytes 12296 | tf_op jit(solution)/shard_map/ppermute | solution.py:270
  34.2 0.6 %copy-start.5 = (f32[8,128]{1,0:T(8,128)}, f32[8,128]{1,0:T(8,128)S(1)}, u32[]{:S(2)}) copy-start(f32[8,128]{1,0:T(8,128)S(1)} %collective-permute-done.8.other_ref) | copy-start | bytes 12292
  34.8 0.6 %copy-start.6 = (f32[8,128]{1,0:T(8,128)}, f32[8,128]{1,0:T(8,128)S(1)}, u32[]{:S(2)}) copy-start(f32[8,128]{1,0:T(8,128)S(1)} %collective-permute-done.7.mate_ref) | copy-start | bytes 12292

commit v2 on v1

--- a/solution.py
+++ b/solution.py
@@ -23,7 +23,16 @@
 FIELDS = 8
 SUM_X, SUM_Y, COUNT, SEA, WIND_X, WIND_Y, DAMP = range(7)
 VMEM = pl.BlockSpec(memory_space=pltpu.VMEM)
-SMEM = pl.BlockSpec(memory_space=pltpu.SMEM)
+
+
+def near(*arrays):
+    return [pltpu.with_memory_space_constraint(array, pltpu.VMEM) for array in arrays]
+
+
+def place():
+    me = lax.axis_index("dev")
+    odd = lax.rem(me, 2)
+    return me - odd - 1, odd, lax.axis_index("grp")
 
 
 def level_groups(levels):
@@ -33,23 +42,24 @@
     return levels, 1
 
 
-def slots_of(coupling, width, shape_ref, columns):
+def slots_of(coupling, width, first, columns):
     col = lax.div(coupling, jnp.int32(width))
     row = coupling - col * width
-    slot = col - shape_ref[0]
+    slot = col - first
     slot = jnp.where(slot < 0, slot + columns, slot)
     slot = jnp.where(slot >= columns, slot - columns, slot)
     return row, slot
 
 
-def band_kernel(columns, where_ref, coupling_ref, currents_ref, spectrum_ref, sea_ref, wind_ref, band_ref):
+def band_kernel(columns, coupling_ref, currents_ref, spectrum_ref, sea_ref, wind_ref, band_ref):
     width = spectrum_ref.shape[1]
     bins = spectrum_ref.shape[0]
-    is_ocean = where_ref[2] > 0
+    first, odd, group = place()
+    is_ocean = group > 0
 
     @pl.when(is_ocean)
     def _():
-        row, slot = slots_of(coupling_ref[...], width, where_ref, columns)
+        row, slot = slots_of(coupling_ref[...], width, first, columns)
         cells = row.shape[1]
         parts_x, parts_y = [], []
         for comp, parts in ((0, parts_x), (1, parts_y)):
@@ -94,7 +104,7 @@
         square = mean_freq * mean_freq
         steep = STEEP_SCALE * total * (square * square)
         damp = WHITECAP * (steep * steep) / square
-        own = where_ref[1] + 1
+        own = odd + 1
         band_ref[pl.ds(SEA * SLOTS + own, 1), :] = sea
         band_ref[pl.ds(WIND_X * SLOTS + own, 1), :] = wind_ref[0:1, :]
         band_ref[pl.ds(WIND_Y * SLOTS + own, 1), :] = wind_ref[1:2, :]
@@ -102,11 +112,12 @@
 
 
 def step_kernel(
-    where_ref, table_ref, own_ref, mate_ref, other_ref, band_ref, before_ref, after_ref, updated_ref, drift_ref
+    table_ref, own_ref, mate_ref, other_ref, band_ref, before_ref, after_ref, updated_ref, drift_ref
 ):
     bins, width = own_ref.shape
     lanes = 8
-    odd = where_ref[1]
+    outer_count, inner_count = level_groups(bins // NDIR)
+    _, odd, _ = place()
     slot_own, slot_mate, slot_other = 1 + odd, 2 - odd, 3 * odd
 
     def field(index, slot):
@@ -149,7 +160,6 @@
         lax.broadcasted_iota(jnp.int32, (lanes, width), 1) < width - 1, 1.0, 0.0
     )
     signed_cosine = [sign * cosine[k] for k in range(4)]
-    outer_count, inner_count = level_groups(bins // NDIR)
 
     def level_step(index, carry):
         frequency, speed, sums = carry
@@ -203,13 +213,13 @@
     drift_ref[2:8, :] = jnp.zeros((6, width), jnp.float32)
 
 
-def pick_kernel(columns, where_ref, coupling_ref, own_ref, mate_ref, other_ref, cells_ref):
+def pick_kernel(columns, coupling_ref, own_ref, mate_ref, other_ref, cells_ref):
     width = own_ref.shape[1]
-    odd = where_ref[1]
-    ocean = jnp.where(where_ref[2] > 0, 1.0, 0.0)
+    first, odd, group = place()
+    ocean = jnp.where(group > 0, 1.0, 0.0)
     for start in range(0, coupling_ref.shape[1], width):
         part = pl.ds(start, width)
-        row, slot = slots_of(coupling_ref[:, part], width, where_ref, columns)
+        row, slot = slots_of(coupling_ref[:, part], width, first, columns)
         row = jnp.broadcast_to(row, (8, width))
         own = jnp.take_along_axis(own_ref[...], row, axis=1)[0:2]
         mate = jnp.take_along_axis(mate_ref[...], row, axis=1)[0:2]
@@ -228,10 +238,6 @@
     bins, _, width = spectrum.shape
     devices = lax.axis_size("dev")
     groups = lax.axis_size("grp")
-    me = lax.axis_index("dev")
-    odd = me % 2
-    first = me - odd - 1
-    where = jnp.stack([first, odd, lax.axis_index("grp")]).astype(jnp.int32)
     mates = [(i, i ^ 1) for i in range(devices)]
     others = [(i, (i + (1 if i % 2 else -1)) % devices) for i in range(devices)]
 
@@ -244,11 +250,12 @@
 
     band = pl.pallas_call(
         functools.partial(band_kernel, devices),
-        out_shape=jax.ShapeDtypeStruct((FIELDS * SLOTS, width), jnp.float32),
-        in_specs=[SMEM] + [VMEM] * 5,
+        out_shape=pltpu.VMEM((FIELDS * SLOTS, width), jnp.float32),
+        in_specs=[VMEM] * 5,
         out_specs=VMEM,
-    )(where, coupling, currents[0], own, sea_mask, wind[:, 0])
+    )(*near(coupling, currents[0], own, sea_mask, wind[:, 0]))
     band = band + lax.ppermute(band, "dev", mates)
+    band, mate = lax.optimization_barrier((band, mate))
     reach = 1
     while reach < groups:
         band = band + lax.ppermute(band, "grp", [(i, i ^ reach) for i in range(groups)])
@@ -259,21 +266,21 @@
     updated, drift = pl.pallas_call(
         step_kernel,
         out_shape=(
-            jax.ShapeDtypeStruct((bins, width), jnp.float32),
-            jax.ShapeDtypeStruct((8, width), jnp.float32),
+            pltpu.VMEM((bins, width), jnp.float32),
+            pltpu.VMEM((8, width), jnp.float32),
         ),
-        in_specs=[SMEM] + [VMEM] * 7,
+        in_specs=[VMEM] * 7,
         out_specs=(VMEM, VMEM),
-    )(where, direction_table(width), own, mate, other, band, before, after)
+    )(*near(direction_table(width), own, mate, other, band, before, after))
 
     drift_other = lax.ppermute(drift, "dev", others)
     drift_mate = lax.ppermute(drift, "dev", mates)
     cells = pl.pallas_call(
         functools.partial(pick_kernel, devices),
         out_shape=jax.ShapeDtypeStruct(currents.shape[1:], jnp.float32),
-        in_specs=[SMEM] + [VMEM] * 4,
+        in_specs=[VMEM] * 4,
         out_specs=VMEM,
-    )(where, coupling, drift, drift_mate, drift_other)
+    )(*near(coupling, drift, drift_mate, drift_other))
     return updated.reshape(spectrum.shape), cells[None]
 
 

time: 37.2 us -> 30.7 us (0.83)
  Pallas kernels: 7.25 us -> 2.43 us
  other arithmetic: 1.35 us -> 0.01 us
  waiting for transfers between devices: 14.5 us -> 13.4 us
  local copies, waits for them, and re-layouts: 2.81 us -> 3.26 us
    pallas_call x2, Pallas kernels: 5.75 us -> 1.73 us  [the longest x1 1.67 us: body(): pl.pallas_call(step_kernel, out_shape=(pltpu.VMEM((bins, width), jnp.floa...]
    ppermute x1, waiting for transfers between devices: 5.03 us -> 3.92 us  [body(): drift_other = lax.ppermute(drift, 'dev', others)]
    pallas_call x1, Pallas kernels: 1.5 us -> 0.7 us  [body(): pl.pallas_call(functools.partial(pick_kernel, devices), out_shape=jax.Sha...]
    add x1, other arithmetic: 0.72 us -> 0.01 us  [body(): band = band + lax.ppermute(band, 'dev', mates)]
    another operation x1 -> x0, other arithmetic: 0.62 us -> none  [body(): where = jnp.stack([first, odd, lax.axis_index('grp')]).astype(jnp.int32)]
    ppermute x1, starting transfers between devices: 0.01 us -> 0.52 us  [body(): mate = lax.ppermute(own, 'dev', mates)]
    unnamed x14 -> x15, local copies, waits for them, and re-layouts: 2.81 us -> 3.26 us
    ppermute x1, starting transfers between devices: 0.51 us -> 0.07 us  [body(): band = band + lax.ppermute(band, 'dev', mates)]
  transfers between devices with their start and end apart: 9 -> 9, of which waited for: 6 -> 7; matrix products, arithmetic and copies ran while one was open for 4% -> 3% of each run, Pallas kernels for 5% -> 0%
where the time goes in v2:
time: 30.7 us; the launch traced here: 30.4 us
  waiting for transfers between devices  13.4 us (44%)
  starting transfers between devices  10.6 us (35%)
  local copies, waits for them, and re-layouts  3.26 us (11%)
  Pallas kernels  2.43 us (8%)
  between operations  0.69 us (2%)
    ppermute x1, starting transfers between devices, body(): other = lax.ppermute(own, 'dev', others)  4.71 us
    ppermute x2, waiting for transfers between devices, body(): lax.ppermute(band, 'grp', [(i, i ^ reach) for i in range(groups)])  4.38 us
    ppermute x1, waiting for transfers between devices, body(): drift_other = lax.ppermute(drift, 'dev', others)  3.92 us
    ppermute x2, waiting for transfers between devices, shifted(): lax.ppermute(value, 'dev', [(i, (i + steps) % devices) for i in range(dev...  3.91 us
    unnamed x15, local copies, waits for them, and re-layouts  3.26 us
    ppermute x2, starting transfers between devices, body(): lax.ppermute(band, 'grp', [(i, i ^ reach) for i in range(groups)])  3.16 us
    ppermute x2, starting transfers between devices, shifted(): lax.ppermute(value, 'dev', [(i, (i + steps) % devices) for i in range(dev...  2.03 us
    pallas_call x1, Pallas kernels, body(): pl.pallas_call(step_kernel, out_shape=(pltpu.VMEM((bins, width), jnp.floa...  1.67 us
  transfers between devices with their start and end apart: 9, of which 7 were waited for; matrix products, arithmetic and copies ran while one was open for 3% of the time, Pallas kernels for 0%

profile of v2, /device:TPU:0, one launch (start us, length us, event | category | flops | bytes accessed | tf_op | source)
XLA Modules:
  0.0 30.4 jit_solution(1731636527538131340)
XLA Ops:
  0.6 0.0 copy-start.3
  0.6 0.5 %collective-permute-start.1 = (f32[1152,128]{1,0:T(8,128)}, f32[1152,128]{1,0:T(8,128)S(1)}, u32[]{:S(2)}, u32[]{:S(2)}) collective-permute-start(f32[1152,128]{1,0:T(8,128)} %bitcast.8), channel_id=1, source_target_pairs={{0,1},{1,0},{2,3},{3,2},{4,5},{5,4},{6,7},{7,6},{8,9},{9,8},{10,11... | collective-permute-start | bytes 1769480 | tf_op jit(solution)/shard_map/ppermute | solution.py:249
  1.2 4.7 %collective-permute-start.2 = (f32[1152,128]{1,0:T(8,128)}, f32[1152,128]{1,0:T(8,128)S(1)}, u32[]{:S(2)}, u32[]{:S(2)}) collective-permute-start(f32[1152,128]{1,0:T(8,128)} %bitcast.9), channel_id=1, source_target_pairs={{0,7},{1,2},{2,1},{3,4},{4,3},{5,6},{6,5},{7,0},{8,15},{9,10},{10,... | collective-permute-start | bytes 1769480 | tf_op jit(solution)/shard_map/ppermute | solution.py:248
  5.9 0.0 copy-start.5
  5.9 0.0 copy-start.6
  5.9 0.0 copy-done.3
  5.9 0.7 %copy-done.5 = f32[2,1,128]{2,1,0:T(1,128)S(1)} copy-done((f32[2,1,128]{2,1,0:T(1,128)S(1)}, f32[2,1,128]{2,1,0:T(1,128)}, u32[]{:S(2)}) %copy-start.5) | copy-done | bytes 1048
  6.5 0.0 copy-done.6
  6.6 0.0 copy-start
  6.6 1.1 %copy-done = f32[1152,1,128]{2,1,0:T(1,128)S(1)} copy-done((f32[1152,1,128]{2,1,0:T(1,128)S(1)}, f32[1152,1,128]{2,1,0:T(1,128)}, u32[]{:S(2)}) %copy-start) | copy-done | bytes 589848
  7.6 0.0 copy-start.4
  7.6 0.7 %copy-done.4 = f32[1,2,512]{2,1,0:T(2,128)S(1)} copy-done((f32[1,2,512]{2,1,0:T(2,128)S(1)}, f32[1,2,512]{2,1,0:T(2,128)}, u32[]{:S(2)}) %copy-start.4) | copy-done | bytes 4120
  8.3 0.0 copy-start.1
  8.3 0.1 shard_map.77
  8.4 0.1 collective-permute-start
  8.4 1.2 %collective-permute-done = f32[32,128]{1,0:T(8,128)S(1)} collective-permute-done((f32[32,128]{1,0:T(8,128)S(1)}, f32[32,128]{1,0:T(8,128)S(1)}, u32[]{:S(2)}, u32[]{:S(2)}) %collective-permute-start) | collective-permute-done | bytes 16416 | tf_op jit(solution)/shard_map/ppermute | solution.py:257
  9.6 0.0 collective-permute-done.1.mate_ref
  9.6 1.6 %collective-permute-start.3 = (f32[32,128]{1,0:T(8,128)S(1)}, f32[32,128]{1,0:T(8,128)S(1)}, u32[]{:S(2)}, u32[]{:S(2)}) collective-permute-start(f32[32,128]{1,0:T(8,128)S(1)} %add.9), channel_id=1, source_target_pairs={{0,8},{8,0},{16,24},{24,16},{1,9},{9,1},{17,25},{25,17},{2,10},{10... | collective-permute-start | bytes 49160 | tf_op jit(solution)/shard_map/ppermute | solution.py:261
  11.2 2.2 %collective-permute-done.3 = f32[32,128]{1,0:T(8,128)S(1)} collective-permute-done((f32[32,128]{1,0:T(8,128)S(1)}, f32[32,128]{1,0:T(8,128)S(1)}, u32[]{:S(2)}, u32[]{:S(2)}) %collective-permute-start.3) | collective-permute-done | bytes 16416 | tf_op jit(solution)/shard_map/ppermute | solution.py:261
  13.4 0.0 copy-start.2
  13.4 1.6 %collective-permute-start.4 = (f32[32,128]{1,0:T(8,128)S(1)}, f32[32,128]{1,0:T(8,128)S(1)}, u32[]{:S(2)}, u32[]{:S(2)}) collective-permute-start(f32[32,128]{1,0:T(8,128)S(1)} %add.10), channel_id=1, source_target_pairs={{0,16},{8,24},{16,0},{24,8},{1,17},{9,25},{17,1},{25,9},{2,18},{10... | collective-permute-start | bytes 49160 | tf_op jit(solution)/shard_map/ppermute | solution.py:261
  15.0 2.2 %collective-permute-done.4 = f32[32,128]{1,0:T(8,128)S(1)} collective-permute-done((f32[32,128]{1,0:T(8,128)S(1)}, f32[32,128]{1,0:T(8,128)S(1)}, u32[]{:S(2)}, u32[]{:S(2)}) %collective-permute-start.4) | collective-permute-done | bytes 16416 | tf_op jit(solution)/shard_map/ppermute | solution.py:261
  17.2 0.4 %collective-permute-start.6 = (f32[32,128]{1,0:T(8,128)S(1)}, f32[32,128]{1,0:T(8,128)S(1)}, u32[]{:S(2)}, u32[]{:S(2)}) collective-permute-start(f32[32,128]{1,0:T(8,128)S(1)} %add.11.band_ref), channel_id=1, source_target_pairs={{0,6},{1,7},{2,0},{3,1},{4,2},{5,3},{6,4},{7,5},{8,14},{9,15},{10,... | collective-permute-start | bytes 49160 | tf_op jit(solution)/shard_map/ppermute | solution.py:245
  17.6 1.6 %collective-permute-start.5 = (f32[32,128]{1,0:T(8,128)S(1)}, f32[32,128]{1,0:T(8,128)S(1)}, u32[]{:S(2)}, u32[]{:S(2)}) collective-permute-start(f32[32,128]{1,0:T(8,128)S(1)} %add.11.band_ref), channel_id=1, source_target_pairs={{0,2},{1,3},{2,4},{3,5},{4,6},{5,7},{6,0},{7,1},{8,10},{9,11},{10,... | collective-permute-start | bytes 49160 | tf_op jit(solution)/shard_map/ppermute | solution.py:245
  19.2 0.1 collective-permute-done.2.other_ref
  19.3 1.7 %collective-permute-done.6.after_ref = f32[32,128]{1,0:T(8,128)S(1)} collective-permute-done((f32[32,128]{1,0:T(8,128)S(1)}, f32[32,128]{1,0:T(8,128)S(1)}, u32[]{:S(2)}, u32[]{:S(2)}) %collective-permute-start.6) | collective-permute-done | bytes 16416 | tf_op jit(solution)/shard_map/ppermute | solution.py:245
  20.9 2.2 %collective-permute-done.5.before_ref = f32[32,128]{1,0:T(8,128)S(1)} collective-permute-done((f32[32,128]{1,0:T(8,128)S(1)}, f32[32,128]{1,0:T(8,128)S(1)}, u32[]{:S(2)}, u32[]{:S(2)}) %collective-permute-start.5) | collective-permute-done | bytes 16416 | tf_op jit(solution)/shard_map/ppermute | solution.py:245
  23.2 0.0 copy-done.1
  23.2 0.0 copy-done.2
  23.2 1.7 %shard_map.78 = (f32[1152,128]{1,0:T(8,128)S(1)}, f32[8,128]{1,0:T(8,128)S(1)}) custom-call(f32[64,128]{1,0:T(8,128)S(1)} %copy-done.2, f32[1152,128]{1,0:T(8,128)S(1)} %bitcast.11, f32[1152,128]{1,0:T(8,128)S(1)} %collective-permute-done.1.mate_ref, f32[1152,128]{1,0:T(8,128)S(1)} %collective-permute-done.2.other_ref, f32[32,128]{1,0:T(8,128)S(1)} %add.11.band_ref, ...), custom_call_target="tpu_custom_call" | custom-call | tf_op jit(solution)/shard_map/pallas_call | solution.py:266
  24.9 0.1 collective-permute-start.8
  24.9 0.1 collective-permute-start.7
  25.0 0.8 %copy.9 = f32[1152,1,128]{2,1,0:T(1,128)} copy(f32[1152,1,128]{2,1,0:T(1,128)S(1)} %bitcast.7) | data formatting | bytes 1179648
  25.8 3.9 %collective-permute-done.8.other_ref = f32[8,128]{1,0:T(8,128)S(1)} collective-permute-done((f32[8,128]{1,0:T(8,128)S(1)}, f32[8,128]{1,0:T(8,128)S(1)}, u32[]{:S(2)}, u32[]{:S(2)}) %collective-permute-start.8) | collective-permute-done | bytes 4128 | tf_op jit(solution)/shard_map/ppermute | solution.py:276
  29.7 0.0 collective-permute-done.7.mate_ref
  29.8 0.7 %shard_map.79 = f32[2,512]{1,0:T(2,128)} custom-call(s32[1,512]{1,0:T(1,128)S(1)} %copy-done.3, f32[8,128]{1,0:T(8,128)S(1)} %get-tuple-element.9.own_ref, f32[8,128]{1,0:T(8,128)S(1)} %collective-permute-done.7.mate_ref, f32[8,128]{1,0:T(8,128)S(1)} %collective-permute-done.8.other_ref), custom_call_target="tpu_custom_call" | custom-call | tf_op jit(solution)/shard_map/pallas_call | solution.py:278
  (3 shorter events, 0.0 us)
Async XLA Ops:
  0.6 5.2 %copy-start.3 = (s32[1,512]{1,0:T(1,128)S(1)}, s32[1,512]{1,0:T(1,128)}, u32[]{:S(2)}) copy-start(s32[1,512]{1,0:T(1,128)} %coupling_ref.3) | copy-start | bytes 6148
  0.6 9.0 %collective-permute-start.1 = (f32[1152,128]{1,0:T(8,128)}, f32[1152,128]{1,0:T(8,128)S(1)}, u32[]{:S(2)}, u32[]{:S(2)}) collective-permute-start(f32[1152,128]{1,0:T(8,128)} %bitcast.8), channel_id=1, source_target_pairs={{0,1},{1,0},{2,3},{3,2},{4,5},{5,4},{6,7},{7,6},{8,9},{9,8},{10,11... | collective-permute-start | bytes 1769480 | tf_op jit(solution)/shard_map/ppermute | solution.py:249
  1.2 18.1 %collective-permute-start.2 = (f32[1152,128]{1,0:T(8,128)}, f32[1152,128]{1,0:T(8,128)S(1)}, u32[]{:S(2)}, u32[]{:S(2)}) collective-permute-start(f32[1152,128]{1,0:T(8,128)} %bitcast.9), channel_id=1, source_target_pairs={{0,7},{1,2},{2,1},{3,4},{4,3},{5,6},{6,5},{7,0},{8,15},{9,10},{10,... | collective-permute-start | bytes 1769480 | tf_op jit(solution)/shard_map/ppermute | solution.py:248
  5.9 0.7 %copy-start.5 = (f32[2,1,128]{2,1,0:T(1,128)S(1)}, f32[2,1,128]{2,1,0:T(1,128)}, u32[]{:S(2)}) copy-start(f32[2,1,128]{2,1,0:T(1,128)} %param.8) | copy-start | bytes 3076
  5.9 0.7 %copy-start.6 = (s32[1,128]{1,0:T(1,128)S(1)}, s32[1,128]{1,0:T(1,128)}, u32[]{:S(2)}) copy-start(s32[1,128]{1,0:T(1,128)} %sea_ref.1) | copy-start | bytes 1540
  6.6 1.1 %copy-start = (f32[1152,1,128]{2,1,0:T(1,128)S(1)}, f32[1152,1,128]{2,1,0:T(1,128)}, u32[]{:S(2)}) copy-start(f32[1152,1,128]{2,1,0:T(1,128)} %param.6) | copy-start | bytes 1769476
  7.6 0.7 %copy-start.4 = (f32[1,2,512]{2,1,0:T(2,128)S(1)}, f32[1,2,512]{2,1,0:T(2,128)}, u32[]{:S(2)}) copy-start(f32[1,2,512]{2,1,0:T(2,128)} %param.9) | copy-start | bytes 12292
  8.3 14.9 %copy-start.1 = (f32[1152,1,128]{2,1,0:T(1,128)S(1)}, f32[1152,1,128]{2,1,0:T(1,128)}, u32[]{:S(2)}) copy-start(f32[1152,1,128]{2,1,0:T(1,128)} %param.6) | copy-start | bytes 1769476
  8.4 1.2 %collective-permute-start = (f32[32,128]{1,0:T(8,128)S(1)}, f32[32,128]{1,0:T(8,128)S(1)}, u32[]{:S(2)}, u32[]{:S(2)}) collective-permute-start(f32[32,128]{1,0:T(8,128)S(1)} %shard_map.77), channel_id=1, source_target_pairs={{0,1},{1,0},{2,3},{3,2},{4,5},{5,4},{6,7},{7,6},{8,9},{9,8},{10,11... | collective-permute-start | bytes 49160 | tf_op jit(solution)/shard_map/ppermute | solution.py:257
  9.6 3.8 %collective-permute-start.3 = (f32[32,128]{1,0:T(8,128)S(1)}, f32[32,128]{1,0:T(8,128)S(1)}, u32[]{:S(2)}, u32[]{:S(2)}) collective-permute-start(f32[32,128]{1,0:T(8,128)S(1)} %add.9), channel_id=1, source_target_pairs={{0,8},{8,0},{16,24},{24,16},{1,9},{9,1},{17,25},{25,17},{2,10},{10... | collective-permute-start | bytes 49160 | tf_op jit(solution)/shard_map/ppermute | solution.py:261
  13.4 9.7 %copy-start.2 = (f32[64,128]{1,0:T(8,128)S(1)}, f32[64,128]{1,0:T(8,128)}, u32[]{:S(2)}) copy-start(f32[64,128]{1,0:T(8,128)} %constant.2.clone.table_ref) | copy-start | bytes 98308
  13.4 3.7 %collective-permute-start.4 = (f32[32,128]{1,0:T(8,128)S(1)}, f32[32,128]{1,0:T(8,128)S(1)}, u32[]{:S(2)}, u32[]{:S(2)}) collective-permute-start(f32[32,128]{1,0:T(8,128)S(1)} %add.10), channel_id=1, source_target_pairs={{0,16},{8,24},{16,0},{24,8},{1,17},{9,25},{17,1},{25,9},{2,18},{10... | collective-permute-start | bytes 49160 | tf_op jit(solution)/shard_map/ppermute | solution.py:261
  17.2 3.7 %collective-permute-start.6 = (f32[32,128]{1,0:T(8,128)S(1)}, f32[32,128]{1,0:T(8,128)S(1)}, u32[]{:S(2)}, u32[]{:S(2)}) collective-permute-start(f32[32,128]{1,0:T(8,128)S(1)} %add.11.band_ref), channel_id=1, source_target_pairs={{0,6},{1,7},{2,0},{3,1},{4,2},{5,3},{6,4},{7,5},{8,14},{9,15},{10,... | collective-permute-start | bytes 49160 | tf_op jit(solution)/shard_map/ppermute | solution.py:245
  17.6 5.5 %collective-permute-start.5 = (f32[32,128]{1,0:T(8,128)S(1)}, f32[32,128]{1,0:T(8,128)S(1)}, u32[]{:S(2)}, u32[]{:S(2)}) collective-permute-start(f32[32,128]{1,0:T(8,128)S(1)} %add.11.band_ref), channel_id=1, source_target_pairs={{0,2},{1,3},{2,4},{3,5},{4,6},{5,7},{6,0},{7,1},{8,10},{9,11},{10,... | collective-permute-start | bytes 49160 | tf_op jit(solution)/shard_map/ppermute | solution.py:245
  24.9 4.9 %collective-permute-start.8 = (f32[8,128]{1,0:T(8,128)S(1)}, f32[8,128]{1,0:T(8,128)S(1)}, u32[]{:S(2)}, u32[]{:S(2)}) collective-permute-start(f32[8,128]{1,0:T(8,128)S(1)} %get-tuple-element.9.own_ref), channel_id=1, source_target_pairs={{0,7},{1,2},{2,1},{3,4},{4,3},{5,6},{6,5},{7,0},{8,15},{9,10},{10,... | collective-permute-start | bytes 12296 | tf_op jit(solution)/shard_map/ppermute | solution.py:276
  24.9 4.8 %collective-permute-start.7 = (f32[8,128]{1,0:T(8,128)S(1)}, f32[8,128]{1,0:T(8,128)S(1)}, u32[]{:S(2)}, u32[]{:S(2)}) collective-permute-start(f32[8,128]{1,0:T(8,128)S(1)} %get-tuple-element.9.own_ref), channel_id=1, source_target_pairs={{0,1},{1,0},{2,3},{3,2},{4,5},{5,4},{6,7},{7,6},{8,9},{9,8},{10,11... | collective-permute-start | bytes 12296 | tf_op jit(solution)/shard_map/ppermute | solution.py:277

commit v3 on v2

v3 whole, which is shorter than its diff:
```python
import functools
import math

import jax
import jax.numpy as jnp
import numpy as np
from jax import lax
from jax.experimental import pallas as pl
from jax.experimental.pallas import tpu as pltpu
from jax.sharding import PartitionSpec as P

NDIR = 32
FIRST_FREQ = 0.04
GROWTH = 1.1
SPEED_TOP = 0.45
CURRENT_TOP = 0.2
WIND_GAIN = 0.03
WHITECAP = 0.3
STEEP_SCALE = 0.4
STOKES_GAIN = 3.0

SLOTS = 4
FIELDS = 8
SUM_X, SUM_Y, COUNT, SEA, WIND_X, WIND_Y, DAMP = range(7)
VMEM = pl.BlockSpec(memory_space=pltpu.VMEM)


def near(*arrays):
    return [pltpu.with_memory_space_constraint(array, pltpu.VMEM) for array in arrays]


def place():
    me = lax.axis_index("dev")
    odd = lax.rem(me, 2)
    return me - odd - 1, odd, lax.axis_index("grp")


def level_groups(levels):
    for size in (4, 3, 2):
        if levels % size == 0:
            return levels // size, size
    return levels, 1


def slots_of(coupling, width, first, columns):
    col = lax.div(coupling, jnp.int32(width))
    row = coupling - col * width
    slot = col - first
    slot = jnp.where(slot < 0, slot + columns, slot)
    slot = jnp.where(slot >= columns, slot - columns, slot)
    return row, slot


def band_kernel(
    columns, coupling_hbm, currents_hbm, spectrum_hbm, sea_hbm, wind_hbm, band_ref,
    coupling_ref, currents_ref, spectrum_ref, sea_ref, wind_ref, sems,
):
    bins, width = spectrum_ref.shape
    first, odd, group = place()
    is_ocean = group > 0

    @pl.when(is_ocean)
    def _():
        copies = [
            pltpu.make_async_copy(coupling_hbm, coupling_ref, sems.at[0]),
            pltpu.make_async_copy(currents_hbm, currents_ref, sems.at[1]),
        ]
        for copy in copies:
            copy.start()
        for copy in copies:
            copy.wait()
        row, slot = slots_of(coupling_ref[...], width, first, columns)
        cells = row.shape[1]
        parts_x, parts_y = [], []
        for comp, parts in ((0, parts_x), (1, parts_y)):
            rest = currents_ref[comp : comp + 1, :]
            for _ in range(3):
                part = rest.astype(jnp.bfloat16).astype(jnp.float32)
                parts.append(part)
                rest = rest - part
        slot_id = lax.broadcasted_iota(jnp.int32, (SLOTS, cells), 0)
        here = jnp.where(slot_id == slot, 1.0, 0.0)
        rows = []
        for part in range(3):
            rows += [here * parts_x[part], here * parts_y[part]]
        rows += [here, jnp.zeros_like(here)]
        values = jnp.concatenate(rows, axis=0).astype(jnp.bfloat16)
        row_id = lax.broadcasted_iota(jnp.int32, (width, cells), 0)
        hot = jnp.where(row_id == row, 1.0, 0.0).astype(jnp.bfloat16)
        sums = lax.dot_general(
            values, hot, (((1,), (1,)), ((), ())), preferred_element_type=jnp.float32
        )
        step = 2 * SLOTS
        band_ref[0:step, :] = sums[0:step] + sums[step : 2 * step] + sums[2 * step : 3 * step]
        band_ref[step : 2 * step, :] = sums[3 * step : 4 * step]
        band_ref[2 * step : 4 * step, :] = jnp.zeros((2 * step, width), jnp.float32)

    @pl.when(jnp.logical_not(is_ocean))
    def _():
        copies = [
            pltpu.make_async_copy(spectrum_hbm, spectrum_ref, sems.at[2]),
            pltpu.make_async_copy(sea_hbm, sea_ref, sems.at[3]),
            pltpu.make_async_copy(wind_hbm, wind_ref, sems.at[4]),
        ]
        for copy in copies:
            copy.start()
        band_ref[...] = jnp.zeros_like(band_ref)
        for copy in copies:
            copy.wait()
        total = jnp.zeros((8, width), jnp.float32)
        moment = jnp.zeros((8, width), jnp.float32)
        for level in range(bins // NDIR):
            frequency = FIRST_FREQ * GROWTH**level
            block = spectrum_ref[level * NDIR : (level + 1) * NDIR, :]
            block = block[0:8] + block[8:16] + (block[16:24] + block[24:32])
            total += (0.1 * frequency) * block
            moment += (0.1 * frequency * frequency) * block
        sea = sea_ref[...].astype(jnp.float32)
        total = jnp.sum(total, axis=0, keepdims=True) * sea
        moment = jnp.sum(moment, axis=0, keepdims=True) * sea
        is_sea = sea > 0.5
        mean_freq = jnp.where(is_sea, moment / jnp.where(is_sea, total, 1.0), 1.0)
        square = mean_freq * mean_freq
        steep = STEEP_SCALE * total * (square * square)
        damp = WHITECAP * (steep * steep) / square
        own = odd + 1
        band_ref[pl.ds(SEA * SLOTS + own, 1), :] = sea
        band_ref[pl.ds(WIND_X * SLOTS + own, 1), :] = wind_ref[0:1, :]
        band_ref[pl.ds(WIND_Y * SLOTS + own, 1), :] = wind_ref[1:2, :]
        band_ref[pl.ds(DAMP * SLOTS + own, 1), :] = damp


def tables_of(table_ref):
    cosine = [table_ref[8 * k : 8 * k + 8, :] for k in range(4)]
    sine = [table_ref[NDIR + 8 * k : NDIR + 8 * k + 8, :] for k in range(4)]
    return cosine, sine


def row_of(total_ref, index, slot):
    return total_ref[pl.ds(index * SLOTS + slot, 1), :]


def flow_of(total_ref, index, slot):
    count = jnp.maximum(row_of(total_ref, COUNT, slot), 1.0)
    return CURRENT_TOP * jnp.tanh(row_of(total_ref, index, slot) / count)


def source_state(total_ref, slot, cosine, sine):
    count = jnp.maximum(row_of(total_ref, COUNT, slot), 1.0)
    gain = WIND_GAIN * 0.64
    rel_x = gain * (row_of(total_ref, WIND_X, slot) - row_of(total_ref, SUM_X, slot) / count)
    rel_y = gain * (row_of(total_ref, WIND_Y, slot) - row_of(total_ref, SUM_Y, slot) / count)
    along = [rel_x * cosine[k] + rel_y * sine[k] for k in range(4)]
    sea = jnp.broadcast_to(row_of(total_ref, SEA, slot), cosine[0].shape)
    damp = jnp.broadcast_to(row_of(total_ref, DAMP, slot), cosine[0].shape)
    return along, sea, damp


def forced_of(energy, scale, frequency, along):
    return (energy * scale) * jnp.maximum(frequency * along + (1.0 - WIND_GAIN), 1.0)


def over_levels(bins, level_body, sums):
    outer_count, inner_count = level_groups(bins // NDIR)

    def step(index, carry):
        frequency, speed, values = carry
        for sub in range(inner_count):
            base = (index * inner_count + sub) * NDIR
            values = level_body(base, frequency, speed, values)
            frequency = frequency * GROWTH
            speed = speed * (1.0 / GROWTH)
        return frequency, speed, values

    start = (jnp.float32(FIRST_FREQ), jnp.float32(SPEED_TOP), sums)
    return lax.fori_loop(0, outer_count, step, start)[2]


def own_column(total_ref, odd, cosine, sine):
    lanes = cosine[0].shape
    width = lanes[1]
    along, sea, damp = source_state(total_ref, 1 + odd, cosine, sine)
    flow_x = flow_of(total_ref, SUM_X, 1 + odd)
    flow_low = flow_of(total_ref, SUM_X, odd)
    flow_high = flow_of(total_ref, SUM_X, 2 + odd)
    flow_y = jnp.broadcast_to(flow_of(total_ref, SUM_Y, 1 + odd), lanes)
    inner = jnp.where(lax.broadcasted_iota(jnp.int32, lanes, 1) < width - 1, 1.0, 0.0)
    return {
        "along": along,
        "sea": sea,
        "damp": damp,
        "cosine": cosine,
        "face_low": jnp.broadcast_to(-0.5 * (flow_low + flow_x), lanes),
        "face_high": jnp.broadcast_to(0.5 * (flow_x + flow_high), lanes),
        "face_north": (0.5 * inner) * (flow_y + pltpu.roll(flow_y, width - 1, 1)),
        "sine": [inner * sine[k] for k in range(4)],
    }


def kept_and_sent(own, energy, scale, frequency, speed, k):
    width = energy.shape[1]
    forced = forced_of(energy, scale, frequency, own["along"][k])
    speed_x = speed * own["cosine"][k]
    to_high = jnp.maximum(own["face_high"] + speed_x, 0.0) * forced
    to_low = jnp.maximum(own["face_low"] - speed_x, 0.0) * forced
    north = speed * own["sine"][k] + own["face_north"]
    flux = jnp.maximum(north, 0.0) * forced
    flux = flux + jnp.minimum(north, 0.0) * pltpu.roll(forced, width - 1, 1)
    keep = (forced - (to_high + to_low)) - (flux - pltpu.roll(flux, 1, 1))
    return keep, to_low, to_high


def home_kernel(table_ref, own_ref, _, band_ref, before_ref, after_ref, out_ref, total_ref):
    bins, width = own_ref.shape
    _, odd, _ = place()
    rows = band_ref.shape[0]
    low = lax.broadcasted_iota(jnp.int32, (rows, width), 0) % SLOTS < 2
    total_ref[...] = band_ref[...] + jnp.where(
        low, pltpu.roll(before_ref[...], rows - 2, 0), pltpu.roll(after_ref[...], 2, 0)
    )
    cosine, sine = tables_of(table_ref)
    lanes = cosine[0].shape
    own = own_column(total_ref, odd, cosine, sine)

    def level(base, frequency, speed, sums):
        kept, lows, highs = (list(part) for part in sums)
        square = frequency * frequency
        scale = own["sea"] / (1.0 + square * own["damp"])
        weight = (STOKES_GAIN * 0.1) * (square * square)
        for k in range(4):
            at = pl.ds(pl.multiple_of(base + 8 * k, 8), 8)
            keep, to_low, to_high = kept_and_sent(own, own_ref[at, :], scale, frequency, speed, k)
            kept[k] = kept[k] + weight * keep
            lows[k] = lows[k] + weight * to_low
            highs[k] = highs[k] + weight * to_high
        return tuple(kept), tuple(lows), tuple(highs)

    zero = (jnp.zeros(lanes, jnp.float32),) * 4
    parts = over_levels(bins, level, (zero, zero, zero))
    out_ref[...] = jnp.zeros_like(out_ref)
    for index, part in enumerate(parts):
        for comp, turn in enumerate((cosine, sine)):
            value = part[0] * turn[0]
            for k in range(1, 4):
                value = value + part[k] * turn[k]
            at = pl.ds((2 * index + comp) * SLOTS + 1 + odd, 1)
            out_ref[at, :] = jnp.sum(value, axis=0, keepdims=True)


def update_kernel(table_ref, own_ref, mate_ref, other_ref, total_ref, updated_ref):
    bins = own_ref.shape[0]
    _, odd, _ = place()
    slot_mate, slot_other = 2 - odd, 3 * odd
    cosine, sine = tables_of(table_ref)
    lanes = cosine[0].shape
    along_mate, sea_mate, damp_mate = source_state(total_ref, slot_mate, cosine, sine)
    along_other, sea_other, damp_other = source_state(total_ref, slot_other, cosine, sine)
    own = own_column(total_ref, odd, cosine, sine)
    flow_x = flow_of(total_ref, SUM_X, 1 + odd)
    sign = jnp.where(odd > 0, 1.0, -1.0)
    face_mate = (0.5 * sign) * (flow_x + flow_of(total_ref, SUM_X, slot_mate))
    face_other = (-0.5 * sign) * (flow_x + flow_of(total_ref, SUM_X, slot_other))
    face_mate = jnp.broadcast_to(face_mate, lanes)
    face_other = jnp.broadcast_to(face_other, lanes)
    signed_cosine = [sign * cosine[k] for k in range(4)]

    def level(base, frequency, speed, sums):
        square = frequency * frequency
        scale = own["sea"] / (1.0 + square * own["damp"])
        scale_mate = sea_mate / (1.0 + square * damp_mate)
        scale_other = sea_other / (1.0 + square * damp_other)
        for k in range(4):
            at = pl.ds(pl.multiple_of(base + 8 * k, 8), 8)
            mate = forced_of(mate_ref[at, :], scale_mate, frequency, along_mate[k])
            other = forced_of(other_ref[at, :], scale_other, frequency, along_other[k])
            speed_x = speed * signed_cosine[k]
            mate = jnp.maximum(face_mate + speed_x, 0.0) * mate
            other = jnp.maximum(face_other - speed_x, 0.0) * other
            keep, _, _ = kept_and_sent(own, own_ref[at, :], scale, frequency, speed, k)
            updated_ref[at, :] = (keep + (mate + other)) * own["sea"]
        return sums

    over_levels(bins, level, ())


def pick_kernel(columns, coupling_ref, total_ref, out_ref, before_ref, after_ref, cells_ref):
    width = out_ref.shape[1]
    first, _, group = place()
    ocean = jnp.where(group > 0, 1.0, 0.0)
    kept, low, high = 0, 2 * SLOTS, 4 * SLOTS

    def comp(ref, field, index, slot):
        start = field + index * SLOTS + slot
        return ref[start : start + 1, :]

    rows = []
    for index in range(2):
        rows += [
            comp(before_ref, kept, index, 2) + comp(before_ref, high, index, 1) + comp(out_ref, low, index, 1),
            comp(out_ref, kept, index, 1) + comp(before_ref, high, index, 2) + comp(out_ref, low, index, 2),
            comp(out_ref, kept, index, 2) + comp(out_ref, high, index, 1) + comp(after_ref, low, index, 1),
            comp(after_ref, kept, index, 1) + comp(out_ref, high, index, 2) + comp(after_ref, low, index, 2),
        ]
    sea = total_ref[SEA * SLOTS : (SEA + 1) * SLOTS, :] * ocean
    drift = jnp.concatenate(rows, axis=0) * jnp.concatenate([sea, sea], axis=0)
    for start in range(0, coupling_ref.shape[1], width):
        part = pl.ds(start, width)
        row, slot = slots_of(coupling_ref[:, part], width, first, columns)
        value = jnp.take_along_axis(drift, jnp.broadcast_to(row, drift.shape), axis=1)
        picked = []
        for index in range(2):
            base = index * SLOTS
            picked.append(
                jnp.where(
                    slot < 2,
                    jnp.where(slot < 1, value[base : base + 1], value[base + 1 : base + 2]),
                    jnp.where(slot < 3, value[base + 2 : base + 3], value[base + 3 : base + 4]),
                )
            )
        cells_ref[0:1, part] = picked[0]
        cells_ref[1:2, part] = picked[1]


def direction_table(width):
    heading = np.arange(NDIR) * (2.0 * math.pi / NDIR)
    table = np.concatenate([np.cos(heading), np.sin(heading)]).astype(np.float32)
    return jnp.asarray(np.repeat(table[:, None], width, axis=1))


def body(spectrum, sea_mask, wind, currents, coupling):
    bins, _, width = spectrum.shape
    cells = coupling.shape[1]
    devices = lax.axis_size("dev")
    groups = lax.axis_size("grp")
    mates = [(i, i ^ 1) for i in range(devices)]
    others = [(i, (i + (1 if i % 2 else -1)) % devices) for i in range(devices)]

    def crossed(value, group_step, chip_step):
        def target(group, dev):
            if groups & (groups - 1):
                group = (group + group_step) % groups
            else:
                group = group ^ group_step
            return group * devices + ((dev + 2 * chip_step) % devices ^ 1)

        pairs = [(g * devices + d, target(g, d)) for g in range(groups) for d in range(devices)]
        return lax.ppermute(value, ("grp", "dev"), pairs)

    own = spectrum.reshape(bins, width)
    mate = lax.ppermute(own, "dev", mates)
    other = lax.ppermute(own, "dev", others)

    anywhere = pl.BlockSpec(memory_space=pl.ANY)
    band = pl.pallas_call(
        functools.partial(band_kernel, devices),
        out_shape=pltpu.VMEM((FIELDS * SLOTS, width), jnp.float32),
        in_specs=[anywhere] * 5,
        out_specs=VMEM,
        scratch_shapes=[
            pltpu.VMEM((1, cells), jnp.int32),
            pltpu.VMEM((2, cells), jnp.float32),
            pltpu.VMEM((bins, width), jnp.float32),
            pltpu.VMEM((1, width), jnp.int32),
            pltpu.VMEM((2, width), jnp.float32),
            pltpu.SemaphoreType.DMA((5,)),
        ],
    )(coupling, currents[0], own, sea_mask, wind[:, 0])
    band = band + lax.ppermute(band, "dev", mates)
    parts = [crossed(band, step, 0) for step in range(1, groups)]
    for part in parts:
        band = band + part
    before = crossed(band, 0, 1)
    after = crossed(band, 0, -1)

    table = direction_table(width)
    out, total = pl.pallas_call(
        home_kernel,
        out_shape=(
            pltpu.VMEM((6 * SLOTS, width), jnp.float32),
            pltpu.VMEM((FIELDS * SLOTS, width), jnp.float32),
        ),
        in_specs=[VMEM] * 6,
        out_specs=(VMEM,) * 2,
    )(*near(table, own, mate, band, before, after))
    out = out + lax.ppermute(out, "dev", mates)
    out_before = crossed(out, 0, 1)
    out_after = crossed(out, 0, -1)
    updated = pl.pallas_call(
        update_kernel,
        out_shape=pltpu.VMEM((bins, width), jnp.float32),
        in_specs=[VMEM] * 5,
        out_specs=VMEM,
    )(*near(table, own, mate, other, total))
    cell_drift = pl.pallas_call(
        functools.partial(pick_kernel, devices),
        out_shape=jax.ShapeDtypeStruct(currents.shape[1:], jnp.float32),
        in_specs=[VMEM] * 5,
        out_specs=VMEM,
    )(*near(coupling, total, out, out_before, out_after))
    return updated.reshape(spectrum.shape), cell_drift[None]


def solution(mesh):
    return jax.shard_map(
        body,
        mesh=mesh,
        in_specs=(
            P(None, "dev", None),
            P("dev", None),
            P(None, "dev", None),
            P("grp", None, "dev"),
            P("grp", "dev"),
        ),
        out_specs=(P(None, "dev", None), P("grp", None, "dev")),
        check_vma=False,
    )
```

time: 30.7 us -> 32.2 us (1.049)
  starting transfers between devices: 10.6 us -> 15.6 us
  waiting for transfers between devices: 13.4 us -> 8.63 us
  Pallas kernels: 2.43 us -> 5.2 us
  local copies, waits for them, and re-layouts: 3.26 us -> 1.9 us
    ppermute x6 -> x8, starting transfers between devices: 5.33 us -> 10.3 us  [the longest x7 9.92 us: crossed(): return lax.ppermute(value, ('grp', 'dev'), pairs)]
    ppermute x6 -> x8, waiting for transfers between devices: 12.2 us -> 7.46 us  [the longest x7 6.54 us: crossed(): return lax.ppermute(value, ('grp', 'dev'), pairs)]
    pallas_call x1 -> x2, Pallas kernels: 1.67 us -> 3.29 us  [the longest x1 1.65 us: body(): pl.pallas_call(home_kernel, out_shape=(pltpu.VMEM((6 * SLOTS, width), jnp...]
    unnamed x15 -> x11, local copies, waits for them, and re-layouts: 3.26 us -> 1.9 us
    pallas_call x1, Pallas kernels: 0.06 us -> 1.21 us  [body(): pl.pallas_call(functools.partial(band_kernel, devices), out_shape=pltpu.V...]
  transfers between devices with their start and end apart: 9 -> 11, of which waited for: 7 -> 7; matrix products, arithmetic and copies ran while one was open for 3% -> 3% of each run, Pallas kernels for 0% -> 14%
where the time goes in v3:
time: 32.2 us; the launch traced here: 32 us
  starting transfers between devices  15.6 us (48%)
  waiting for transfers between devices  8.63 us (27%)
  Pallas kernels  5.2 us (16%)
  local copies, waits for them, and re-layouts  1.9 us (6%)
  between operations  0.73 us (2%)
    ppermute x7, starting transfers between devices, crossed(): return lax.ppermute(value, ('grp', 'dev'), pairs)  9.92 us
    ppermute x7, waiting for transfers between devices, crossed(): return lax.ppermute(value, ('grp', 'dev'), pairs)  6.54 us
    ppermute x1, starting transfers between devices, body(): other = lax.ppermute(own, 'dev', others)  4.71 us
    unnamed x11, local copies, waits for them, and re-layouts  1.9 us
    pallas_call x1, Pallas kernels, body(): pl.pallas_call(home_kernel, out_shape=(pltpu.VMEM((6 * SLOTS, width), jnp...  1.65 us
    pallas_call x1, Pallas kernels, body(): pl.pallas_call(update_kernel, out_shape=pltpu.VMEM((bins, width), jnp.flo...  1.64 us
    pallas_call x1, Pallas kernels, body(): pl.pallas_call(functools.partial(band_kernel, devices), out_shape=pltpu.V...  1.21 us
    ppermute x1, waiting for transfers between devices, body(): band = band + lax.ppermute(band, 'dev', mates)  1.17 us
  transfers between devices with their start and end apart: 11, of which 7 were waited for; matrix products, arithmetic and copies ran while one was open for 3% of the time, Pallas kernels for 14%

profile of v3, /device:TPU:0, one launch (start us, length us, event | category | flops | bytes accessed | tf_op | source)
XLA Modules:
  0.0 32.0 jit_solution(8258832292917490803)
XLA Ops:
  0.6 0.0 copy-start
  0.6 0.5 %collective-permute-start = (f32[1152,128]{1,0:T(8,128)}, f32[1152,128]{1,0:T(8,128)S(1)}, u32[]{:S(2)}, u32[]{:S(2)}) collective-permute-start(f32[1152,128]{1,0:T(8,128)} %bitcast.8), channel_id=1, source_target_pairs={{0,1},{1,0},{2,3},{3,2},{4,5},{5,4},{6,7},{7,6},{8,9},{9,8},{10,11... | collective-permute-start | bytes 1769480 | tf_op jit(solution)/shard_map/ppermute | solution.py:350
  1.2 4.7 %collective-permute-start.1 = (f32[1152,128]{1,0:T(8,128)}, f32[1152,128]{1,0:T(8,128)S(1)}, u32[]{:S(2)}, u32[]{:S(2)}) collective-permute-start(f32[1152,128]{1,0:T(8,128)} %bitcast.9), channel_id=1, source_target_pairs={{0,7},{1,2},{2,1},{3,4},{4,3},{5,6},{6,5},{7,0},{8,15},{9,10},{10,... | collective-permute-start | bytes 1769480 | tf_op jit(solution)/shard_map/ppermute | solution.py:351
  5.9 1.2 %shard_map.77 = f32[32,128]{1,0:T(8,128)S(1)} custom-call(s32[1,512]{1,0:T(1,128)} %coupling_ref.1, f32[2,512]{1,0:T(2,128)} %bitcast.13, f32[1152,128]{1,0:T(8,128)} %bitcast.10, s32[1,128]{1,0:T(1,128)} %sea_hbm.1, f32[2,128]{1,0:T(2,128)} %bitcast.15), custom_call_target="tpu_custom_call" | custom-call | tf_op jit(solution)/shard_map/pallas_call | solution.py:354
  7.1 0.1 collective-permute-start.2
  7.2 1.2 %collective-permute-done.2 = f32[32,128]{1,0:T(8,128)S(1)} collective-permute-done((f32[32,128]{1,0:T(8,128)S(1)}, f32[32,128]{1,0:T(8,128)S(1)}, u32[]{:S(2)}, u32[]{:S(2)}) %collective-permute-start.2) | collective-permute-done | bytes 16416 | tf_op jit(solution)/shard_map/ppermute | solution.py:368
  8.3 0.0 copy-start.3
  8.3 1.0 %collective-permute-start.3 = (f32[32,128]{1,0:T(8,128)S(1)}, f32[32,128]{1,0:T(8,128)S(1)}, u32[]{:S(2)}, u32[]{:S(2)}) collective-permute-start(f32[32,128]{1,0:T(8,128)S(1)} %add.15), channel_id=1, source_target_pairs={{0,9},{1,8},{2,11},{3,10},{4,13},{5,12},{6,15},{7,14},{8,1},{9,0},... | collective-permute-start | bytes 49160 | tf_op jit(solution)/shard_map/ppermute | solution.py:347
  9.3 1.5 %collective-permute-start.4 = (f32[32,128]{1,0:T(8,128)S(1)}, f32[32,128]{1,0:T(8,128)S(1)}, u32[]{:S(2)}, u32[]{:S(2)}) collective-permute-start(f32[32,128]{1,0:T(8,128)S(1)} %add.15), channel_id=1, source_target_pairs={{0,17},{1,16},{2,19},{3,18},{4,21},{5,20},{6,23},{7,22},{8,25},{9,... | collective-permute-start | bytes 49160 | tf_op jit(solution)/shard_map/ppermute | solution.py:347
  10.8 0.5 %collective-permute-start.5 = (f32[32,128]{1,0:T(8,128)S(1)}, f32[32,128]{1,0:T(8,128)S(1)}, u32[]{:S(2)}, u32[]{:S(2)}) collective-permute-start(f32[32,128]{1,0:T(8,128)S(1)} %add.15), channel_id=1, source_target_pairs={{0,25},{1,24},{2,27},{3,26},{4,29},{5,28},{6,31},{7,30},{8,17},{9,... | collective-permute-start | bytes 49160 | tf_op jit(solution)/shard_map/ppermute | solution.py:347
  11.3 0.2 collective-permute-done.3
  11.5 1.0 %collective-permute-done.4 = f32[32,128]{1,0:T(8,128)S(1)} collective-permute-done((f32[32,128]{1,0:T(8,128)S(1)}, f32[32,128]{1,0:T(8,128)S(1)}, u32[]{:S(2)}, u32[]{:S(2)}) %collective-permute-start.4) | collective-permute-done | bytes 16416 | tf_op jit(solution)/shard_map/ppermute | solution.py:347
  12.5 2.4 %collective-permute-done.5 = f32[32,128]{1,0:T(8,128)S(1)} collective-permute-done((f32[32,128]{1,0:T(8,128)S(1)}, f32[32,128]{1,0:T(8,128)S(1)}, u32[]{:S(2)}, u32[]{:S(2)}) %collective-permute-start.5) | collective-permute-done | bytes 16416 | tf_op jit(solution)/shard_map/ppermute | solution.py:347
  14.8 0.0 collective-permute-start.6
  14.9 3.5 %collective-permute-start.7 = (f32[32,128]{1,0:T(8,128)S(1)}, f32[32,128]{1,0:T(8,128)S(1)}, u32[]{:S(2)}, u32[]{:S(2)}) collective-permute-start(f32[32,128]{1,0:T(8,128)S(1)} %add_add_fusion.band_ref), channel_id=1, source_target_pairs={{0,7},{1,6},{2,1},{3,0},{4,3},{5,2},{6,5},{7,4},{8,15},{9,14},{10,... | collective-permute-start | bytes 49160 | tf_op jit(solution)/shard_map/ppermute | solution.py:347
  18.4 1.7 %collective-permute-done.6.before_ref = f32[32,128]{1,0:T(8,128)S(1)} collective-permute-done((f32[32,128]{1,0:T(8,128)S(1)}, f32[32,128]{1,0:T(8,128)S(1)}, u32[]{:S(2)}, u32[]{:S(2)}) %collective-permute-start.6) | collective-permute-done | bytes 16416 | tf_op jit(solution)/shard_map/ppermute | solution.py:347
  20.1 0.0 collective-permute-done.7.after_ref
  20.1 0.0 collective-permute-done._.mate_ref
  20.1 0.0 copy-done
  20.1 0.0 copy-done.3
  20.1 0.0 copy-start.1
  20.1 1.6 %shard_map.78 = (f32[24,128]{1,0:T(8,128)S(1)}, f32[32,128]{1,0:T(8,128)S(1)}) custom-call(f32[64,128]{1,0:T(8,128)S(1)} %copy-done.3, f32[1152,128]{1,0:T(8,128)S(1)} %bitcast.11, f32[1152,128]{1,0:T(8,128)S(1)} %collective-permute-done._.mate_ref, f32[32,128]{1,0:T(8,128)S(1)} %add_add_fusion.band_ref, f32[32,128]{1,0:T(8,128)S(1)} %collective-permute-done.6.before_ref, ...), custom_call_target="tpu_custom_call" | custom-call | tf_op jit(solution)/shard_map/pallas_call | solution.py:376
  21.7 0.0 copy-done.1
  21.8 0.3 %collective-permute-start.8 = (f32[24,128]{1,0:T(8,128)S(1)}, f32[24,128]{1,0:T(8,128)S(1)}, u32[]{:S(2)}, u32[]{:S(2)}) collective-permute-start(f32[24,128]{1,0:T(8,128)S(1)} %get-tuple-element.5), channel_id=1, source_target_pairs={{0,1},{1,0},{2,3},{3,2},{4,5},{5,4},{6,7},{7,6},{8,9},{9,8},{10,11... | collective-permute-start | bytes 36872 | tf_op jit(solution)/shard_map/ppermute | solution.py:385
  22.1 0.9 %collective-permute-done.8 = f32[24,128]{1,0:T(8,128)S(1)} collective-permute-done((f32[24,128]{1,0:T(8,128)S(1)}, f32[24,128]{1,0:T(8,128)S(1)}, u32[]{:S(2)}, u32[]{:S(2)}) %collective-permute-start.8) | collective-permute-done | bytes 12320 | tf_op jit(solution)/shard_map/ppermute | solution.py:385
  23.0 3.4 %collective-permute-start.10 = (f32[24,128]{1,0:T(8,128)S(1)}, f32[24,128]{1,0:T(8,128)S(1)}, u32[]{:S(2)}, u32[]{:S(2)}) collective-permute-start(f32[24,128]{1,0:T(8,128)S(1)} %add.19.out_ref), channel_id=1, source_target_pairs={{0,7},{1,6},{2,1},{3,0},{4,3},{5,2},{6,5},{7,4},{8,15},{9,14},{10,... | collective-permute-start | bytes 36872 | tf_op jit(solution)/shard_map/ppermute | solution.py:347
  26.4 0.0 collective-permute-start.9
  26.4 0.0 collective-permute-done.1.other_ref
  26.4 0.0 copy-start.2
  26.4 1.1 %copy-done.2 = f32[1152,128]{1,0:T(8,128)S(1)} copy-done((f32[1152,128]{1,0:T(8,128)S(1)}, f32[1152,128]{1,0:T(8,128)}, u32[]{:S(2)}) %copy-start.2) | copy-done | bytes 589848
  27.5 1.6 %shard_map.79 = f32[1152,128]{1,0:T(8,128)S(1)} custom-call(f32[64,128]{1,0:T(8,128)S(1)} %copy-done.3, f32[1152,128]{1,0:T(8,128)S(1)} %bitcast.12, f32[1152,128]{1,0:T(8,128)S(1)} %copy-done.2, f32[1152,128]{1,0:T(8,128)S(1)} %collective-permute-done.1.other_ref, f32[32,128]{1,0:T(8,128)S(1)} %get-tuple-element.4.total_ref), custom_call_target="tpu_custom_call" | custom-call | tf_op jit(solution)/shard_map/pallas_call | solution.py:388
  29.1 0.0 copy-start.4
  29.1 0.8 %copy.9 = f32[1152,1,128]{2,1,0:T(1,128)} copy(f32[1152,1,128]{2,1,0:T(1,128)S(1)} %bitcast.7) | data formatting | bytes 1179648
  30.0 0.0 collective-permute-done.10.after_ref
  30.0 1.4 %collective-permute-done.9.before_ref = f32[24,128]{1,0:T(8,128)S(1)} collective-permute-done((f32[24,128]{1,0:T(8,128)S(1)}, f32[24,128]{1,0:T(8,128)S(1)}, u32[]{:S(2)}, u32[]{:S(2)}) %collective-permute-start.9) | collective-permute-done | bytes 12320 | tf_op jit(solution)/shard_map/ppermute | solution.py:347
  31.3 0.0 copy-done.4
  31.3 0.7 %shard_map.80 = f32[2,512]{1,0:T(2,128)} custom-call(s32[1,512]{1,0:T(1,128)S(1)} %copy-done.4, f32[32,128]{1,0:T(8,128)S(1)} %get-tuple-element.4.total_ref, f32[24,128]{1,0:T(8,128)S(1)} %add.19.out_ref, f32[24,128]{1,0:T(8,128)S(1)} %collective-permute-done.9.before_ref, f32[24,128]{1,0:T(8,128)S(1)} %collective-permute-done.10.after_ref), custom_call_target="tpu_custom_call" | custom-call | tf_op jit(solution)/shard_map/pallas_call | solution.py:394
  (3 shorter events, 0.0 us)
Async XLA Ops:
  0.6 19.4 %copy-start = (f32[1152,1,128]{2,1,0:T(1,128)S(1)}, f32[1152,1,128]{2,1,0:T(1,128)}, u32[]{:S(2)}) copy-start(f32[1152,1,128]{2,1,0:T(1,128)} %param.6) | copy-start | bytes 1769476
  0.6 19.4 %collective-permute-start = (f32[1152,128]{1,0:T(8,128)}, f32[1152,128]{1,0:T(8,128)S(1)}, u32[]{:S(2)}, u32[]{:S(2)}) collective-permute-start(f32[1152,128]{1,0:T(8,128)} %bitcast.8), channel_id=1, source_target_pairs={{0,1},{1,0},{2,3},{3,2},{4,5},{5,4},{6,7},{7,6},{8,9},{9,8},{10,11... | collective-permute-start | bytes 1769480 | tf_op jit(solution)/shard_map/ppermute | solution.py:350
  1.2 25.3 %collective-permute-start.1 = (f32[1152,128]{1,0:T(8,128)}, f32[1152,128]{1,0:T(8,128)S(1)}, u32[]{:S(2)}, u32[]{:S(2)}) collective-permute-start(f32[1152,128]{1,0:T(8,128)} %bitcast.9), channel_id=1, source_target_pairs={{0,7},{1,2},{2,1},{3,4},{4,3},{5,6},{6,5},{7,0},{8,15},{9,10},{10,... | collective-permute-start | bytes 1769480 | tf_op jit(solution)/shard_map/ppermute | solution.py:351
  7.1 1.2 %collective-permute-start.2 = (f32[32,128]{1,0:T(8,128)S(1)}, f32[32,128]{1,0:T(8,128)S(1)}, u32[]{:S(2)}, u32[]{:S(2)}) collective-permute-start(f32[32,128]{1,0:T(8,128)S(1)} %shard_map.77), channel_id=1, source_target_pairs={{0,1},{1,0},{2,3},{3,2},{4,5},{5,4},{6,7},{7,6},{8,9},{9,8},{10,11... | collective-permute-start | bytes 49160 | tf_op jit(solution)/shard_map/ppermute | solution.py:368
  8.3 11.7 %copy-start.3 = (f32[64,128]{1,0:T(8,128)S(1)}, f32[64,128]{1,0:T(8,128)}, u32[]{:S(2)}) copy-start(f32[64,128]{1,0:T(8,128)} %constant.2.clone.table_ref) | copy-start | bytes 98308
  8.3 3.2 %collective-permute-start.3 = (f32[32,128]{1,0:T(8,128)S(1)}, f32[32,128]{1,0:T(8,128)S(1)}, u32[]{:S(2)}, u32[]{:S(2)}) collective-permute-start(f32[32,128]{1,0:T(8,128)S(1)} %add.15), channel_id=1, source_target_pairs={{0,9},{1,8},{2,11},{3,10},{4,13},{5,12},{6,15},{7,14},{8,1},{9,0},... | collective-permute-start | bytes 49160 | tf_op jit(solution)/shard_map/ppermute | solution.py:347
  9.3 3.2 %collective-permute-start.4 = (f32[32,128]{1,0:T(8,128)S(1)}, f32[32,128]{1,0:T(8,128)S(1)}, u32[]{:S(2)}, u32[]{:S(2)}) collective-permute-start(f32[32,128]{1,0:T(8,128)S(1)} %add.15), channel_id=1, source_target_pairs={{0,17},{1,16},{2,19},{3,18},{4,21},{5,20},{6,23},{7,22},{8,25},{9,... | collective-permute-start | bytes 49160 | tf_op jit(solution)/shard_map/ppermute | solution.py:347
  10.8 4.1 %collective-permute-start.5 = (f32[32,128]{1,0:T(8,128)S(1)}, f32[32,128]{1,0:T(8,128)S(1)}, u32[]{:S(2)}, u32[]{:S(2)}) collective-permute-start(f32[32,128]{1,0:T(8,128)S(1)} %add.15), channel_id=1, source_target_pairs={{0,25},{1,24},{2,27},{3,26},{4,29},{5,28},{6,31},{7,30},{8,17},{9,... | collective-permute-start | bytes 49160 | tf_op jit(solution)/shard_map/ppermute | solution.py:347
  14.8 5.2 %collective-permute-start.6 = (f32[32,128]{1,0:T(8,128)S(1)}, f32[32,128]{1,0:T(8,128)S(1)}, u32[]{:S(2)}, u32[]{:S(2)}) collective-permute-start(f32[32,128]{1,0:T(8,128)S(1)} %add_add_fusion.band_ref), channel_id=1, source_target_pairs={{0,3},{1,2},{2,5},{3,4},{4,7},{5,6},{6,1},{7,0},{8,11},{9,10},{10,... | collective-permute-start | bytes 49160 | tf_op jit(solution)/shard_map/ppermute | solution.py:347
  14.9 5.2 %collective-permute-start.7 = (f32[32,128]{1,0:T(8,128)S(1)}, f32[32,128]{1,0:T(8,128)S(1)}, u32[]{:S(2)}, u32[]{:S(2)}) collective-permute-start(f32[32,128]{1,0:T(8,128)S(1)} %add_add_fusion.band_ref), channel_id=1, source_target_pairs={{0,7},{1,6},{2,1},{3,0},{4,3},{5,2},{6,5},{7,4},{8,15},{9,14},{10,... | collective-permute-start | bytes 49160 | tf_op jit(solution)/shard_map/ppermute | solution.py:347
  20.1 1.7 %copy-start.1 = (f32[1152,128]{1,0:T(8,128)}, f32[1152,128]{1,0:T(8,128)S(1)}, u32[]{:S(2)}) copy-start(f32[1152,128]{1,0:T(8,128)S(1)} %collective-permute-done._.mate_ref) | copy-start | bytes 1769476
  21.8 1.2 %collective-permute-start.8 = (f32[24,128]{1,0:T(8,128)S(1)}, f32[24,128]{1,0:T(8,128)S(1)}, u32[]{:S(2)}, u32[]{:S(2)}) collective-permute-start(f32[24,128]{1,0:T(8,128)S(1)} %get-tuple-element.5), channel_id=1, source_target_pairs={{0,1},{1,0},{2,3},{3,2},{4,5},{5,4},{6,7},{7,6},{8,9},{9,8},{10,11... | collective-permute-start | bytes 36872 | tf_op jit(solution)/shard_map/ppermute | solution.py:385
  23.0 7.0 %collective-permute-start.10 = (f32[24,128]{1,0:T(8,128)S(1)}, f32[24,128]{1,0:T(8,128)S(1)}, u32[]{:S(2)}, u32[]{:S(2)}) collective-permute-start(f32[24,128]{1,0:T(8,128)S(1)} %add.19.out_ref), channel_id=1, source_target_pairs={{0,7},{1,6},{2,1},{3,0},{4,3},{5,2},{6,5},{7,4},{8,15},{9,14},{10,... | collective-permute-start | bytes 36872 | tf_op jit(solution)/shard_map/ppermute | solution.py:347
  26.4 4.9 %collective-permute-start.9 = (f32[24,128]{1,0:T(8,128)S(1)}, f32[24,128]{1,0:T(8,128)S(1)}, u32[]{:S(2)}, u32[]{:S(2)}) collective-permute-start(f32[24,128]{1,0:T(8,128)S(1)} %add.19.out_ref), channel_id=1, source_target_pairs={{0,3},{1,2},{2,5},{3,4},{4,7},{5,6},{6,1},{7,0},{8,11},{9,10},{10,... | collective-permute-start | bytes 36872 | tf_op jit(solution)/shard_map/ppermute | solution.py:347
  26.4 1.1 %copy-start.2 = (f32[1152,128]{1,0:T(8,128)S(1)}, f32[1152,128]{1,0:T(8,128)}, u32[]{:S(2)}) copy-start(f32[1152,128]{1,0:T(8,128)} %copy-done.1) | copy-start | bytes 1769476
  29.1 2.2 %copy-start.4 = (s32[1,512]{1,0:T(1,128)S(1)}, s32[1,512]{1,0:T(1,128)}, u32[]{:S(2)}) copy-start(s32[1,512]{1,0:T(1,128)} %coupling_ref.1) | copy-start | bytes 6148

commit v4 on v2

--- a/solution.py
+++ b/solution.py
@@ -36,7 +36,7 @@
 
 
 def level_groups(levels):
-    for size in (4, 3, 2):
+    for size in (12, 6, 4, 3, 2):
         if levels % size == 0:
             return levels // size, size
     return levels, 1
@@ -51,14 +51,24 @@
     return row, slot
 
 
-def band_kernel(columns, coupling_ref, currents_ref, spectrum_ref, sea_ref, wind_ref, band_ref):
-    width = spectrum_ref.shape[1]
-    bins = spectrum_ref.shape[0]
+def band_kernel(
+    columns, coupling_hbm, currents_hbm, spectrum_ref, sea_hbm, wind_hbm, band_ref,
+    coupling_ref, currents_ref, sea_ref, wind_ref, sems,
+):
+    bins, width = spectrum_ref.shape
     first, odd, group = place()
     is_ocean = group > 0
 
     @pl.when(is_ocean)
     def _():
+        copies = [
+            pltpu.make_async_copy(coupling_hbm, coupling_ref, sems.at[0]),
+            pltpu.make_async_copy(currents_hbm, currents_ref, sems.at[1]),
+        ]
+        for copy in copies:
+            copy.start()
+        for copy in copies:
+            copy.wait()
         row, slot = slots_of(coupling_ref[...], width, first, columns)
         cells = row.shape[1]
         parts_x, parts_y = [], []
@@ -87,6 +97,12 @@
 
     @pl.when(jnp.logical_not(is_ocean))
     def _():
+        copies = [
+            pltpu.make_async_copy(sea_hbm, sea_ref, sems.at[2]),
+            pltpu.make_async_copy(wind_hbm, wind_ref, sems.at[3]),
+        ]
+        for copy in copies:
+            copy.start()
         band_ref[...] = jnp.zeros_like(band_ref)
         total = jnp.zeros((8, width), jnp.float32)
         moment = jnp.zeros((8, width), jnp.float32)
@@ -96,6 +112,8 @@
             block = block[0:8] + block[8:16] + (block[16:24] + block[24:32])
             total += (0.1 * frequency) * block
             moment += (0.1 * frequency * frequency) * block
+        for copy in copies:
+            copy.wait()
         sea = sea_ref[...].astype(jnp.float32)
         total = jnp.sum(total, axis=0, keepdims=True) * sea
         moment = jnp.sum(moment, axis=0, keepdims=True) * sea
@@ -238,30 +256,46 @@
     bins, _, width = spectrum.shape
     devices = lax.axis_size("dev")
     groups = lax.axis_size("grp")
+    cells = coupling.shape[1]
     mates = [(i, i ^ 1) for i in range(devices)]
     others = [(i, (i + (1 if i % 2 else -1)) % devices) for i in range(devices)]
 
-    def shifted(value, steps):
-        return lax.ppermute(value, "dev", [(i, (i + steps) % devices) for i in range(devices)])
+    def crossed(value, group_step, chip_step):
+        def target(group, dev):
+            if groups & (groups - 1):
+                group = (group + group_step) % groups
+            else:
+                group = group ^ group_step
+            return group * devices + ((dev + 2 * chip_step) % devices ^ 1)
+
+        pairs = [(g * devices + d, target(g, d)) for g in range(groups) for d in range(devices)]
+        return lax.ppermute(value, ("grp", "dev"), pairs)
 
     own = spectrum.reshape(bins, width)
+    mate = lax.ppermute(own, "dev", mates)
     other = lax.ppermute(own, "dev", others)
-    mate = lax.ppermute(own, "dev", mates)
-
+
+    anywhere = pl.BlockSpec(memory_space=pl.ANY)
     band = pl.pallas_call(
         functools.partial(band_kernel, devices),
         out_shape=pltpu.VMEM((FIELDS * SLOTS, width), jnp.float32),
-        in_specs=[VMEM] * 5,
+        in_specs=[anywhere, anywhere, VMEM, anywhere, anywhere],
         out_specs=VMEM,
-    )(*near(coupling, currents[0], own, sea_mask, wind[:, 0]))
+        scratch_shapes=[
+            pltpu.VMEM((1, cells), jnp.int32),
+            pltpu.VMEM((2, cells), jnp.float32),
+            pltpu.VMEM((1, width), jnp.int32),
+            pltpu.VMEM((2, width), jnp.float32),
+            pltpu.SemaphoreType.DMA((4,)),
+        ],
+    )(coupling, currents[0], *near(own), sea_mask, wind[:, 0])
     band = band + lax.ppermute(band, "dev", mates)
     band, mate = lax.optimization_barrier((band, mate))
-    reach = 1
-    while reach < groups:
-        band = band + lax.ppermute(band, "grp", [(i, i ^ reach) for i in range(groups)])
-        reach *= 2
-    before = shifted(band, 2)
-    after = shifted(band, -2)
+    parts = [crossed(band, step, 0) for step in range(1, groups)]
+    for part in parts:
+        band = band + part
+    before = crossed(band, 0, 1)
+    after = crossed(band, 0, -1)
 
     updated, drift = pl.pallas_call(
         step_kernel,
@@ -275,13 +309,13 @@
 
     drift_other = lax.ppermute(drift, "dev", others)
     drift_mate = lax.ppermute(drift, "dev", mates)
-    cells = pl.pallas_call(
+    cell_drift = pl.pallas_call(
         functools.partial(pick_kernel, devices),
         out_shape=jax.ShapeDtypeStruct(currents.shape[1:], jnp.float32),
         in_specs=[VMEM] * 4,
         out_specs=VMEM,
     )(*near(coupling, drift, drift_mate, drift_other))
-    return updated.reshape(spectrum.shape), cells[None]
+    return updated.reshape(spectrum.shape), cell_drift[None]
 
 
 def solution(mesh):

time: 30.7 us -> 27.4 us (0.89)
  waiting for transfers between devices: 13.4 us -> 10.4 us
  local copies, waits for them, and re-layouts: 3.26 us -> 1.92 us
  starting transfers between devices: 10.6 us -> 11.7 us
    ppermute x4 -> x5, waiting for transfers between devices: 8.29 us -> 4.27 us  [crossed(): return lax.ppermute(value, ('grp', 'dev'), pairs)]
    ppermute x1, waiting for transfers between devices: 0.05 us -> 2.46 us  [body(): other = lax.ppermute(own, 'dev', others)]
    ppermute x1, starting transfers between devices: 0.07 us -> 1.62 us  [body(): drift_other = lax.ppermute(drift, 'dev', others)]
    ppermute x1, waiting for transfers between devices: 3.92 us -> 2.45 us  [body(): drift_other = lax.ppermute(drift, 'dev', others)]
    unnamed x15 -> x7, local copies, waits for them, and re-layouts: 3.26 us -> 1.92 us
    pallas_call x1, Pallas kernels: 0.06 us -> 0.75 us  [body(): pl.pallas_call(functools.partial(band_kernel, devices), out_shape=pltpu.V...]
    pallas_call x1, Pallas kernels: 1.67 us -> 1.05 us  [body(): pl.pallas_call(step_kernel, out_shape=(pltpu.VMEM((bins, width), jnp.floa...]
    ppermute x4 -> x5, starting transfers between devices: 5.18 us -> 4.79 us  [crossed(): return lax.ppermute(value, ('grp', 'dev'), pairs)]
  transfers between devices with their start and end apart: 9 -> 10, of which waited for: 7 -> 7; matrix products, arithmetic and copies ran while one was open for 3% -> 3% of each run, Pallas kernels for 0% -> 3%
where the time goes in v4:
time: 27.4 us; the launch traced here: 27.2 us
  starting transfers between devices  11.7 us (43%)
  waiting for transfers between devices  10.4 us (38%)
  Pallas kernels  2.51 us (9%)
  local copies, waits for them, and re-layouts  1.92 us (7%)
  between operations  0.66 us (2%)
    ppermute x5, starting transfers between devices, crossed(): return lax.ppermute(value, ('grp', 'dev'), pairs)  4.79 us
    ppermute x1, starting transfers between devices, body(): other = lax.ppermute(own, 'dev', others)  4.71 us
    ppermute x5, waiting for transfers between devices, crossed(): return lax.ppermute(value, ('grp', 'dev'), pairs)  4.27 us
    ppermute x1, waiting for transfers between devices, body(): other = lax.ppermute(own, 'dev', others)  2.46 us
    ppermute x1, waiting for transfers between devices, body(): drift_other = lax.ppermute(drift, 'dev', others)  2.45 us
    unnamed x7, local copies, waits for them, and re-layouts  1.92 us
    ppermute x1, starting transfers between devices, body(): drift_other = lax.ppermute(drift, 'dev', others)  1.62 us
    ppermute x1, waiting for transfers between devices, body(): band = band + lax.ppermute(band, 'dev', mates)  1.17 us
  transfers between devices with their start and end apart: 10, of which 7 were waited for; matrix products, arithmetic and copies ran while one was open for 3% of the time, Pallas kernels for 3%

profile of v4, /device:TPU:0, one launch (start us, length us, event | category | flops | bytes accessed | tf_op | source)
XLA Modules:
  0.0 27.2 jit_solution(1737742314311660507)
XLA Ops:
  0.6 0.5 %collective-permute-start.1 = (f32[1152,128]{1,0:T(8,128)}, f32[1152,128]{1,0:T(8,128)S(1)}, u32[]{:S(2)}, u32[]{:S(2)}) collective-permute-start(f32[1152,128]{1,0:T(8,128)} %bitcast.8), channel_id=1, source_target_pairs={{0,1},{1,0},{2,3},{3,2},{4,5},{5,4},{6,7},{7,6},{8,9},{9,8},{10,11... | collective-permute-start | bytes 1769480 | tf_op jit(solution)/shard_map/ppermute | solution.py:275
  1.1 4.7 %collective-permute-start.2 = (f32[1152,128]{1,0:T(8,128)}, f32[1152,128]{1,0:T(8,128)S(1)}, u32[]{:S(2)}, u32[]{:S(2)}) collective-permute-start(f32[1152,128]{1,0:T(8,128)} %bitcast.9), channel_id=1, source_target_pairs={{0,7},{1,2},{2,1},{3,4},{4,3},{5,6},{6,5},{7,0},{8,15},{9,10},{10,... | collective-permute-start | bytes 1769480 | tf_op jit(solution)/shard_map/ppermute | solution.py:276
  5.9 0.0 copy-start
  5.9 1.1 %copy-done = f32[1152,1,128]{2,1,0:T(1,128)S(1)} copy-done((f32[1152,1,128]{2,1,0:T(1,128)S(1)}, f32[1152,1,128]{2,1,0:T(1,128)}, u32[]{:S(2)}) %copy-start) | copy-done | bytes 589848
  7.0 0.8 %shard_map.77 = f32[32,128]{1,0:T(8,128)S(1)} custom-call(s32[1,512]{1,0:T(1,128)} %coupling_ref.1, f32[2,512]{1,0:T(2,128)} %bitcast.12, f32[1152,128]{1,0:T(8,128)S(1)} %bitcast.10, s32[1,128]{1,0:T(1,128)} %sea_hbm.1, f32[2,128]{1,0:T(2,128)} %bitcast.14), custom_call_target="tpu_custom_call" | custom-call | tf_op jit(solution)/shard_map/pallas_call | solution.py:279
  7.7 0.1 collective-permute-start
  7.8 1.2 %collective-permute-done = f32[32,128]{1,0:T(8,128)S(1)} collective-permute-done((f32[32,128]{1,0:T(8,128)S(1)}, f32[32,128]{1,0:T(8,128)S(1)}, u32[]{:S(2)}, u32[]{:S(2)}) %collective-permute-start) | collective-permute-done | bytes 16416 | tf_op jit(solution)/shard_map/ppermute | solution.py:292
  9.0 0.0 copy-start.1
  9.0 0.0 collective-permute-done.1.mate_ref
  9.0 2.4 %collective-permute-start.5 = (f32[32,128]{1,0:T(8,128)S(1)}, f32[32,128]{1,0:T(8,128)S(1)}, u32[]{:S(2)}, u32[]{:S(2)}) collective-permute-start(f32[32,128]{1,0:T(8,128)S(1)} %add.12), channel_id=1, source_target_pairs={{0,25},{1,24},{2,27},{3,26},{4,29},{5,28},{6,31},{7,30},{8,17},{9,... | collective-permute-start | bytes 49160 | tf_op jit(solution)/shard_map/ppermute | solution.py:272
  11.4 0.5 %collective-permute-start.4 = (f32[32,128]{1,0:T(8,128)S(1)}, f32[32,128]{1,0:T(8,128)S(1)}, u32[]{:S(2)}, u32[]{:S(2)}) collective-permute-start(f32[32,128]{1,0:T(8,128)S(1)} %add.12), channel_id=1, source_target_pairs={{0,17},{1,16},{2,19},{3,18},{4,21},{5,20},{6,23},{7,22},{8,25},{9,... | collective-permute-start | bytes 49160 | tf_op jit(solution)/shard_map/ppermute | solution.py:272
  11.9 0.2 collective-permute-start.3
  12.0 1.1 %collective-permute-done.5 = f32[32,128]{1,0:T(8,128)S(1)} collective-permute-done((f32[32,128]{1,0:T(8,128)S(1)}, f32[32,128]{1,0:T(8,128)S(1)}, u32[]{:S(2)}, u32[]{:S(2)}) %collective-permute-start.5) | collective-permute-done | bytes 16416 | tf_op jit(solution)/shard_map/ppermute | solution.py:272
  13.1 1.5 %collective-permute-done.4 = f32[32,128]{1,0:T(8,128)S(1)} collective-permute-done((f32[32,128]{1,0:T(8,128)S(1)}, f32[32,128]{1,0:T(8,128)S(1)}, u32[]{:S(2)}, u32[]{:S(2)}) %collective-permute-start.4) | collective-permute-done | bytes 16416 | tf_op jit(solution)/shard_map/ppermute | solution.py:272
  14.6 0.5 %collective-permute-done.3 = f32[32,128]{1,0:T(8,128)S(1)} collective-permute-done((f32[32,128]{1,0:T(8,128)S(1)}, f32[32,128]{1,0:T(8,128)S(1)}, u32[]{:S(2)}, u32[]{:S(2)}) %collective-permute-start.3) | collective-permute-done | bytes 16416 | tf_op jit(solution)/shard_map/ppermute | solution.py:272
  15.0 0.5 %collective-permute-start.7 = (f32[32,128]{1,0:T(8,128)S(1)}, f32[32,128]{1,0:T(8,128)S(1)}, u32[]{:S(2)}, u32[]{:S(2)}) collective-permute-start(f32[32,128]{1,0:T(8,128)S(1)} %add_add_fusion.band_ref), channel_id=1, source_target_pairs={{0,7},{1,6},{2,1},{3,0},{4,3},{5,2},{6,5},{7,4},{8,15},{9,14},{10,... | collective-permute-start | bytes 49160 | tf_op jit(solution)/shard_map/ppermute | solution.py:272
  15.6 1.2 %collective-permute-start.6 = (f32[32,128]{1,0:T(8,128)S(1)}, f32[32,128]{1,0:T(8,128)S(1)}, u32[]{:S(2)}, u32[]{:S(2)}) collective-permute-start(f32[32,128]{1,0:T(8,128)S(1)} %add_add_fusion.band_ref), channel_id=1, source_target_pairs={{0,3},{1,2},{2,5},{3,4},{4,7},{5,6},{6,1},{7,0},{8,11},{9,10},{10,... | collective-permute-start | bytes 49160 | tf_op jit(solution)/shard_map/ppermute | solution.py:272
  16.8 2.5 %collective-permute-done.2.other_ref = f32[1152,128]{1,0:T(8,128)S(1)} collective-permute-done((f32[1152,128]{1,0:T(8,128)}, f32[1152,128]{1,0:T(8,128)S(1)}, u32[]{:S(2)}, u32[]{:S(2)}) %collective-permute-start.2) | collective-permute-done | bytes 589856 | tf_op jit(solution)/shard_map/ppermute | solution.py:276
  19.3 0.0 collective-permute-done.7.after_ref
  19.3 1.3 %collective-permute-done.6.before_ref = f32[32,128]{1,0:T(8,128)S(1)} collective-permute-done((f32[32,128]{1,0:T(8,128)S(1)}, f32[32,128]{1,0:T(8,128)S(1)}, u32[]{:S(2)}, u32[]{:S(2)}) %collective-permute-start.6) | collective-permute-done | bytes 16416 | tf_op jit(solution)/shard_map/ppermute | solution.py:272
  20.5 0.0 copy-done.1
  20.5 1.1 %shard_map.78 = (f32[1152,128]{1,0:T(8,128)S(1)}, f32[8,128]{1,0:T(8,128)S(1)}) custom-call(f32[64,128]{1,0:T(8,128)S(1)} %copy-done.1, f32[1152,128]{1,0:T(8,128)S(1)} %bitcast.11, f32[1152,128]{1,0:T(8,128)S(1)} %collective-permute-done.1.mate_ref, f32[1152,128]{1,0:T(8,128)S(1)} %collective-permute-done.2.other_ref, f32[32,128]{1,0:T(8,128)S(1)} %add_add_fusion.band_ref, ...), custom_call_target="tpu_custom_call" | custom-call | tf_op jit(solution)/shard_map/pallas_call | solution.py:300
  21.6 1.6 %collective-permute-start.9 = (f32[8,128]{1,0:T(8,128)S(1)}, f32[8,128]{1,0:T(8,128)S(1)}, u32[]{:S(2)}, u32[]{:S(2)}) collective-permute-start(f32[8,128]{1,0:T(8,128)S(1)} %get-tuple-element.9.own_ref), channel_id=1, source_target_pairs={{0,7},{1,2},{2,1},{3,4},{4,3},{5,6},{6,5},{7,0},{8,15},{9,10},{10,... | collective-permute-start | bytes 12296 | tf_op jit(solution)/shard_map/ppermute | solution.py:310
  23.2 0.0 collective-permute-start.8
  23.2 0.0 copy-start.2
  23.2 0.8 %copy.9 = f32[1152,1,128]{2,1,0:T(1,128)} copy(f32[1152,1,128]{2,1,0:T(1,128)S(1)} %bitcast.7) | data formatting | bytes 1179648
  24.0 2.5 %collective-permute-done.9.other_ref = f32[8,128]{1,0:T(8,128)S(1)} collective-permute-done((f32[8,128]{1,0:T(8,128)S(1)}, f32[8,128]{1,0:T(8,128)S(1)}, u32[]{:S(2)}, u32[]{:S(2)}) %collective-permute-start.9) | collective-permute-done | bytes 4128 | tf_op jit(solution)/shard_map/ppermute | solution.py:310
  26.5 0.0 collective-permute-done.8.mate_ref
  26.5 0.0 copy-done.2
  26.5 0.7 %shard_map.79 = f32[2,512]{1,0:T(2,128)} custom-call(s32[1,512]{1,0:T(1,128)S(1)} %copy-done.2, f32[8,128]{1,0:T(8,128)S(1)} %get-tuple-element.9.own_ref, f32[8,128]{1,0:T(8,128)S(1)} %collective-permute-done.8.mate_ref, f32[8,128]{1,0:T(8,128)S(1)} %collective-permute-done.9.other_ref), custom_call_target="tpu_custom_call" | custom-call | tf_op jit(solution)/shard_map/pallas_call | solution.py:312
  (2 shorter events, 0.0 us)
Async XLA Ops:
  0.6 8.3 %collective-permute-start.1 = (f32[1152,128]{1,0:T(8,128)}, f32[1152,128]{1,0:T(8,128)S(1)}, u32[]{:S(2)}, u32[]{:S(2)}) collective-permute-start(f32[1152,128]{1,0:T(8,128)} %bitcast.8), channel_id=1, source_target_pairs={{0,1},{1,0},{2,3},{3,2},{4,5},{5,4},{6,7},{7,6},{8,9},{9,8},{10,11... | collective-permute-start | bytes 1769480 | tf_op jit(solution)/shard_map/ppermute | solution.py:275
  1.1 18.1 %collective-permute-start.2 = (f32[1152,128]{1,0:T(8,128)}, f32[1152,128]{1,0:T(8,128)S(1)}, u32[]{:S(2)}, u32[]{:S(2)}) collective-permute-start(f32[1152,128]{1,0:T(8,128)} %bitcast.9), channel_id=1, source_target_pairs={{0,7},{1,2},{2,1},{3,4},{4,3},{5,6},{6,5},{7,0},{8,15},{9,10},{10,... | collective-permute-start | bytes 1769480 | tf_op jit(solution)/shard_map/ppermute | solution.py:276
  5.9 1.1 %copy-start = (f32[1152,1,128]{2,1,0:T(1,128)S(1)}, f32[1152,1,128]{2,1,0:T(1,128)}, u32[]{:S(2)}) copy-start(f32[1152,1,128]{2,1,0:T(1,128)} %param.6) | copy-start | bytes 1769476
  7.7 1.2 %collective-permute-start = (f32[32,128]{1,0:T(8,128)S(1)}, f32[32,128]{1,0:T(8,128)S(1)}, u32[]{:S(2)}, u32[]{:S(2)}) collective-permute-start(f32[32,128]{1,0:T(8,128)S(1)} %shard_map.77), channel_id=1, source_target_pairs={{0,1},{1,0},{2,3},{3,2},{4,5},{5,4},{6,7},{7,6},{8,9},{9,8},{10,11... | collective-permute-start | bytes 49160 | tf_op jit(solution)/shard_map/ppermute | solution.py:292
  9.0 11.5 %copy-start.1 = (f32[64,128]{1,0:T(8,128)S(1)}, f32[64,128]{1,0:T(8,128)}, u32[]{:S(2)}) copy-start(f32[64,128]{1,0:T(8,128)} %constant.2.clone.table_ref) | copy-start | bytes 98308
  9.0 4.1 %collective-permute-start.5 = (f32[32,128]{1,0:T(8,128)S(1)}, f32[32,128]{1,0:T(8,128)S(1)}, u32[]{:S(2)}, u32[]{:S(2)}) collective-permute-start(f32[32,128]{1,0:T(8,128)S(1)} %add.12), channel_id=1, source_target_pairs={{0,25},{1,24},{2,27},{3,26},{4,29},{5,28},{6,31},{7,30},{8,17},{9,... | collective-permute-start | bytes 49160 | tf_op jit(solution)/shard_map/ppermute | solution.py:272
  11.4 3.2 %collective-permute-start.4 = (f32[32,128]{1,0:T(8,128)S(1)}, f32[32,128]{1,0:T(8,128)S(1)}, u32[]{:S(2)}, u32[]{:S(2)}) collective-permute-start(f32[32,128]{1,0:T(8,128)S(1)} %add.12), channel_id=1, source_target_pairs={{0,17},{1,16},{2,19},{3,18},{4,21},{5,20},{6,23},{7,22},{8,25},{9,... | collective-permute-start | bytes 49160 | tf_op jit(solution)/shard_map/ppermute | solution.py:272
  11.9 3.2 %collective-permute-start.3 = (f32[32,128]{1,0:T(8,128)S(1)}, f32[32,128]{1,0:T(8,128)S(1)}, u32[]{:S(2)}, u32[]{:S(2)}) collective-permute-start(f32[32,128]{1,0:T(8,128)S(1)} %add.12), channel_id=1, source_target_pairs={{0,9},{1,8},{2,11},{3,10},{4,13},{5,12},{6,15},{7,14},{8,1},{9,0},... | collective-permute-start | bytes 49160 | tf_op jit(solution)/shard_map/ppermute | solution.py:272
  15.0 4.2 %collective-permute-start.7 = (f32[32,128]{1,0:T(8,128)S(1)}, f32[32,128]{1,0:T(8,128)S(1)}, u32[]{:S(2)}, u32[]{:S(2)}) collective-permute-start(f32[32,128]{1,0:T(8,128)S(1)} %add_add_fusion.band_ref), channel_id=1, source_target_pairs={{0,7},{1,6},{2,1},{3,0},{4,3},{5,2},{6,5},{7,4},{8,15},{9,14},{10,... | collective-permute-start | bytes 49160 | tf_op jit(solution)/shard_map/ppermute | solution.py:272
  15.6 5.0 %collective-permute-start.6 = (f32[32,128]{1,0:T(8,128)S(1)}, f32[32,128]{1,0:T(8,128)S(1)}, u32[]{:S(2)}, u32[]{:S(2)}) collective-permute-start(f32[32,128]{1,0:T(8,128)S(1)} %add_add_fusion.band_ref), channel_id=1, source_target_pairs={{0,3},{1,2},{2,5},{3,4},{4,7},{5,6},{6,1},{7,0},{8,11},{9,10},{10,... | collective-permute-start | bytes 49160 | tf_op jit(solution)/shard_map/ppermute | solution.py:272
  21.6 4.9 %collective-permute-start.9 = (f32[8,128]{1,0:T(8,128)S(1)}, f32[8,128]{1,0:T(8,128)S(1)}, u32[]{:S(2)}, u32[]{:S(2)}) collective-permute-start(f32[8,128]{1,0:T(8,128)S(1)} %get-tuple-element.9.own_ref), channel_id=1, source_target_pairs={{0,7},{1,2},{2,1},{3,4},{4,3},{5,6},{6,5},{7,0},{8,15},{9,10},{10,... | collective-permute-start | bytes 12296 | tf_op jit(solution)/shard_map/ppermute | solution.py:310
  23.2 3.3 %collective-permute-start.8 = (f32[8,128]{1,0:T(8,128)S(1)}, f32[8,128]{1,0:T(8,128)S(1)}, u32[]{:S(2)}, u32[]{:S(2)}) collective-permute-start(f32[8,128]{1,0:T(8,128)S(1)} %get-tuple-element.9.own_ref), channel_id=1, source_target_pairs={{0,1},{1,0},{2,3},{3,2},{4,5},{5,4},{6,7},{7,6},{8,9},{9,8},{10,11... | collective-permute-start | bytes 12296 | tf_op jit(solution)/shard_map/ppermute | solution.py:311
  23.2 3.3 %copy-start.2 = (s32[1,512]{1,0:T(1,128)S(1)}, s32[1,512]{1,0:T(1,128)}, u32[]{:S(2)}) copy-start(s32[1,512]{1,0:T(1,128)} %coupling_ref.1) | copy-start | bytes 6148

commit v5 on v4

--- a/solution.py
+++ b/solution.py
@@ -52,12 +52,14 @@
 
 
 def band_kernel(
-    columns, coupling_hbm, currents_hbm, spectrum_ref, sea_hbm, wind_hbm, band_ref,
+    columns, coupling_hbm, currents_hbm, spectrum_hbm, sea_hbm, wind_hbm, band_ref, spectrum_ref,
     coupling_ref, currents_ref, sea_ref, wind_ref, sems,
 ):
     bins, width = spectrum_ref.shape
     first, odd, group = place()
     is_ocean = group > 0
+    fetch = pltpu.make_async_copy(spectrum_hbm, spectrum_ref, sems.at[4])
+    fetch.start()
 
     @pl.when(is_ocean)
     def _():
@@ -94,6 +96,7 @@
         band_ref[0:step, :] = sums[0:step] + sums[step : 2 * step] + sums[2 * step : 3 * step]
         band_ref[step : 2 * step, :] = sums[3 * step : 4 * step]
         band_ref[2 * step : 4 * step, :] = jnp.zeros((2 * step, width), jnp.float32)
+        fetch.wait()
 
     @pl.when(jnp.logical_not(is_ocean))
     def _():
@@ -104,6 +107,7 @@
         for copy in copies:
             copy.start()
         band_ref[...] = jnp.zeros_like(band_ref)
+        fetch.wait()
         total = jnp.zeros((8, width), jnp.float32)
         moment = jnp.zeros((8, width), jnp.float32)
         for level in range(bins // NDIR):
@@ -276,19 +280,22 @@
     other = lax.ppermute(own, "dev", others)
 
     anywhere = pl.BlockSpec(memory_space=pl.ANY)
-    band = pl.pallas_call(
+    band, own_near = pl.pallas_call(
         functools.partial(band_kernel, devices),
-        out_shape=pltpu.VMEM((FIELDS * SLOTS, width), jnp.float32),
-        in_specs=[anywhere, anywhere, VMEM, anywhere, anywhere],
-        out_specs=VMEM,
+        out_shape=(
+            pltpu.VMEM((FIELDS * SLOTS, width), jnp.float32),
+            pltpu.VMEM((bins, width), jnp.float32),
+        ),
+        in_specs=[anywhere] * 5,
+        out_specs=(VMEM, VMEM),
         scratch_shapes=[
             pltpu.VMEM((1, cells), jnp.int32),
             pltpu.VMEM((2, cells), jnp.float32),
             pltpu.VMEM((1, width), jnp.int32),
             pltpu.VMEM((2, width), jnp.float32),
-            pltpu.SemaphoreType.DMA((4,)),
+            pltpu.SemaphoreType.DMA((5,)),
         ],
-    )(coupling, currents[0], *near(own), sea_mask, wind[:, 0])
+    )(coupling, currents[0], own, sea_mask, wind[:, 0])
     band = band + lax.ppermute(band, "dev", mates)
     band, mate = lax.optimization_barrier((band, mate))
     parts = [crossed(band, step, 0) for step in range(1, groups)]
@@ -305,7 +312,7 @@
         ),
         in_specs=[VMEM] * 7,
         out_specs=(VMEM, VMEM),
-    )(*near(direction_table(width), own, mate, other, band, before, after))
+    )(*near(direction_table(width), own_near, mate, other, band, before, after))
 
     drift_other = lax.ppermute(drift, "dev", others)
     drift_mate = lax.ppermute(drift, "dev", mates)

time: 27.4 us -> 26.8 us (0.978)
  local copies, waits for them, and re-layouts: 1.92 us -> 0.82 us
  starting transfers between devices: 11.7 us -> 12.3 us
  waiting for transfers between devices: 10.4 us -> 9.89 us
  Pallas kernels: 2.51 us -> 2.96 us
    unnamed x7 -> x5, local copies, waits for them, and re-layouts: 1.92 us -> 0.82 us
    ppermute x1, waiting for transfers between devices: 2.46 us -> 3.32 us  [body(): other = lax.ppermute(own, 'dev', others)]
    ppermute x5, waiting for transfers between devices: 4.27 us -> 3.49 us  [crossed(): return lax.ppermute(value, ('grp', 'dev'), pairs)]
    ppermute x1, starting transfers between devices: 1.62 us -> 2.17 us  [body(): drift_other = lax.ppermute(drift, 'dev', others)]
    ppermute x1, waiting for transfers between devices: 2.45 us -> 1.9 us  [body(): drift_other = lax.ppermute(drift, 'dev', others)]
    pallas_call x1, Pallas kernels: 0.75 us -> 1.21 us  [body(): pl.pallas_call(functools.partial(band_kernel, devices), out_shape=(pltpu....]
  transfers between devices with their start and end apart: 10 -> 10, of which waited for: 7 -> 7; matrix products, arithmetic and copies ran while one was open for 3% -> 3% of each run, Pallas kernels for 3% -> 5%
where the time goes in v5:
time: 26.8 us; the launch traced here: 26.6 us
  starting transfers between devices  12.3 us (46%)
  waiting for transfers between devices  9.89 us (37%)
  Pallas kernels  2.96 us (11%)
  local copies, waits for them, and re-layouts  0.82 us (3%)
  between operations  0.66 us (2%)
    ppermute x5, starting transfers between devices, crossed(): return lax.ppermute(value, ('grp', 'dev'), pairs)  4.79 us
    ppermute x1, starting transfers between devices, body(): other = lax.ppermute(own, 'dev', others)  4.71 us
    ppermute x5, waiting for transfers between devices, crossed(): return lax.ppermute(value, ('grp', 'dev'), pairs)  3.49 us
    ppermute x1, waiting for transfers between devices, body(): other = lax.ppermute(own, 'dev', others)  3.32 us
    ppermute x1, starting transfers between devices, body(): drift_other = lax.ppermute(drift, 'dev', others)  2.17 us
    ppermute x1, waiting for transfers between devices, body(): drift_other = lax.ppermute(drift, 'dev', others)  1.9 us
    pallas_call x1, Pallas kernels, body(): pl.pallas_call(functools.partial(band_kernel, devices), out_shape=(pltpu....  1.21 us
    ppermute x1, waiting for transfers between devices, body(): band = band + lax.ppermute(band, 'dev', mates)  1.17 us
  transfers between devices with their start and end apart: 10, of which 7 were waited for; matrix products, arithmetic and copies ran while one was open for 3% of the time, Pallas kernels for 5%

profile of v5, /device:TPU:0, one launch (start us, length us, event | category | flops | bytes accessed | tf_op | source)
XLA Modules:
  0.0 26.6 jit_solution(14699700326715486815)
XLA Ops:
  0.6 0.5 %collective-permute-start.1 = (f32[1152,128]{1,0:T(8,128)}, f32[1152,128]{1,0:T(8,128)S(1)}, u32[]{:S(2)}, u32[]{:S(2)}) collective-permute-start(f32[1152,128]{1,0:T(8,128)} %bitcast.8), channel_id=1, source_target_pairs={{0,1},{1,0},{2,3},{3,2},{4,5},{5,4},{6,7},{7,6},{8,9},{9,8},{10,11... | collective-permute-start | bytes 1769480 | tf_op jit(solution)/shard_map/ppermute | solution.py:279
  1.1 4.7 %collective-permute-start.2 = (f32[1152,128]{1,0:T(8,128)}, f32[1152,128]{1,0:T(8,128)S(1)}, u32[]{:S(2)}, u32[]{:S(2)}) collective-permute-start(f32[1152,128]{1,0:T(8,128)} %bitcast.9), channel_id=1, source_target_pairs={{0,7},{1,2},{2,1},{3,4},{4,3},{5,6},{6,5},{7,0},{8,15},{9,10},{10,... | collective-permute-start | bytes 1769480 | tf_op jit(solution)/shard_map/ppermute | solution.py:280
  5.9 1.2 %shard_map.77 = (f32[32,128]{1,0:T(8,128)S(1)}, f32[1152,128]{1,0:T(8,128)S(1)}) custom-call(s32[1,512]{1,0:T(1,128)} %coupling_ref.1, f32[2,512]{1,0:T(2,128)} %bitcast.11, f32[1152,128]{1,0:T(8,128)} %bitcast.10, s32[1,128]{1,0:T(1,128)} %sea_hbm.1, f32[2,128]{1,0:T(2,128)} %bitcast.13), custom_call_target="tpu_custom_call" | custom-call | tf_op jit(solution)/shard_map/pallas_call | solution.py:283
  7.1 0.1 collective-permute-start
  7.2 1.2 %collective-permute-done = f32[32,128]{1,0:T(8,128)S(1)} collective-permute-done((f32[32,128]{1,0:T(8,128)S(1)}, f32[32,128]{1,0:T(8,128)S(1)}, u32[]{:S(2)}, u32[]{:S(2)}) %collective-permute-start) | collective-permute-done | bytes 16416 | tf_op jit(solution)/shard_map/ppermute | solution.py:299
  8.3 0.0 copy-start
  8.3 0.0 collective-permute-done.1.mate_ref
  8.3 2.2 %collective-permute-start.5 = (f32[32,128]{1,0:T(8,128)S(1)}, f32[32,128]{1,0:T(8,128)S(1)}, u32[]{:S(2)}, u32[]{:S(2)}) collective-permute-start(f32[32,128]{1,0:T(8,128)S(1)} %add.12), channel_id=1, source_target_pairs={{0,25},{1,24},{2,27},{3,26},{4,29},{5,28},{6,31},{7,30},{8,17},{9,... | collective-permute-start | bytes 49160 | tf_op jit(solution)/shard_map/ppermute | solution.py:276
  10.6 0.5 %collective-permute-start.4 = (f32[32,128]{1,0:T(8,128)S(1)}, f32[32,128]{1,0:T(8,128)S(1)}, u32[]{:S(2)}, u32[]{:S(2)}) collective-permute-start(f32[32,128]{1,0:T(8,128)S(1)} %add.12), channel_id=1, source_target_pairs={{0,17},{1,16},{2,19},{3,18},{4,21},{5,20},{6,23},{7,22},{8,25},{9,... | collective-permute-start | bytes 49160 | tf_op jit(solution)/shard_map/ppermute | solution.py:276
  11.0 0.4 %collective-permute-start.3 = (f32[32,128]{1,0:T(8,128)S(1)}, f32[32,128]{1,0:T(8,128)S(1)}, u32[]{:S(2)}, u32[]{:S(2)}) collective-permute-start(f32[32,128]{1,0:T(8,128)S(1)} %add.12), channel_id=1, source_target_pairs={{0,9},{1,8},{2,11},{3,10},{4,13},{5,12},{6,15},{7,14},{8,1},{9,0},... | collective-permute-start | bytes 49160 | tf_op jit(solution)/shard_map/ppermute | solution.py:276
  11.4 1.1 %collective-permute-done.5 = f32[32,128]{1,0:T(8,128)S(1)} collective-permute-done((f32[32,128]{1,0:T(8,128)S(1)}, f32[32,128]{1,0:T(8,128)S(1)}, u32[]{:S(2)}, u32[]{:S(2)}) %collective-permute-start.5) | collective-permute-done | bytes 16416 | tf_op jit(solution)/shard_map/ppermute | solution.py:276
  12.5 1.2 %collective-permute-done.4 = f32[32,128]{1,0:T(8,128)S(1)} collective-permute-done((f32[32,128]{1,0:T(8,128)S(1)}, f32[32,128]{1,0:T(8,128)S(1)}, u32[]{:S(2)}, u32[]{:S(2)}) %collective-permute-start.4) | collective-permute-done | bytes 16416 | tf_op jit(solution)/shard_map/ppermute | solution.py:276
  13.7 0.5 %collective-permute-done.3 = f32[32,128]{1,0:T(8,128)S(1)} collective-permute-done((f32[32,128]{1,0:T(8,128)S(1)}, f32[32,128]{1,0:T(8,128)S(1)}, u32[]{:S(2)}, u32[]{:S(2)}) %collective-permute-start.3) | collective-permute-done | bytes 16416 | tf_op jit(solution)/shard_map/ppermute | solution.py:276
  14.2 0.5 %collective-permute-start.7 = (f32[32,128]{1,0:T(8,128)S(1)}, f32[32,128]{1,0:T(8,128)S(1)}, u32[]{:S(2)}, u32[]{:S(2)}) collective-permute-start(f32[32,128]{1,0:T(8,128)S(1)} %add_add_fusion.band_ref), channel_id=1, source_target_pairs={{0,7},{1,6},{2,1},{3,0},{4,3},{5,2},{6,5},{7,4},{8,15},{9,14},{10,... | collective-permute-start | bytes 49160 | tf_op jit(solution)/shard_map/ppermute | solution.py:276
  14.7 1.2 %collective-permute-start.6 = (f32[32,128]{1,0:T(8,128)S(1)}, f32[32,128]{1,0:T(8,128)S(1)}, u32[]{:S(2)}, u32[]{:S(2)}) collective-permute-start(f32[32,128]{1,0:T(8,128)S(1)} %add_add_fusion.band_ref), channel_id=1, source_target_pairs={{0,3},{1,2},{2,5},{3,4},{4,7},{5,6},{6,1},{7,0},{8,11},{9,10},{10,... | collective-permute-start | bytes 49160 | tf_op jit(solution)/shard_map/ppermute | solution.py:276
  15.9 3.3 %collective-permute-done.2.other_ref = f32[1152,128]{1,0:T(8,128)S(1)} collective-permute-done((f32[1152,128]{1,0:T(8,128)}, f32[1152,128]{1,0:T(8,128)S(1)}, u32[]{:S(2)}, u32[]{:S(2)}) %collective-permute-start.2) | collective-permute-done | bytes 589856 | tf_op jit(solution)/shard_map/ppermute | solution.py:280
  19.3 0.0 collective-permute-done.7.after_ref
  19.3 0.7 %collective-permute-done.6.before_ref = f32[32,128]{1,0:T(8,128)S(1)} collective-permute-done((f32[32,128]{1,0:T(8,128)S(1)}, f32[32,128]{1,0:T(8,128)S(1)}, u32[]{:S(2)}, u32[]{:S(2)}) %collective-permute-start.6) | collective-permute-done | bytes 16416 | tf_op jit(solution)/shard_map/ppermute | solution.py:276
  20.0 0.0 copy-done
  20.0 1.1 %shard_map.78 = (f32[1152,128]{1,0:T(8,128)S(1)}, f32[8,128]{1,0:T(8,128)S(1)}) custom-call(f32[64,128]{1,0:T(8,128)S(1)} %copy-done, f32[1152,128]{1,0:T(8,128)S(1)} %get-tuple-element.8.own_ref, f32[1152,128]{1,0:T(8,128)S(1)} %collective-permute-done.1.mate_ref, f32[1152,128]{1,0:T(8,128)S(1)} %collective-permute-done.2.other_ref, ...), custom_call_target="tpu_custom_call" | custom-call | tf_op jit(solution)/shard_map/pallas_call | solution.py:307
  21.0 2.2 %collective-permute-start.9 = (f32[8,128]{1,0:T(8,128)S(1)}, f32[8,128]{1,0:T(8,128)S(1)}, u32[]{:S(2)}, u32[]{:S(2)}) collective-permute-start(f32[8,128]{1,0:T(8,128)S(1)} %get-tuple-element.13.own_ref), channel_id=1, source_target_pairs={{0,7},{1,2},{2,1},{3,4},{4,3},{5,6},{6,5},{7,0},{8,15},{9,10},{10,... | collective-permute-start | bytes 12296 | tf_op jit(solution)/shard_map/ppermute | solution.py:317
  23.2 0.0 collective-permute-start.8
  23.2 0.0 copy-start.1
  23.2 0.8 %copy.9 = f32[1152,1,128]{2,1,0:T(1,128)} copy(f32[1152,1,128]{2,1,0:T(1,128)S(1)} %bitcast.7) | data formatting | bytes 1179648
  24.0 1.9 %collective-permute-done.9.other_ref = f32[8,128]{1,0:T(8,128)S(1)} collective-permute-done((f32[8,128]{1,0:T(8,128)S(1)}, f32[8,128]{1,0:T(8,128)S(1)}, u32[]{:S(2)}, u32[]{:S(2)}) %collective-permute-start.9) | collective-permute-done | bytes 4128 | tf_op jit(solution)/shard_map/ppermute | solution.py:317
  25.9 0.0 collective-permute-done.8.mate_ref
  25.9 0.0 copy-done.1
  25.9 0.7 %shard_map.79 = f32[2,512]{1,0:T(2,128)} custom-call(s32[1,512]{1,0:T(1,128)S(1)} %copy-done.1, f32[8,128]{1,0:T(8,128)S(1)} %get-tuple-element.13.own_ref, f32[8,128]{1,0:T(8,128)S(1)} %collective-permute-done.8.mate_ref, f32[8,128]{1,0:T(8,128)S(1)} %collective-permute-done.9.other_ref), custom_call_target="tpu_custom_call" | custom-call | tf_op jit(solution)/shard_map/pallas_call | solution.py:319
  (2 shorter events, 0.0 us)
Async XLA Ops:
  0.6 7.7 %collective-permute-start.1 = (f32[1152,128]{1,0:T(8,128)}, f32[1152,128]{1,0:T(8,128)S(1)}, u32[]{:S(2)}, u32[]{:S(2)}) collective-permute-start(f32[1152,128]{1,0:T(8,128)} %bitcast.8), channel_id=1, source_target_pairs={{0,1},{1,0},{2,3},{3,2},{4,5},{5,4},{6,7},{7,6},{8,9},{9,8},{10,11... | collective-permute-start | bytes 1769480 | tf_op jit(solution)/shard_map/ppermute | solution.py:279
  1.1 18.1 %collective-permute-start.2 = (f32[1152,128]{1,0:T(8,128)}, f32[1152,128]{1,0:T(8,128)S(1)}, u32[]{:S(2)}, u32[]{:S(2)}) collective-permute-start(f32[1152,128]{1,0:T(8,128)} %bitcast.9), channel_id=1, source_target_pairs={{0,7},{1,2},{2,1},{3,4},{4,3},{5,6},{6,5},{7,0},{8,15},{9,10},{10,... | collective-permute-start | bytes 1769480 | tf_op jit(solution)/shard_map/ppermute | solution.py:280
  7.1 1.2 %collective-permute-start = (f32[32,128]{1,0:T(8,128)S(1)}, f32[32,128]{1,0:T(8,128)S(1)}, u32[]{:S(2)}, u32[]{:S(2)}) collective-permute-start(f32[32,128]{1,0:T(8,128)S(1)} %get-tuple-element.9), channel_id=1, source_target_pairs={{0,1},{1,0},{2,3},{3,2},{4,5},{5,4},{6,7},{7,6},{8,9},{9,8},{10,11... | collective-permute-start | bytes 49160 | tf_op jit(solution)/shard_map/ppermute | solution.py:299
  8.3 11.6 %copy-start = (f32[64,128]{1,0:T(8,128)S(1)}, f32[64,128]{1,0:T(8,128)}, u32[]{:S(2)}) copy-start(f32[64,128]{1,0:T(8,128)} %constant.2.clone.table_ref) | copy-start | bytes 98308
  8.3 4.1 %collective-permute-start.5 = (f32[32,128]{1,0:T(8,128)S(1)}, f32[32,128]{1,0:T(8,128)S(1)}, u32[]{:S(2)}, u32[]{:S(2)}) collective-permute-start(f32[32,128]{1,0:T(8,128)S(1)} %add.12), channel_id=1, source_target_pairs={{0,25},{1,24},{2,27},{3,26},{4,29},{5,28},{6,31},{7,30},{8,17},{9,... | collective-permute-start | bytes 49160 | tf_op jit(solution)/shard_map/ppermute | solution.py:276
  10.6 3.2 %collective-permute-start.4 = (f32[32,128]{1,0:T(8,128)S(1)}, f32[32,128]{1,0:T(8,128)S(1)}, u32[]{:S(2)}, u32[]{:S(2)}) collective-permute-start(f32[32,128]{1,0:T(8,128)S(1)} %add.12), channel_id=1, source_target_pairs={{0,17},{1,16},{2,19},{3,18},{4,21},{5,20},{6,23},{7,22},{8,25},{9,... | collective-permute-start | bytes 49160 | tf_op jit(solution)/shard_map/ppermute | solution.py:276
  11.0 3.2 %collective-permute-start.3 = (f32[32,128]{1,0:T(8,128)S(1)}, f32[32,128]{1,0:T(8,128)S(1)}, u32[]{:S(2)}, u32[]{:S(2)}) collective-permute-start(f32[32,128]{1,0:T(8,128)S(1)} %add.12), channel_id=1, source_target_pairs={{0,9},{1,8},{2,11},{3,10},{4,13},{5,12},{6,15},{7,14},{8,1},{9,0},... | collective-permute-start | bytes 49160 | tf_op jit(solution)/shard_map/ppermute | solution.py:276
  14.2 5.1 %collective-permute-start.7 = (f32[32,128]{1,0:T(8,128)S(1)}, f32[32,128]{1,0:T(8,128)S(1)}, u32[]{:S(2)}, u32[]{:S(2)}) collective-permute-start(f32[32,128]{1,0:T(8,128)S(1)} %add_add_fusion.band_ref), channel_id=1, source_target_pairs={{0,7},{1,6},{2,1},{3,0},{4,3},{5,2},{6,5},{7,4},{8,15},{9,14},{10,... | collective-permute-start | bytes 49160 | tf_op jit(solution)/shard_map/ppermute | solution.py:276
  14.7 5.3 %collective-permute-start.6 = (f32[32,128]{1,0:T(8,128)S(1)}, f32[32,128]{1,0:T(8,128)S(1)}, u32[]{:S(2)}, u32[]{:S(2)}) collective-permute-start(f32[32,128]{1,0:T(8,128)S(1)} %add_add_fusion.band_ref), channel_id=1, source_target_pairs={{0,3},{1,2},{2,5},{3,4},{4,7},{5,6},{6,1},{7,0},{8,11},{9,10},{10,... | collective-permute-start | bytes 49160 | tf_op jit(solution)/shard_map/ppermute | solution.py:276
  21.0 4.9 %collective-permute-start.9 = (f32[8,128]{1,0:T(8,128)S(1)}, f32[8,128]{1,0:T(8,128)S(1)}, u32[]{:S(2)}, u32[]{:S(2)}) collective-permute-start(f32[8,128]{1,0:T(8,128)S(1)} %get-tuple-element.13.own_ref), channel_id=1, source_target_pairs={{0,7},{1,2},{2,1},{3,4},{4,3},{5,6},{6,5},{7,0},{8,15},{9,10},{10,... | collective-permute-start | bytes 12296 | tf_op jit(solution)/shard_map/ppermute | solution.py:317
  23.2 2.7 %collective-permute-start.8 = (f32[8,128]{1,0:T(8,128)S(1)}, f32[8,128]{1,0:T(8,128)S(1)}, u32[]{:S(2)}, u32[]{:S(2)}) collective-permute-start(f32[8,128]{1,0:T(8,128)S(1)} %get-tuple-element.13.own_ref), channel_id=1, source_target_pairs={{0,1},{1,0},{2,3},{3,2},{4,5},{5,4},{6,7},{7,6},{8,9},{9,8},{10,11... | collective-permute-start | bytes 12296 | tf_op jit(solution)/shard_map/ppermute | solution.py:318
  23.2 2.7 %copy-start.1 = (s32[1,512]{1,0:T(1,128)S(1)}, s32[1,512]{1,0:T(1,128)}, u32[]{:S(2)}) copy-start(s32[1,512]{1,0:T(1,128)} %coupling_ref.1) | copy-start | bytes 6148

commit v6 on v4

--- a/solution.py
+++ b/solution.py
@@ -20,8 +20,8 @@
 STOKES_GAIN = 3.0
 
 SLOTS = 4
-FIELDS = 8
-SUM_X, SUM_Y, COUNT, SEA, WIND_X, WIND_Y, DAMP = range(7)
+FIELDS = 6
+SUM_X, SUM_Y, COUNT, SEA, WIND_X, WIND_Y = range(FIELDS)
 VMEM = pl.BlockSpec(memory_space=pltpu.VMEM)
 
 
@@ -36,7 +36,7 @@
 
 
 def level_groups(levels):
-    for size in (12, 6, 4, 3, 2):
+    for size in (36, 18, 12, 6, 4, 3, 2):
         if levels % size == 0:
             return levels // size, size
     return levels, 1
@@ -52,10 +52,10 @@
 
 
 def band_kernel(
-    columns, coupling_hbm, currents_hbm, spectrum_ref, sea_hbm, wind_hbm, band_ref,
+    columns, coupling_hbm, currents_hbm, sea_hbm, wind_hbm, band_ref,
     coupling_ref, currents_ref, sea_ref, wind_ref, sems,
 ):
-    bins, width = spectrum_ref.shape
+    width = band_ref.shape[1]
     first, odd, group = place()
     is_ocean = group > 0
 
@@ -93,7 +93,7 @@
         step = 2 * SLOTS
         band_ref[0:step, :] = sums[0:step] + sums[step : 2 * step] + sums[2 * step : 3 * step]
         band_ref[step : 2 * step, :] = sums[3 * step : 4 * step]
-        band_ref[2 * step : 4 * step, :] = jnp.zeros((2 * step, width), jnp.float32)
+        band_ref[2 * step : 3 * step, :] = jnp.zeros((step, width), jnp.float32)
 
     @pl.when(jnp.logical_not(is_ocean))
     def _():
@@ -104,36 +104,54 @@
         for copy in copies:
             copy.start()
         band_ref[...] = jnp.zeros_like(band_ref)
-        total = jnp.zeros((8, width), jnp.float32)
-        moment = jnp.zeros((8, width), jnp.float32)
-        for level in range(bins // NDIR):
-            frequency = FIRST_FREQ * GROWTH**level
-            block = spectrum_ref[level * NDIR : (level + 1) * NDIR, :]
-            block = block[0:8] + block[8:16] + (block[16:24] + block[24:32])
-            total += (0.1 * frequency) * block
-            moment += (0.1 * frequency * frequency) * block
         for copy in copies:
             copy.wait()
-        sea = sea_ref[...].astype(jnp.float32)
-        total = jnp.sum(total, axis=0, keepdims=True) * sea
-        moment = jnp.sum(moment, axis=0, keepdims=True) * sea
-        is_sea = sea > 0.5
-        mean_freq = jnp.where(is_sea, moment / jnp.where(is_sea, total, 1.0), 1.0)
-        square = mean_freq * mean_freq
-        steep = STEEP_SCALE * total * (square * square)
-        damp = WHITECAP * (steep * steep) / square
         own = odd + 1
-        band_ref[pl.ds(SEA * SLOTS + own, 1), :] = sea
+        band_ref[pl.ds(SEA * SLOTS + own, 1), :] = sea_ref[...].astype(jnp.float32)
         band_ref[pl.ds(WIND_X * SLOTS + own, 1), :] = wind_ref[0:1, :]
         band_ref[pl.ds(WIND_Y * SLOTS + own, 1), :] = wind_ref[1:2, :]
-        band_ref[pl.ds(DAMP * SLOTS + own, 1), :] = damp
+
+
+def spectrum_sums(ref, sums_ref, first_row):
+    bins, width = ref.shape
+    total = jnp.zeros((8, width), jnp.float32)
+    moment = jnp.zeros((8, width), jnp.float32)
+    for level in range(bins // NDIR):
+        frequency = FIRST_FREQ * GROWTH**level
+        block = ref[level * NDIR : (level + 1) * NDIR, :]
+        block = block[0:8] + block[8:16] + (block[16:24] + block[24:32])
+        total += (0.1 * frequency) * block
+        moment += (0.1 * frequency * frequency) * block
+    sums_ref[first_row : first_row + 1, :] = jnp.sum(total, axis=0, keepdims=True)
+    sums_ref[first_row + 1 : first_row + 2, :] = jnp.sum(moment, axis=0, keepdims=True)
+
+
+def fetch_kernel(own_hbm, _, own_ref, sums_ref, sem):
+    fetch = pltpu.make_async_copy(own_hbm, own_ref, sem)
+    fetch.start()
+    sums_ref[...] = jnp.zeros_like(sums_ref)
+    fetch.wait()
+    spectrum_sums(own_ref, sums_ref, 0)
+
+
+def damping_of(sums_ref, place_row, sea):
+    total = sums_ref[place_row : place_row + 1, :] * sea
+    moment = sums_ref[place_row + 1 : place_row + 2, :] * sea
+    is_sea = sea > 0.5
+    mean_freq = jnp.where(is_sea, moment / jnp.where(is_sea, total, 1.0), 1.0)
+    square = mean_freq * mean_freq
+    steep = STEEP_SCALE * total * (square * square)
+    return WHITECAP * (steep * steep) / square
 
 
 def step_kernel(
-    table_ref, own_ref, mate_ref, other_ref, band_ref, before_ref, after_ref, updated_ref, drift_ref
+    table_ref, own_ref, sums_ref, mate_ref, other_ref, band_ref, before_ref, after_ref, updated_ref, drift_ref,
+    other_sums_ref,
 ):
     bins, width = own_ref.shape
     lanes = 8
+    spectrum_sums(mate_ref, other_sums_ref, 2)
+    spectrum_sums(other_ref, other_sums_ref, 0)
     outer_count, inner_count = level_groups(bins // NDIR)
     _, odd, _ = place()
     slot_own, slot_mate, slot_other = 1 + odd, 2 - odd, 3 * odd
@@ -148,7 +166,7 @@
     cosine = [table_ref[8 * k : 8 * k + 8, :] for k in range(4)]
     sine = [table_ref[NDIR + 8 * k : NDIR + 8 * k + 8, :] for k in range(4)]
 
-    def column_state(slot):
+    def column_state(slot, sums, place_row):
         count = jnp.maximum(field(COUNT, slot), 1.0)
         mean_x = field(SUM_X, slot) / count
         mean_y = field(SUM_Y, slot) / count
@@ -156,13 +174,14 @@
         rel_y = field(WIND_Y, slot) - mean_y
         gain = WIND_GAIN * 0.64
         along = [(gain * rel_x) * cosine[k] + (gain * rel_y) * sine[k] for k in range(4)]
-        sea = jnp.broadcast_to(field(SEA, slot), (lanes, width))
-        damp = jnp.broadcast_to(field(DAMP, slot), (lanes, width))
+        sea = field(SEA, slot)
+        damp = jnp.broadcast_to(damping_of(sums, place_row, sea), (lanes, width))
+        sea = jnp.broadcast_to(sea, (lanes, width))
         return mean_x, mean_y, along, sea, damp
 
-    own_x, own_y, along_own, sea_own, damp_own = column_state(slot_own)
-    mate_x, _, along_mate, sea_mate, damp_mate = column_state(slot_mate)
-    other_x, _, along_other, sea_other, damp_other = column_state(slot_other)
+    own_x, own_y, along_own, sea_own, damp_own = column_state(slot_own, sums_ref, 0)
+    mate_x, _, along_mate, sea_mate, damp_mate = column_state(slot_mate, other_sums_ref, 2)
+    other_x, _, along_other, sea_other, damp_other = column_state(slot_other, other_sums_ref, 0)
     flow_x = CURRENT_TOP * jnp.tanh(own_x)
     flow_y = CURRENT_TOP * jnp.tanh(own_y)
     sign = jnp.where(odd > 0, 1.0, -1.0)
@@ -272,14 +291,14 @@
         return lax.ppermute(value, ("grp", "dev"), pairs)
 
     own = spectrum.reshape(bins, width)
+    other = lax.ppermute(own, "dev", others)
     mate = lax.ppermute(own, "dev", mates)
-    other = lax.ppermute(own, "dev", others)
 
     anywhere = pl.BlockSpec(memory_space=pl.ANY)
     band = pl.pallas_call(
         functools.partial(band_kernel, devices),
         out_shape=pltpu.VMEM((FIELDS * SLOTS, width), jnp.float32),
-        in_specs=[anywhere, anywhere, VMEM, anywhere, anywhere],
+        in_specs=[anywhere] * 4,
         out_specs=VMEM,
         scratch_shapes=[
             pltpu.VMEM((1, cells), jnp.int32),
@@ -288,24 +307,34 @@
             pltpu.VMEM((2, width), jnp.float32),
             pltpu.SemaphoreType.DMA((4,)),
         ],
-    )(coupling, currents[0], *near(own), sea_mask, wind[:, 0])
+    )(coupling, currents[0], sea_mask, wind[:, 0])
     band = band + lax.ppermute(band, "dev", mates)
-    band, mate = lax.optimization_barrier((band, mate))
     parts = [crossed(band, step, 0) for step in range(1, groups)]
     for part in parts:
         band = band + part
     before = crossed(band, 0, 1)
     after = crossed(band, 0, -1)
 
+    own_near, sums = pl.pallas_call(
+        fetch_kernel,
+        out_shape=(
+            pltpu.VMEM((bins, width), jnp.float32),
+            pltpu.VMEM((8, width), jnp.float32),
+        ),
+        in_specs=[anywhere, VMEM],
+        out_specs=(VMEM, VMEM),
+        scratch_shapes=[pltpu.SemaphoreType.DMA],
+    )(own, *near(band))
     updated, drift = pl.pallas_call(
         step_kernel,
         out_shape=(
             pltpu.VMEM((bins, width), jnp.float32),
             pltpu.VMEM((8, width), jnp.float32),
         ),
-        in_specs=[VMEM] * 7,
+        in_specs=[VMEM] * 8,
         out_specs=(VMEM, VMEM),
-    )(*near(direction_table(width), own, mate, other, band, before, after))
+        scratch_shapes=[pltpu.VMEM((8, width), jnp.float32)],
+    )(*near(direction_table(width), own_near, sums, mate, other, band, before, after))
 
     drift_other = lax.ppermute(drift, "dev", others)
     drift_mate = lax.ppermute(drift, "dev", mates)

time: 27.4 us -> 26.2 us (0.956)
  waiting for transfers between devices: 10.4 us -> 8.49 us
  Pallas kernels: 2.51 us -> 3.61 us
  local copies, waits for them, and re-layouts: 1.92 us -> 0.82 us
  starting transfers between devices: 11.7 us -> 12.4 us
    ppermute x1, waiting for transfers between devices: 2.46 us -> 0.01 us  [body(): other = lax.ppermute(own, 'dev', others)]
    ppermute x5, waiting for transfers between devices: 4.27 us -> 5.92 us  [crossed(): return lax.ppermute(value, ('grp', 'dev'), pairs)]
    pallas_call x0 -> x1, Pallas kernels: none -> 1.13 us  [body(): pl.pallas_call(fetch_kernel, out_shape=(pltpu.VMEM((bins, width), jnp.flo...]
    unnamed x7 -> x5, local copies, waits for them, and re-layouts: 1.92 us -> 0.82 us
    ppermute x1, waiting for transfers between devices: 2.45 us -> 1.73 us  [body(): drift_other = lax.ppermute(drift, 'dev', others)]
    ppermute x1, starting transfers between devices: 1.62 us -> 2.34 us  [body(): drift_other = lax.ppermute(drift, 'dev', others)]
    ppermute x1, starting transfers between devices: 0.52 us -> 0.01 us  [body(): mate = lax.ppermute(own, 'dev', mates)]
    ppermute x1, starting transfers between devices: 0.07 us -> 0.57 us  [body(): band = band + lax.ppermute(band, 'dev', mates)]
  transfers between devices with their start and end apart: 10 -> 10, of which waited for: 7 -> 7; matrix products, arithmetic and copies ran while one was open for 3% -> 3% of each run, Pallas kernels for 3% -> 7%
where the time goes in v6:
time: 26.2 us; the launch traced here: 26 us
  starting transfers between devices  12.4 us (47%)
  waiting for transfers between devices  8.49 us (32%)
  Pallas kernels  3.61 us (14%)
  local copies, waits for them, and re-layouts  0.82 us (3%)
  between operations  0.66 us (3%)
    ppermute x5, waiting for transfers between devices, crossed(): return lax.ppermute(value, ('grp', 'dev'), pairs)  5.92 us
    ppermute x5, starting transfers between devices, crossed(): return lax.ppermute(value, ('grp', 'dev'), pairs)  4.95 us
    ppermute x1, starting transfers between devices, body(): other = lax.ppermute(own, 'dev', others)  4.55 us
    ppermute x1, starting transfers between devices, body(): drift_other = lax.ppermute(drift, 'dev', others)  2.34 us
    ppermute x1, waiting for transfers between devices, body(): drift_other = lax.ppermute(drift, 'dev', others)  1.73 us
    pallas_call x1, Pallas kernels, body(): pl.pallas_call(fetch_kernel, out_shape=(pltpu.VMEM((bins, width), jnp.flo...  1.13 us
    pallas_call x1, Pallas kernels, body(): pl.pallas_call(step_kernel, out_shape=(pltpu.VMEM((bins, width), jnp.floa...  1.05 us
    ppermute x1, waiting for transfers between devices, body(): band = band + lax.ppermute(band, 'dev', mates)  0.83 us
  transfers between devices with their start and end apart: 10, of which 7 were waited for; matrix products, arithmetic and copies ran while one was open for 3% of the time, Pallas kernels for 7%

profile of v6, /device:TPU:0, one launch (start us, length us, event | category | flops | bytes accessed | tf_op | source)
XLA Modules:
  0.0 26.0 jit_solution(14888520008975947921)
XLA Ops:
  0.6 4.6 %collective-permute-start.5 = (f32[1152,128]{1,0:T(8,128)}, f32[1152,128]{1,0:T(8,128)S(1)}, u32[]{:S(2)}, u32[]{:S(2)}) collective-permute-start(f32[1152,128]{1,0:T(8,128)} %bitcast.8), channel_id=1, source_target_pairs={{0,7},{1,2},{2,1},{3,4},{4,3},{5,6},{6,5},{7,0},{8,15},{9,10},{10,... | collective-permute-start | bytes 1769480 | tf_op jit(solution)/shard_map/ppermute | solution.py:294
  5.2 0.0 collective-permute-start.4
  5.2 0.7 %shard_map.77 = f32[24,128]{1,0:T(8,128)S(1)} custom-call(s32[1,512]{1,0:T(1,128)} %coupling_ref.1, f32[2,512]{1,0:T(2,128)} %bitcast.11, s32[1,128]{1,0:T(1,128)} %sea_hbm.1, f32[2,128]{1,0:T(2,128)} %bitcast.13), custom_call_target="tpu_custom_call" | custom-call | tf_op jit(solution)/shard_map/pallas_call | solution.py:298
  5.9 0.6 %collective-permute-start = (f32[24,128]{1,0:T(8,128)S(1)}, f32[24,128]{1,0:T(8,128)S(1)}, u32[]{:S(2)}, u32[]{:S(2)}) collective-permute-start(f32[24,128]{1,0:T(8,128)S(1)} %shard_map.77), channel_id=1, source_target_pairs={{0,1},{1,0},{2,3},{3,2},{4,5},{5,4},{6,7},{7,6},{8,9},{9,8},{10,11... | collective-permute-start | bytes 36872 | tf_op jit(solution)/shard_map/ppermute | solution.py:311
  6.5 0.8 %collective-permute-done = f32[24,128]{1,0:T(8,128)S(1)} collective-permute-done((f32[24,128]{1,0:T(8,128)S(1)}, f32[24,128]{1,0:T(8,128)S(1)}, u32[]{:S(2)}, u32[]{:S(2)}) %collective-permute-start) | collective-permute-done | bytes 12320 | tf_op jit(solution)/shard_map/ppermute | solution.py:311
  7.3 2.6 %collective-permute-start.3 = (f32[24,128]{1,0:T(8,128)S(1)}, f32[24,128]{1,0:T(8,128)S(1)}, u32[]{:S(2)}, u32[]{:S(2)}) collective-permute-start(f32[24,128]{1,0:T(8,128)S(1)} %add.12), channel_id=1, source_target_pairs={{0,25},{1,24},{2,27},{3,26},{4,29},{5,28},{6,31},{7,30},{8,17},{9,... | collective-permute-start | bytes 36872 | tf_op jit(solution)/shard_map/ppermute | solution.py:291
  9.9 0.3 %collective-permute-start.2 = (f32[24,128]{1,0:T(8,128)S(1)}, f32[24,128]{1,0:T(8,128)S(1)}, u32[]{:S(2)}, u32[]{:S(2)}) collective-permute-start(f32[24,128]{1,0:T(8,128)S(1)} %add.12), channel_id=1, source_target_pairs={{0,17},{1,16},{2,19},{3,18},{4,21},{5,20},{6,23},{7,22},{8,25},{9,... | collective-permute-start | bytes 36872 | tf_op jit(solution)/shard_map/ppermute | solution.py:291
  10.2 0.3 %collective-permute-start.1 = (f32[24,128]{1,0:T(8,128)S(1)}, f32[24,128]{1,0:T(8,128)S(1)}, u32[]{:S(2)}, u32[]{:S(2)}) collective-permute-start(f32[24,128]{1,0:T(8,128)S(1)} %add.12), channel_id=1, source_target_pairs={{0,9},{1,8},{2,11},{3,10},{4,13},{5,12},{6,15},{7,14},{8,1},{9,0},... | collective-permute-start | bytes 36872 | tf_op jit(solution)/shard_map/ppermute | solution.py:291
  10.5 0.9 %collective-permute-done.3 = f32[24,128]{1,0:T(8,128)S(1)} collective-permute-done((f32[24,128]{1,0:T(8,128)S(1)}, f32[24,128]{1,0:T(8,128)S(1)}, u32[]{:S(2)}, u32[]{:S(2)}) %collective-permute-start.3) | collective-permute-done | bytes 12320 | tf_op jit(solution)/shard_map/ppermute | solution.py:291
  11.4 1.7 %collective-permute-done.2 = f32[24,128]{1,0:T(8,128)S(1)} collective-permute-done((f32[24,128]{1,0:T(8,128)S(1)}, f32[24,128]{1,0:T(8,128)S(1)}, u32[]{:S(2)}, u32[]{:S(2)}) %collective-permute-start.2) | collective-permute-done | bytes 12320 | tf_op jit(solution)/shard_map/ppermute | solution.py:291
  13.0 0.3 %collective-permute-done.1 = f32[24,128]{1,0:T(8,128)S(1)} collective-permute-done((f32[24,128]{1,0:T(8,128)S(1)}, f32[24,128]{1,0:T(8,128)S(1)}, u32[]{:S(2)}, u32[]{:S(2)}) %collective-permute-start.1) | collective-permute-done | bytes 12320 | tf_op jit(solution)/shard_map/ppermute | solution.py:291
  13.3 0.0 copy-start
  13.3 0.9 %collective-permute-start.7 = (f32[24,128]{1,0:T(8,128)S(1)}, f32[24,128]{1,0:T(8,128)S(1)}, u32[]{:S(2)}, u32[]{:S(2)}) collective-permute-start(f32[24,128]{1,0:T(8,128)S(1)} %add_add_fusion._.band_ref), channel_id=1, source_target_pairs={{0,7},{1,6},{2,1},{3,0},{4,3},{5,2},{6,5},{7,4},{8,15},{9,14},{10,... | collective-permute-start | bytes 36872 | tf_op jit(solution)/shard_map/ppermute | solution.py:291
  14.2 0.9 %collective-permute-start.6 = (f32[24,128]{1,0:T(8,128)S(1)}, f32[24,128]{1,0:T(8,128)S(1)}, u32[]{:S(2)}, u32[]{:S(2)}) collective-permute-start(f32[24,128]{1,0:T(8,128)S(1)} %add_add_fusion._.band_ref), channel_id=1, source_target_pairs={{0,3},{1,2},{2,5},{3,4},{4,7},{5,6},{6,1},{7,0},{8,11},{9,10},{10,... | collective-permute-start | bytes 36872 | tf_op jit(solution)/shard_map/ppermute | solution.py:291
  15.1 1.1 %shard_map.78 = (f32[1152,128]{1,0:T(8,128)S(1)}, f32[8,128]{1,0:T(8,128)S(1)}) custom-call(f32[1152,128]{1,0:T(8,128)} %bitcast.10, f32[24,128]{1,0:T(8,128)S(1)} %add_add_fusion._.band_ref), custom_call_target="tpu_custom_call" | custom-call | tf_op jit(solution)/shard_map/pallas_call | solution.py:318
  16.2 1.3 %collective-permute-done.7.after_ref = f32[24,128]{1,0:T(8,128)S(1)} collective-permute-done((f32[24,128]{1,0:T(8,128)S(1)}, f32[24,128]{1,0:T(8,128)S(1)}, u32[]{:S(2)}, u32[]{:S(2)}) %collective-permute-start.7) | collective-permute-done | bytes 12320 | tf_op jit(solution)/shard_map/ppermute | solution.py:291
  17.5 1.8 %collective-permute-done.6.before_ref = f32[24,128]{1,0:T(8,128)S(1)} collective-permute-done((f32[24,128]{1,0:T(8,128)S(1)}, f32[24,128]{1,0:T(8,128)S(1)}, u32[]{:S(2)}, u32[]{:S(2)}) %collective-permute-start.6) | collective-permute-done | bytes 12320 | tf_op jit(solution)/shard_map/ppermute | solution.py:291
  19.4 0.0 collective-permute-done.5.other_ref
  19.4 0.0 collective-permute-done.4.mate_ref
  19.4 0.0 copy-done
  19.4 1.0 %shard_map.79 = (f32[1152,128]{1,0:T(8,128)S(1)}, f32[8,128]{1,0:T(8,128)S(1)}) custom-call(f32[64,128]{1,0:T(8,128)S(1)} %copy-done, f32[1152,128]{1,0:T(8,128)S(1)} %get-tuple-element.6.own_ref, f32[8,128]{1,0:T(8,128)S(1)} %get-tuple-element.7.sums_ref, f32[1152,128]{1,0:T(8,128)S(1)} %collective-permute-done.4.mate_ref, ...), custom_call_target="tpu_custom_call" | custom-call | tf_op jit(solution)/shard_map/pallas_call | solution.py:328
  20.4 2.3 %collective-permute-start.9 = (f32[8,128]{1,0:T(8,128)S(1)}, f32[8,128]{1,0:T(8,128)S(1)}, u32[]{:S(2)}, u32[]{:S(2)}) collective-permute-start(f32[8,128]{1,0:T(8,128)S(1)} %get-tuple-element.9.own_ref), channel_id=1, source_target_pairs={{0,7},{1,2},{2,1},{3,4},{4,3},{5,6},{6,5},{7,0},{8,15},{9,10},{10,... | collective-permute-start | bytes 12296 | tf_op jit(solution)/shard_map/ppermute | solution.py:339
  22.8 0.0 collective-permute-start.8
  22.8 0.0 copy-start.1
  22.8 0.8 %copy.9 = f32[1152,1,128]{2,1,0:T(1,128)} copy(f32[1152,1,128]{2,1,0:T(1,128)S(1)} %bitcast.7) | data formatting | bytes 1179648
  23.6 1.7 %collective-permute-done.9.other_ref = f32[8,128]{1,0:T(8,128)S(1)} collective-permute-done((f32[8,128]{1,0:T(8,128)S(1)}, f32[8,128]{1,0:T(8,128)S(1)}, u32[]{:S(2)}, u32[]{:S(2)}) %collective-permute-start.9) | collective-permute-done | bytes 4128 | tf_op jit(solution)/shard_map/ppermute | solution.py:339
  25.3 0.0 collective-permute-done.8.mate_ref
  25.3 0.0 copy-done.1
  25.3 0.7 %shard_map.80 = f32[2,512]{1,0:T(2,128)} custom-call(s32[1,512]{1,0:T(1,128)S(1)} %copy-done.1, f32[8,128]{1,0:T(8,128)S(1)} %get-tuple-element.9.own_ref, f32[8,128]{1,0:T(8,128)S(1)} %collective-permute-done.8.mate_ref, f32[8,128]{1,0:T(8,128)S(1)} %collective-permute-done.9.other_ref), custom_call_target="tpu_custom_call" | custom-call | tf_op jit(solution)/shard_map/pallas_call | solution.py:341
  (2 shorter events, 0.0 us)
Async XLA Ops:
  0.6 18.7 %collective-permute-start.5 = (f32[1152,128]{1,0:T(8,128)}, f32[1152,128]{1,0:T(8,128)S(1)}, u32[]{:S(2)}, u32[]{:S(2)}) collective-permute-start(f32[1152,128]{1,0:T(8,128)} %bitcast.8), channel_id=1, source_target_pairs={{0,7},{1,2},{2,1},{3,4},{4,3},{5,6},{6,5},{7,0},{8,15},{9,10},{10,... | collective-permute-start | bytes 1769480 | tf_op jit(solution)/shard_map/ppermute | solution.py:294
  5.2 14.2 %collective-permute-start.4 = (f32[1152,128]{1,0:T(8,128)}, f32[1152,128]{1,0:T(8,128)S(1)}, u32[]{:S(2)}, u32[]{:S(2)}) collective-permute-start(f32[1152,128]{1,0:T(8,128)} %bitcast.9), channel_id=1, source_target_pairs={{0,1},{1,0},{2,3},{3,2},{4,5},{5,4},{6,7},{7,6},{8,9},{9,8},{10,11... | collective-permute-start | bytes 1769480 | tf_op jit(solution)/shard_map/ppermute | solution.py:295
  5.9 1.4 %collective-permute-start = (f32[24,128]{1,0:T(8,128)S(1)}, f32[24,128]{1,0:T(8,128)S(1)}, u32[]{:S(2)}, u32[]{:S(2)}) collective-permute-start(f32[24,128]{1,0:T(8,128)S(1)} %shard_map.77), channel_id=1, source_target_pairs={{0,1},{1,0},{2,3},{3,2},{4,5},{5,4},{6,7},{7,6},{8,9},{9,8},{10,11... | collective-permute-start | bytes 36872 | tf_op jit(solution)/shard_map/ppermute | solution.py:311
  7.3 4.0 %collective-permute-start.3 = (f32[24,128]{1,0:T(8,128)S(1)}, f32[24,128]{1,0:T(8,128)S(1)}, u32[]{:S(2)}, u32[]{:S(2)}) collective-permute-start(f32[24,128]{1,0:T(8,128)S(1)} %add.12), channel_id=1, source_target_pairs={{0,25},{1,24},{2,27},{3,26},{4,29},{5,28},{6,31},{7,30},{8,17},{9,... | collective-permute-start | bytes 36872 | tf_op jit(solution)/shard_map/ppermute | solution.py:291
  9.9 3.1 %collective-permute-start.2 = (f32[24,128]{1,0:T(8,128)S(1)}, f32[24,128]{1,0:T(8,128)S(1)}, u32[]{:S(2)}, u32[]{:S(2)}) collective-permute-start(f32[24,128]{1,0:T(8,128)S(1)} %add.12), channel_id=1, source_target_pairs={{0,17},{1,16},{2,19},{3,18},{4,21},{5,20},{6,23},{7,22},{8,25},{9,... | collective-permute-start | bytes 36872 | tf_op jit(solution)/shard_map/ppermute | solution.py:291
  10.2 3.1 %collective-permute-start.1 = (f32[24,128]{1,0:T(8,128)S(1)}, f32[24,128]{1,0:T(8,128)S(1)}, u32[]{:S(2)}, u32[]{:S(2)}) collective-permute-start(f32[24,128]{1,0:T(8,128)S(1)} %add.12), channel_id=1, source_target_pairs={{0,9},{1,8},{2,11},{3,10},{4,13},{5,12},{6,15},{7,14},{8,1},{9,0},... | collective-permute-start | bytes 36872 | tf_op jit(solution)/shard_map/ppermute | solution.py:291
  13.3 6.1 %copy-start = (f32[64,128]{1,0:T(8,128)S(1)}, f32[64,128]{1,0:T(8,128)}, u32[]{:S(2)}) copy-start(f32[64,128]{1,0:T(8,128)} %constant.2.clone.table_ref) | copy-start | bytes 98308
  13.3 4.2 %collective-permute-start.7 = (f32[24,128]{1,0:T(8,128)S(1)}, f32[24,128]{1,0:T(8,128)S(1)}, u32[]{:S(2)}, u32[]{:S(2)}) collective-permute-start(f32[24,128]{1,0:T(8,128)S(1)} %add_add_fusion._.band_ref), channel_id=1, source_target_pairs={{0,7},{1,6},{2,1},{3,0},{4,3},{5,2},{6,5},{7,4},{8,15},{9,14},{10,... | collective-permute-start | bytes 36872 | tf_op jit(solution)/shard_map/ppermute | solution.py:291
  14.2 5.1 %collective-permute-start.6 = (f32[24,128]{1,0:T(8,128)S(1)}, f32[24,128]{1,0:T(8,128)S(1)}, u32[]{:S(2)}, u32[]{:S(2)}) collective-permute-start(f32[24,128]{1,0:T(8,128)S(1)} %add_add_fusion._.band_ref), channel_id=1, source_target_pairs={{0,3},{1,2},{2,5},{3,4},{4,7},{5,6},{6,1},{7,0},{8,11},{9,10},{10,... | collective-permute-start | bytes 36872 | tf_op jit(solution)/shard_map/ppermute | solution.py:291
  20.4 4.9 %collective-permute-start.9 = (f32[8,128]{1,0:T(8,128)S(1)}, f32[8,128]{1,0:T(8,128)S(1)}, u32[]{:S(2)}, u32[]{:S(2)}) collective-permute-start(f32[8,128]{1,0:T(8,128)S(1)} %get-tuple-element.9.own_ref), channel_id=1, source_target_pairs={{0,7},{1,2},{2,1},{3,4},{4,3},{5,6},{6,5},{7,0},{8,15},{9,10},{10,... | collective-permute-start | bytes 12296 | tf_op jit(solution)/shard_map/ppermute | solution.py:339
  22.8 2.6 %collective-permute-start.8 = (f32[8,128]{1,0:T(8,128)S(1)}, f32[8,128]{1,0:T(8,128)S(1)}, u32[]{:S(2)}, u32[]{:S(2)}) collective-permute-start(f32[8,128]{1,0:T(8,128)S(1)} %get-tuple-element.9.own_ref), channel_id=1, source_target_pairs={{0,1},{1,0},{2,3},{3,2},{4,5},{5,4},{6,7},{7,6},{8,9},{9,8},{10,11... | collective-permute-start | bytes 12296 | tf_op jit(solution)/shard_map/ppermute | solution.py:340
  22.8 2.6 %copy-start.1 = (s32[1,512]{1,0:T(1,128)S(1)}, s32[1,512]{1,0:T(1,128)}, u32[]{:S(2)}) copy-start(s32[1,512]{1,0:T(1,128)} %coupling_ref.1) | copy-start | bytes 6148

commit v7 on v6

--- a/solution.py
+++ b/solution.py
@@ -145,7 +145,7 @@
 
 
 def step_kernel(
-    table_ref, own_ref, sums_ref, mate_ref, other_ref, band_ref, before_ref, after_ref, updated_ref, drift_ref,
+    table_ref, own_ref, sums_ref, mate_ref, other_ref, band_ref, after_ref, before_ref, updated_ref, drift_ref,
     other_sums_ref,
 ):
     bins, width = own_ref.shape
@@ -312,8 +312,8 @@
     parts = [crossed(band, step, 0) for step in range(1, groups)]
     for part in parts:
         band = band + part
+    after = crossed(band, 0, -1)
     before = crossed(band, 0, 1)
-    after = crossed(band, 0, -1)
 
     own_near, sums = pl.pallas_call(
         fetch_kernel,
@@ -334,7 +334,7 @@
         in_specs=[VMEM] * 8,
         out_specs=(VMEM, VMEM),
         scratch_shapes=[pltpu.VMEM((8, width), jnp.float32)],
-    )(*near(direction_table(width), own_near, sums, mate, other, band, before, after))
+    )(*near(direction_table(width), own_near, sums, mate, other, band, after, before))
 
     drift_other = lax.ppermute(drift, "dev", others)
     drift_mate = lax.ppermute(drift, "dev", mates)

time: 26.2 us -> 25.6 us (0.977)
  waiting for transfers between devices: 8.49 us -> 4.92 us
  starting transfers between devices: 12.4 us -> 15.4 us
    ppermute x5, waiting for transfers between devices: 5.92 us -> 3.48 us  [crossed(): return lax.ppermute(value, ('grp', 'dev'), pairs)]
    ppermute x5, starting transfers between devices: 4.95 us -> 6.75 us  [crossed(): return lax.ppermute(value, ('grp', 'dev'), pairs)]
    ppermute x1, waiting for transfers between devices: 1.73 us -> 0.59 us  [body(): drift_other = lax.ppermute(drift, 'dev', others)]
    ppermute x1, starting transfers between devices: 2.34 us -> 3.48 us  [body(): drift_other = lax.ppermute(drift, 'dev', others)]
  transfers between devices with their start and end apart: 10 -> 10, of which waited for: 7 -> 6; matrix products, arithmetic and copies ran while one was open for 3% -> 3% of each run, Pallas kernels for 7% -> 7%
where the time goes in v7:
time: 25.6 us; the launch traced here: 25.4 us
  starting transfers between devices  15.4 us (60%)
  waiting for transfers between devices  4.92 us (19%)
  Pallas kernels  3.61 us (14%)
  local copies, waits for them, and re-layouts  0.82 us (3%)
  between operations  0.67 us (3%)
    ppermute x5, starting transfers between devices, crossed(): return lax.ppermute(value, ('grp', 'dev'), pairs)  6.75 us
    ppermute x1, starting transfers between devices, body(): other = lax.ppermute(own, 'dev', others)  4.55 us
    ppermute x5, waiting for transfers between devices, crossed(): return lax.ppermute(value, ('grp', 'dev'), pairs)  3.48 us
    ppermute x1, starting transfers between devices, body(): drift_other = lax.ppermute(drift, 'dev', others)  3.48 us
    pallas_call x1, Pallas kernels, body(): pl.pallas_call(fetch_kernel, out_shape=(pltpu.VMEM((bins, width), jnp.flo...  1.13 us
    pallas_call x1, Pallas kernels, body(): pl.pallas_call(step_kernel, out_shape=(pltpu.VMEM((bins, width), jnp.floa...  1.05 us
    ppermute x1, waiting for transfers between devices, body(): band = band + lax.ppermute(band, 'dev', mates)  0.83 us
    unnamed x5, local copies, waits for them, and re-layouts  0.82 us
  transfers between devices with their start and end apart: 10, of which 6 were waited for; matrix products, arithmetic and copies ran while one was open for 3% of the time, Pallas kernels for 7%

profile of v7, /device:TPU:0, one launch (start us, length us, event | category | flops | bytes accessed | tf_op | source)
XLA Modules:
  0.0 25.4 jit_solution(11362161716143117300)
XLA Ops:
  0.6 4.6 %collective-permute-start.5 = (f32[1152,128]{1,0:T(8,128)}, f32[1152,128]{1,0:T(8,128)S(1)}, u32[]{:S(2)}, u32[]{:S(2)}) collective-permute-start(f32[1152,128]{1,0:T(8,128)} %bitcast.8), channel_id=1, source_target_pairs={{0,7},{1,2},{2,1},{3,4},{4,3},{5,6},{6,5},{7,0},{8,15},{9,10},{10,... | collective-permute-start | bytes 1769480 | tf_op jit(solution)/shard_map/ppermute | solution.py:294
  5.2 0.0 collective-permute-start.4
  5.2 0.7 %shard_map.77 = f32[24,128]{1,0:T(8,128)S(1)} custom-call(s32[1,512]{1,0:T(1,128)} %coupling_ref.1, f32[2,512]{1,0:T(2,128)} %bitcast.11, s32[1,128]{1,0:T(1,128)} %sea_hbm.1, f32[2,128]{1,0:T(2,128)} %bitcast.13), custom_call_target="tpu_custom_call" | custom-call | tf_op jit(solution)/shard_map/pallas_call | solution.py:298
  5.9 0.6 %collective-permute-start = (f32[24,128]{1,0:T(8,128)S(1)}, f32[24,128]{1,0:T(8,128)S(1)}, u32[]{:S(2)}, u32[]{:S(2)}) collective-permute-start(f32[24,128]{1,0:T(8,128)S(1)} %shard_map.77), channel_id=1, source_target_pairs={{0,1},{1,0},{2,3},{3,2},{4,5},{5,4},{6,7},{7,6},{8,9},{9,8},{10,11... | collective-permute-start | bytes 36872 | tf_op jit(solution)/shard_map/ppermute | solution.py:311
  6.5 0.8 %collective-permute-done = f32[24,128]{1,0:T(8,128)S(1)} collective-permute-done((f32[24,128]{1,0:T(8,128)S(1)}, f32[24,128]{1,0:T(8,128)S(1)}, u32[]{:S(2)}, u32[]{:S(2)}) %collective-permute-start) | collective-permute-done | bytes 12320 | tf_op jit(solution)/shard_map/ppermute | solution.py:311
  7.3 2.6 %collective-permute-start.3 = (f32[24,128]{1,0:T(8,128)S(1)}, f32[24,128]{1,0:T(8,128)S(1)}, u32[]{:S(2)}, u32[]{:S(2)}) collective-permute-start(f32[24,128]{1,0:T(8,128)S(1)} %add.12), channel_id=1, source_target_pairs={{0,25},{1,24},{2,27},{3,26},{4,29},{5,28},{6,31},{7,30},{8,17},{9,... | collective-permute-start | bytes 36872 | tf_op jit(solution)/shard_map/ppermute | solution.py:291
  9.9 0.3 %collective-permute-start.2 = (f32[24,128]{1,0:T(8,128)S(1)}, f32[24,128]{1,0:T(8,128)S(1)}, u32[]{:S(2)}, u32[]{:S(2)}) collective-permute-start(f32[24,128]{1,0:T(8,128)S(1)} %add.12), channel_id=1, source_target_pairs={{0,17},{1,16},{2,19},{3,18},{4,21},{5,20},{6,23},{7,22},{8,25},{9,... | collective-permute-start | bytes 36872 | tf_op jit(solution)/shard_map/ppermute | solution.py:291
  10.2 0.3 %collective-permute-start.1 = (f32[24,128]{1,0:T(8,128)S(1)}, f32[24,128]{1,0:T(8,128)S(1)}, u32[]{:S(2)}, u32[]{:S(2)}) collective-permute-start(f32[24,128]{1,0:T(8,128)S(1)} %add.12), channel_id=1, source_target_pairs={{0,9},{1,8},{2,11},{3,10},{4,13},{5,12},{6,15},{7,14},{8,1},{9,0},... | collective-permute-start | bytes 36872 | tf_op jit(solution)/shard_map/ppermute | solution.py:291
  10.5 0.9 %collective-permute-done.3 = f32[24,128]{1,0:T(8,128)S(1)} collective-permute-done((f32[24,128]{1,0:T(8,128)S(1)}, f32[24,128]{1,0:T(8,128)S(1)}, u32[]{:S(2)}, u32[]{:S(2)}) %collective-permute-start.3) | collective-permute-done | bytes 12320 | tf_op jit(solution)/shard_map/ppermute | solution.py:291
  11.4 1.7 %collective-permute-done.2 = f32[24,128]{1,0:T(8,128)S(1)} collective-permute-done((f32[24,128]{1,0:T(8,128)S(1)}, f32[24,128]{1,0:T(8,128)S(1)}, u32[]{:S(2)}, u32[]{:S(2)}) %collective-permute-start.2) | collective-permute-done | bytes 12320 | tf_op jit(solution)/shard_map/ppermute | solution.py:291
  13.0 0.3 %collective-permute-done.1 = f32[24,128]{1,0:T(8,128)S(1)} collective-permute-done((f32[24,128]{1,0:T(8,128)S(1)}, f32[24,128]{1,0:T(8,128)S(1)}, u32[]{:S(2)}, u32[]{:S(2)}) %collective-permute-start.1) | collective-permute-done | bytes 12320 | tf_op jit(solution)/shard_map/ppermute | solution.py:291
  13.3 0.0 copy-start
  13.3 0.2 collective-permute-start.7
  13.5 3.4 %collective-permute-start.6 = (f32[24,128]{1,0:T(8,128)S(1)}, f32[24,128]{1,0:T(8,128)S(1)}, u32[]{:S(2)}, u32[]{:S(2)}) collective-permute-start(f32[24,128]{1,0:T(8,128)S(1)} %add_add_fusion._.band_ref), channel_id=1, source_target_pairs={{0,7},{1,6},{2,1},{3,0},{4,3},{5,2},{6,5},{7,4},{8,15},{9,14},{10,... | collective-permute-start | bytes 36872 | tf_op jit(solution)/shard_map/ppermute | solution.py:291
  16.9 1.1 %shard_map.78 = (f32[1152,128]{1,0:T(8,128)S(1)}, f32[8,128]{1,0:T(8,128)S(1)}) custom-call(f32[1152,128]{1,0:T(8,128)} %bitcast.10, f32[24,128]{1,0:T(8,128)S(1)} %add_add_fusion._.band_ref), custom_call_target="tpu_custom_call" | custom-call | tf_op jit(solution)/shard_map/pallas_call | solution.py:318
  18.0 0.7 %collective-permute-done.7.before_ref = f32[24,128]{1,0:T(8,128)S(1)} collective-permute-done((f32[24,128]{1,0:T(8,128)S(1)}, f32[24,128]{1,0:T(8,128)S(1)}, u32[]{:S(2)}, u32[]{:S(2)}) %collective-permute-start.7) | collective-permute-done | bytes 12320 | tf_op jit(solution)/shard_map/ppermute | solution.py:291
  18.7 0.0 collective-permute-done.6.after_ref
  18.7 0.0 collective-permute-done.5.other_ref
  18.7 0.0 collective-permute-done.4.mate_ref
  18.7 0.0 copy-done
  18.7 1.0 %shard_map.79 = (f32[1152,128]{1,0:T(8,128)S(1)}, f32[8,128]{1,0:T(8,128)S(1)}) custom-call(f32[64,128]{1,0:T(8,128)S(1)} %copy-done, f32[1152,128]{1,0:T(8,128)S(1)} %get-tuple-element.6.own_ref, f32[8,128]{1,0:T(8,128)S(1)} %get-tuple-element.7.sums_ref, f32[1152,128]{1,0:T(8,128)S(1)} %collective-permute-done.4.mate_ref, ...), custom_call_target="tpu_custom_call" | custom-call | tf_op jit(solution)/shard_map/pallas_call | solution.py:328
  19.8 3.5 %collective-permute-start.9 = (f32[8,128]{1,0:T(8,128)S(1)}, f32[8,128]{1,0:T(8,128)S(1)}, u32[]{:S(2)}, u32[]{:S(2)}) collective-permute-start(f32[8,128]{1,0:T(8,128)S(1)} %get-tuple-element.9.own_ref), channel_id=1, source_target_pairs={{0,7},{1,2},{2,1},{3,4},{4,3},{5,6},{6,5},{7,0},{8,15},{9,10},{10,... | collective-permute-start | bytes 12296 | tf_op jit(solution)/shard_map/ppermute | solution.py:339
  23.3 0.0 collective-permute-start.8
  23.3 0.0 copy-start.1
  23.3 0.8 %copy.9 = f32[1152,1,128]{2,1,0:T(1,128)} copy(f32[1152,1,128]{2,1,0:T(1,128)S(1)} %bitcast.7) | data formatting | bytes 1179648
  24.1 0.6 %collective-permute-done.9.other_ref = f32[8,128]{1,0:T(8,128)S(1)} collective-permute-done((f32[8,128]{1,0:T(8,128)S(1)}, f32[8,128]{1,0:T(8,128)S(1)}, u32[]{:S(2)}, u32[]{:S(2)}) %collective-permute-start.9) | collective-permute-done | bytes 4128 | tf_op jit(solution)/shard_map/ppermute | solution.py:339
  24.7 0.0 collective-permute-done.8.mate_ref
  24.7 0.0 copy-done.1
  24.7 0.7 %shard_map.80 = f32[2,512]{1,0:T(2,128)} custom-call(s32[1,512]{1,0:T(1,128)S(1)} %copy-done.1, f32[8,128]{1,0:T(8,128)S(1)} %get-tuple-element.9.own_ref, f32[8,128]{1,0:T(8,128)S(1)} %collective-permute-done.8.mate_ref, f32[8,128]{1,0:T(8,128)S(1)} %collective-permute-done.9.other_ref), custom_call_target="tpu_custom_call" | custom-call | tf_op jit(solution)/shard_map/pallas_call | solution.py:341
  (2 shorter events, 0.0 us)
Async XLA Ops:
  0.6 18.1 %collective-permute-start.5 = (f32[1152,128]{1,0:T(8,128)}, f32[1152,128]{1,0:T(8,128)S(1)}, u32[]{:S(2)}, u32[]{:S(2)}) collective-permute-start(f32[1152,128]{1,0:T(8,128)} %bitcast.8), channel_id=1, source_target_pairs={{0,7},{1,2},{2,1},{3,4},{4,3},{5,6},{6,5},{7,0},{8,15},{9,10},{10,... | collective-permute-start | bytes 1769480 | tf_op jit(solution)/shard_map/ppermute | solution.py:294
  5.2 13.5 %collective-permute-start.4 = (f32[1152,128]{1,0:T(8,128)}, f32[1152,128]{1,0:T(8,128)S(1)}, u32[]{:S(2)}, u32[]{:S(2)}) collective-permute-start(f32[1152,128]{1,0:T(8,128)} %bitcast.9), channel_id=1, source_target_pairs={{0,1},{1,0},{2,3},{3,2},{4,5},{5,4},{6,7},{7,6},{8,9},{9,8},{10,11... | collective-permute-start | bytes 1769480 | tf_op jit(solution)/shard_map/ppermute | solution.py:295
  5.9 1.4 %collective-permute-start = (f32[24,128]{1,0:T(8,128)S(1)}, f32[24,128]{1,0:T(8,128)S(1)}, u32[]{:S(2)}, u32[]{:S(2)}) collective-permute-start(f32[24,128]{1,0:T(8,128)S(1)} %shard_map.77), channel_id=1, source_target_pairs={{0,1},{1,0},{2,3},{3,2},{4,5},{5,4},{6,7},{7,6},{8,9},{9,8},{10,11... | collective-permute-start | bytes 36872 | tf_op jit(solution)/shard_map/ppermute | solution.py:311
  7.3 4.0 %collective-permute-start.3 = (f32[24,128]{1,0:T(8,128)S(1)}, f32[24,128]{1,0:T(8,128)S(1)}, u32[]{:S(2)}, u32[]{:S(2)}) collective-permute-start(f32[24,128]{1,0:T(8,128)S(1)} %add.12), channel_id=1, source_target_pairs={{0,25},{1,24},{2,27},{3,26},{4,29},{5,28},{6,31},{7,30},{8,17},{9,... | collective-permute-start | bytes 36872 | tf_op jit(solution)/shard_map/ppermute | solution.py:291
  9.9 3.1 %collective-permute-start.2 = (f32[24,128]{1,0:T(8,128)S(1)}, f32[24,128]{1,0:T(8,128)S(1)}, u32[]{:S(2)}, u32[]{:S(2)}) collective-permute-start(f32[24,128]{1,0:T(8,128)S(1)} %add.12), channel_id=1, source_target_pairs={{0,17},{1,16},{2,19},{3,18},{4,21},{5,20},{6,23},{7,22},{8,25},{9,... | collective-permute-start | bytes 36872 | tf_op jit(solution)/shard_map/ppermute | solution.py:291
  10.2 3.1 %collective-permute-start.1 = (f32[24,128]{1,0:T(8,128)S(1)}, f32[24,128]{1,0:T(8,128)S(1)}, u32[]{:S(2)}, u32[]{:S(2)}) collective-permute-start(f32[24,128]{1,0:T(8,128)S(1)} %add.12), channel_id=1, source_target_pairs={{0,9},{1,8},{2,11},{3,10},{4,13},{5,12},{6,15},{7,14},{8,1},{9,0},... | collective-permute-start | bytes 36872 | tf_op jit(solution)/shard_map/ppermute | solution.py:291
  13.3 5.4 %copy-start = (f32[64,128]{1,0:T(8,128)S(1)}, f32[64,128]{1,0:T(8,128)}, u32[]{:S(2)}) copy-start(f32[64,128]{1,0:T(8,128)} %constant.2.clone.table_ref) | copy-start | bytes 98308
  13.3 5.4 %collective-permute-start.7 = (f32[24,128]{1,0:T(8,128)S(1)}, f32[24,128]{1,0:T(8,128)S(1)}, u32[]{:S(2)}, u32[]{:S(2)}) collective-permute-start(f32[24,128]{1,0:T(8,128)S(1)} %add_add_fusion._.band_ref), channel_id=1, source_target_pairs={{0,3},{1,2},{2,5},{3,4},{4,7},{5,6},{6,1},{7,0},{8,11},{9,10},{10,... | collective-permute-start | bytes 36872 | tf_op jit(solution)/shard_map/ppermute | solution.py:291
  13.5 5.2 %collective-permute-start.6 = (f32[24,128]{1,0:T(8,128)S(1)}, f32[24,128]{1,0:T(8,128)S(1)}, u32[]{:S(2)}, u32[]{:S(2)}) collective-permute-start(f32[24,128]{1,0:T(8,128)S(1)} %add_add_fusion._.band_ref), channel_id=1, source_target_pairs={{0,7},{1,6},{2,1},{3,0},{4,3},{5,2},{6,5},{7,4},{8,15},{9,14},{10,... | collective-permute-start | bytes 36872 | tf_op jit(solution)/shard_map/ppermute | solution.py:291
  19.8 4.9 %collective-permute-start.9 = (f32[8,128]{1,0:T(8,128)S(1)}, f32[8,128]{1,0:T(8,128)S(1)}, u32[]{:S(2)}, u32[]{:S(2)}) collective-permute-start(f32[8,128]{1,0:T(8,128)S(1)} %get-tuple-element.9.own_ref), channel_id=1, source_target_pairs={{0,7},{1,2},{2,1},{3,4},{4,3},{5,6},{6,5},{7,0},{8,15},{9,10},{10,... | collective-permute-start | bytes 12296 | tf_op jit(solution)/shard_map/ppermute | solution.py:339
  23.3 1.4 %collective-permute-start.8 = (f32[8,128]{1,0:T(8,128)S(1)}, f32[8,128]{1,0:T(8,128)S(1)}, u32[]{:S(2)}, u32[]{:S(2)}) collective-permute-start(f32[8,128]{1,0:T(8,128)S(1)} %get-tuple-element.9.own_ref), channel_id=1, source_target_pairs={{0,1},{1,0},{2,3},{3,2},{4,5},{5,4},{6,7},{7,6},{8,9},{9,8},{10,11... | collective-permute-start | bytes 12296 | tf_op jit(solution)/shard_map/ppermute | solution.py:340
  23.3 1.4 %copy-start.1 = (s32[1,512]{1,0:T(1,128)S(1)}, s32[1,512]{1,0:T(1,128)}, u32[]{:S(2)}) copy-start(s32[1,512]{1,0:T(1,128)} %coupling_ref.1) | copy-start | bytes 6148

commit v8 on v7

--- a/solution.py
+++ b/solution.py
@@ -33,6 +33,10 @@
     me = lax.axis_index("dev")
     odd = lax.rem(me, 2)
     return me - odd - 1, odd, lax.axis_index("grp")
+
+
+def padded(levels):
+    return -(-levels // 8) * 8
 
 
 def level_groups(levels):
@@ -146,7 +150,7 @@
 
 def step_kernel(
     table_ref, own_ref, sums_ref, mate_ref, other_ref, band_ref, after_ref, before_ref, updated_ref, drift_ref,
-    other_sums_ref,
+    other_sums_ref, scale_ref,
 ):
     bins, width = own_ref.shape
     lanes = 8
@@ -165,6 +169,8 @@
 
     cosine = [table_ref[8 * k : 8 * k + 8, :] for k in range(4)]
     sine = [table_ref[NDIR + 8 * k : NDIR + 8 * k + 8, :] for k in range(4)]
+
+    steps = padded(bins // NDIR)
 
     def column_state(slot, sums, place_row):
         count = jnp.maximum(field(COUNT, slot), 1.0)
@@ -175,13 +181,16 @@
         gain = WIND_GAIN * 0.64
         along = [(gain * rel_x) * cosine[k] + (gain * rel_y) * sine[k] for k in range(4)]
         sea = field(SEA, slot)
-        damp = jnp.broadcast_to(damping_of(sums, place_row, sea), (lanes, width))
-        sea = jnp.broadcast_to(sea, (lanes, width))
-        return mean_x, mean_y, along, sea, damp
-
-    own_x, own_y, along_own, sea_own, damp_own = column_state(slot_own, sums_ref, 0)
-    mate_x, _, along_mate, sea_mate, damp_mate = column_state(slot_mate, other_sums_ref, 2)
-    other_x, _, along_other, sea_other, damp_other = column_state(slot_other, other_sums_ref, 0)
+        squares = table_ref[2 * NDIR : 2 * NDIR + steps, :]
+        scale = sea / (1.0 + squares * damping_of(sums, place_row, sea))
+        return mean_x, mean_y, along, sea, scale
+
+    own_x, own_y, along_own, sea_own, scale = column_state(slot_own, sums_ref, 0)
+    scale_ref[0 * steps : 1 * steps, :] = scale
+    mate_x, _, along_mate, sea_mate, scale = column_state(slot_mate, other_sums_ref, 2)
+    scale_ref[1 * steps : 2 * steps, :] = scale
+    other_x, _, along_other, sea_other, scale = column_state(slot_other, other_sums_ref, 0)
+    scale_ref[2 * steps : 3 * steps, :] = scale
     flow_x = CURRENT_TOP * jnp.tanh(own_x)
     flow_y = CURRENT_TOP * jnp.tanh(own_y)
     sign = jnp.where(odd > 0, 1.0, -1.0)
@@ -192,10 +201,13 @@
         (-0.5 * sign) * (flow_x + CURRENT_TOP * jnp.tanh(other_x)), (lanes, width)
     )
     flow_y = jnp.broadcast_to(flow_y, (lanes, width))
-    face_north = 0.5 * (flow_y + pltpu.roll(flow_y, width - 1, 1))
     inner = jnp.where(
         lax.broadcasted_iota(jnp.int32, (lanes, width), 1) < width - 1, 1.0, 0.0
     )
+    face_north = (0.5 * inner) * (flow_y + pltpu.roll(flow_y, width - 1, 1))
+    inner_sine = [inner * sine[k] for k in range(4)]
+    sea_own = jnp.broadcast_to(sea_own, (lanes, width))
+    face_sum = face_mate + face_other
     signed_cosine = [sign * cosine[k] for k in range(4)]
 
     def level_step(index, carry):
@@ -203,11 +215,13 @@
         sums = list(sums)
         for sub in range(inner_count):
             square = frequency * frequency
-            scale_own = sea_own / (1.0 + square * damp_own)
-            scale_mate = sea_mate / (1.0 + square * damp_mate)
-            scale_other = sea_other / (1.0 + square * damp_other)
+            level = index * inner_count + sub
+            scale_own, scale_mate, scale_other = (
+                jnp.broadcast_to(scale_ref[pl.ds(column * steps + level, 1), :], (lanes, width))
+                for column in range(3)
+            )
             weight = (STOKES_GAIN * 0.1) * (square * square)
-            base = (index * inner_count + sub) * NDIR
+            base = level * NDIR
             for k in range(4):
                 rows = pl.ds(pl.multiple_of(base + 8 * k, 8), 8)
 
@@ -223,12 +237,10 @@
                 q_other = face_other - speed_x
                 in_mate = jnp.maximum(q_mate, 0.0)
                 in_other = jnp.maximum(q_other, 0.0)
-                out = (in_mate - q_mate) + (in_other - q_other)
-                north = speed * sine[k] + face_north
-                flux = (
-                    jnp.maximum(north, 0.0) * forced
-                    + jnp.minimum(north, 0.0) * pltpu.roll(forced, width - 1, 1)
-                ) * inner
+                out = (in_mate + in_other) - face_sum
+                north = speed * inner_sine[k] + face_north
+                flux = jnp.maximum(north, 0.0) * forced
+                flux = flux + jnp.minimum(north, 0.0) * pltpu.roll(forced, width - 1, 1)
                 new = forced - out * forced + (in_mate * forced_mate + in_other * forced_other)
                 new = (new - (flux - pltpu.roll(flux, 1, 1))) * sea_own
                 updated_ref[rows, :] = new
@@ -265,9 +277,12 @@
         cells_ref[:, part] = value * ocean
 
 
-def direction_table(width):
+def direction_table(bins, width):
     heading = np.arange(NDIR) * (2.0 * math.pi / NDIR)
     table = np.concatenate([np.cos(heading), np.sin(heading)]).astype(np.float32)
+    levels = np.minimum(np.arange(padded(bins // NDIR)), bins // NDIR - 1)
+    squares = ((FIRST_FREQ * GROWTH**levels) ** 2).astype(np.float32)
+    table = np.concatenate([table, squares])
     return jnp.asarray(np.repeat(table[:, None], width, axis=1))
 
 
@@ -333,8 +348,11 @@
         ),
         in_specs=[VMEM] * 8,
         out_specs=(VMEM, VMEM),
-        scratch_shapes=[pltpu.VMEM((8, width), jnp.float32)],
-    )(*near(direction_table(width), own_near, sums, mate, other, band, after, before))
+        scratch_shapes=[
+            pltpu.VMEM((8, width), jnp.float32),
+            pltpu.VMEM((3 * padded(bins // NDIR), width), jnp.float32),
+        ],
+    )(*near(direction_table(bins, width), own_near, sums, mate, other, band, after, before))
 
     drift_other = lax.ppermute(drift, "dev", others)
     drift_mate = lax.ppermute(drift, "dev", mates)

time: 25.6 us -> 25.5 us (level)
  no operation moved by 1% of the time
where the time goes in v8:
time: 25.5 us; the launch traced here: 25.3 us
  starting transfers between devices  15.4 us (60%)
  waiting for transfers between devices  4.92 us (19%)
  Pallas kernels  3.52 us (14%)
  local copies, waits for them, and re-layouts  0.82 us (3%)
  between operations  0.67 us (3%)
    ppermute x5, starting transfers between devices, crossed(): return lax.ppermute(value, ('grp', 'dev'), pairs)  6.75 us
    ppermute x1, starting transfers between devices, body(): other = lax.ppermute(own, 'dev', others)  4.55 us
    ppermute x5, waiting for transfers between devices, crossed(): return lax.ppermute(value, ('grp', 'dev'), pairs)  3.48 us
    ppermute x1, starting transfers between devices, body(): drift_other = lax.ppermute(drift, 'dev', others)  3.48 us
    pallas_call x1, Pallas kernels, body(): pl.pallas_call(fetch_kernel, out_shape=(pltpu.VMEM((bins, width), jnp.flo...  1.13 us
    pallas_call x1, Pallas kernels, body(): pl.pallas_call(step_kernel, out_shape=(pltpu.VMEM((bins, width), jnp.floa...  0.95 us
    ppermute x1, waiting for transfers between devices, body(): band = band + lax.ppermute(band, 'dev', mates)  0.83 us
    unnamed x5, local copies, waits for them, and re-layouts  0.82 us
  transfers between devices with their start and end apart: 10, of which 6 were waited for; matrix products, arithmetic and copies ran while one was open for 3% of the time, Pallas kernels for 7%

profile of v8, /device:TPU:0, one launch (start us, length us, event | category | flops | bytes accessed | tf_op | source)
XLA Modules:
  0.0 25.3 jit_solution(8284245389221167983)
XLA Ops:
  0.6 4.6 %collective-permute-start.5 = (f32[1152,128]{1,0:T(8,128)}, f32[1152,128]{1,0:T(8,128)S(1)}, u32[]{:S(2)}, u32[]{:S(2)}) collective-permute-start(f32[1152,128]{1,0:T(8,128)} %bitcast.8), channel_id=1, source_target_pairs={{0,7},{1,2},{2,1},{3,4},{4,3},{5,6},{6,5},{7,0},{8,15},{9,10},{10,... | collective-permute-start | bytes 1769480 | tf_op jit(solution)/shard_map/ppermute | solution.py:309
  5.2 0.0 collective-permute-start.4
  5.2 0.7 %shard_map.77 = f32[24,128]{1,0:T(8,128)S(1)} custom-call(s32[1,512]{1,0:T(1,128)} %coupling_ref.1, f32[2,512]{1,0:T(2,128)} %bitcast.11, s32[1,128]{1,0:T(1,128)} %sea_hbm.1, f32[2,128]{1,0:T(2,128)} %bitcast.13), custom_call_target="tpu_custom_call" | custom-call | tf_op jit(solution)/shard_map/pallas_call | solution.py:313
  5.9 0.6 %collective-permute-start = (f32[24,128]{1,0:T(8,128)S(1)}, f32[24,128]{1,0:T(8,128)S(1)}, u32[]{:S(2)}, u32[]{:S(2)}) collective-permute-start(f32[24,128]{1,0:T(8,128)S(1)} %shard_map.77), channel_id=1, source_target_pairs={{0,1},{1,0},{2,3},{3,2},{4,5},{5,4},{6,7},{7,6},{8,9},{9,8},{10,11... | collective-permute-start | bytes 36872 | tf_op jit(solution)/shard_map/ppermute | solution.py:326
  6.5 0.8 %collective-permute-done = f32[24,128]{1,0:T(8,128)S(1)} collective-permute-done((f32[24,128]{1,0:T(8,128)S(1)}, f32[24,128]{1,0:T(8,128)S(1)}, u32[]{:S(2)}, u32[]{:S(2)}) %collective-permute-start) | collective-permute-done | bytes 12320 | tf_op jit(solution)/shard_map/ppermute | solution.py:326
  7.3 2.6 %collective-permute-start.3 = (f32[24,128]{1,0:T(8,128)S(1)}, f32[24,128]{1,0:T(8,128)S(1)}, u32[]{:S(2)}, u32[]{:S(2)}) collective-permute-start(f32[24,128]{1,0:T(8,128)S(1)} %add.12), channel_id=1, source_target_pairs={{0,25},{1,24},{2,27},{3,26},{4,29},{5,28},{6,31},{7,30},{8,17},{9,... | collective-permute-start | bytes 36872 | tf_op jit(solution)/shard_map/ppermute | solution.py:306
  9.9 0.3 %collective-permute-start.2 = (f32[24,128]{1,0:T(8,128)S(1)}, f32[24,128]{1,0:T(8,128)S(1)}, u32[]{:S(2)}, u32[]{:S(2)}) collective-permute-start(f32[24,128]{1,0:T(8,128)S(1)} %add.12), channel_id=1, source_target_pairs={{0,17},{1,16},{2,19},{3,18},{4,21},{5,20},{6,23},{7,22},{8,25},{9,... | collective-permute-start | bytes 36872 | tf_op jit(solution)/shard_map/ppermute | solution.py:306
  10.2 0.3 %collective-permute-start.1 = (f32[24,128]{1,0:T(8,128)S(1)}, f32[24,128]{1,0:T(8,128)S(1)}, u32[]{:S(2)}, u32[]{:S(2)}) collective-permute-start(f32[24,128]{1,0:T(8,128)S(1)} %add.12), channel_id=1, source_target_pairs={{0,9},{1,8},{2,11},{3,10},{4,13},{5,12},{6,15},{7,14},{8,1},{9,0},... | collective-permute-start | bytes 36872 | tf_op jit(solution)/shard_map/ppermute | solution.py:306
  10.5 0.9 %collective-permute-done.3 = f32[24,128]{1,0:T(8,128)S(1)} collective-permute-done((f32[24,128]{1,0:T(8,128)S(1)}, f32[24,128]{1,0:T(8,128)S(1)}, u32[]{:S(2)}, u32[]{:S(2)}) %collective-permute-start.3) | collective-permute-done | bytes 12320 | tf_op jit(solution)/shard_map/ppermute | solution.py:306
  11.4 1.7 %collective-permute-done.2 = f32[24,128]{1,0:T(8,128)S(1)} collective-permute-done((f32[24,128]{1,0:T(8,128)S(1)}, f32[24,128]{1,0:T(8,128)S(1)}, u32[]{:S(2)}, u32[]{:S(2)}) %collective-permute-start.2) | collective-permute-done | bytes 12320 | tf_op jit(solution)/shard_map/ppermute | solution.py:306
  13.0 0.3 %collective-permute-done.1 = f32[24,128]{1,0:T(8,128)S(1)} collective-permute-done((f32[24,128]{1,0:T(8,128)S(1)}, f32[24,128]{1,0:T(8,128)S(1)}, u32[]{:S(2)}, u32[]{:S(2)}) %collective-permute-start.1) | collective-permute-done | bytes 12320 | tf_op jit(solution)/shard_map/ppermute | solution.py:306
  13.3 0.0 copy-start
  13.3 0.2 collective-permute-start.7
  13.5 3.4 %collective-permute-start.6 = (f32[24,128]{1,0:T(8,128)S(1)}, f32[24,128]{1,0:T(8,128)S(1)}, u32[]{:S(2)}, u32[]{:S(2)}) collective-permute-start(f32[24,128]{1,0:T(8,128)S(1)} %add_add_fusion._.band_ref), channel_id=1, source_target_pairs={{0,7},{1,6},{2,1},{3,0},{4,3},{5,2},{6,5},{7,4},{8,15},{9,14},{10,... | collective-permute-start | bytes 36872 | tf_op jit(solution)/shard_map/ppermute | solution.py:306
  16.9 1.1 %shard_map.78 = (f32[1152,128]{1,0:T(8,128)S(1)}, f32[8,128]{1,0:T(8,128)S(1)}) custom-call(f32[1152,128]{1,0:T(8,128)} %bitcast.10, f32[24,128]{1,0:T(8,128)S(1)} %add_add_fusion._.band_ref), custom_call_target="tpu_custom_call" | custom-call | tf_op jit(solution)/shard_map/pallas_call | solution.py:333
  18.0 0.7 %collective-permute-done.7.before_ref = f32[24,128]{1,0:T(8,128)S(1)} collective-permute-done((f32[24,128]{1,0:T(8,128)S(1)}, f32[24,128]{1,0:T(8,128)S(1)}, u32[]{:S(2)}, u32[]{:S(2)}) %collective-permute-start.7) | collective-permute-done | bytes 12320 | tf_op jit(solution)/shard_map/ppermute | solution.py:306
  18.7 0.0 collective-permute-done.6.after_ref
  18.7 0.0 collective-permute-done.5.other_ref
  18.7 0.0 collective-permute-done.4.mate_ref
  18.7 0.0 copy-done
  18.7 1.0 %shard_map.79 = (f32[1152,128]{1,0:T(8,128)S(1)}, f32[8,128]{1,0:T(8,128)S(1)}) custom-call(f32[104,128]{1,0:T(8,128)S(1)} %copy-done, f32[1152,128]{1,0:T(8,128)S(1)} %get-tuple-element.6.own_ref, f32[8,128]{1,0:T(8,128)S(1)} %get-tuple-element.7.sums_ref, f32[1152,128]{1,0:T(8,128)S(1)} %collective-permute-done.4.mate_ref, ...), custom_call_target="tpu_custom_call" | custom-call | tf_op jit(solution)/shard_map/pallas_call | solution.py:343
  19.7 3.5 %collective-permute-start.9 = (f32[8,128]{1,0:T(8,128)S(1)}, f32[8,128]{1,0:T(8,128)S(1)}, u32[]{:S(2)}, u32[]{:S(2)}) collective-permute-start(f32[8,128]{1,0:T(8,128)S(1)} %get-tuple-element.9.own_ref), channel_id=1, source_target_pairs={{0,7},{1,2},{2,1},{3,4},{4,3},{5,6},{6,5},{7,0},{8,15},{9,10},{10,... | collective-permute-start | bytes 12296 | tf_op jit(solution)/shard_map/ppermute | solution.py:357
  23.2 0.0 collective-permute-start.8
  23.2 0.0 copy-start.1
  23.2 0.8 %copy.9 = f32[1152,1,128]{2,1,0:T(1,128)} copy(f32[1152,1,128]{2,1,0:T(1,128)S(1)} %bitcast.7) | data formatting | bytes 1179648
  24.0 0.6 %collective-permute-done.9.other_ref = f32[8,128]{1,0:T(8,128)S(1)} collective-permute-done((f32[8,128]{1,0:T(8,128)S(1)}, f32[8,128]{1,0:T(8,128)S(1)}, u32[]{:S(2)}, u32[]{:S(2)}) %collective-permute-start.9) | collective-permute-done | bytes 4128 | tf_op jit(solution)/shard_map/ppermute | solution.py:357
  24.6 0.0 collective-permute-done.8.mate_ref
  24.6 0.0 copy-done.1
  24.6 0.7 %shard_map.80 = f32[2,512]{1,0:T(2,128)} custom-call(s32[1,512]{1,0:T(1,128)S(1)} %copy-done.1, f32[8,128]{1,0:T(8,128)S(1)} %get-tuple-element.9.own_ref, f32[8,128]{1,0:T(8,128)S(1)} %collective-permute-done.8.mate_ref, f32[8,128]{1,0:T(8,128)S(1)} %collective-permute-done.9.other_ref), custom_call_target="tpu_custom_call" | custom-call | tf_op jit(solution)/shard_map/pallas_call | solution.py:359
  (2 shorter events, 0.0 us)
Async XLA Ops:
  0.6 18.1 %collective-permute-start.5 = (f32[1152,128]{1,0:T(8,128)}, f32[1152,128]{1,0:T(8,128)S(1)}, u32[]{:S(2)}, u32[]{:S(2)}) collective-permute-start(f32[1152,128]{1,0:T(8,128)} %bitcast.8), channel_id=1, source_target_pairs={{0,7},{1,2},{2,1},{3,4},{4,3},{5,6},{6,5},{7,0},{8,15},{9,10},{10,... | collective-permute-start | bytes 1769480 | tf_op jit(solution)/shard_map/ppermute | solution.py:309
  5.2 13.5 %collective-permute-start.4 = (f32[1152,128]{1,0:T(8,128)}, f32[1152,128]{1,0:T(8,128)S(1)}, u32[]{:S(2)}, u32[]{:S(2)}) collective-permute-start(f32[1152,128]{1,0:T(8,128)} %bitcast.9), channel_id=1, source_target_pairs={{0,1},{1,0},{2,3},{3,2},{4,5},{5,4},{6,7},{7,6},{8,9},{9,8},{10,11... | collective-permute-start | bytes 1769480 | tf_op jit(solution)/shard_map/ppermute | solution.py:310
  5.9 1.4 %collective-permute-start = (f32[24,128]{1,0:T(8,128)S(1)}, f32[24,128]{1,0:T(8,128)S(1)}, u32[]{:S(2)}, u32[]{:S(2)}) collective-permute-start(f32[24,128]{1,0:T(8,128)S(1)} %shard_map.77), channel_id=1, source_target_pairs={{0,1},{1,0},{2,3},{3,2},{4,5},{5,4},{6,7},{7,6},{8,9},{9,8},{10,11... | collective-permute-start | bytes 36872 | tf_op jit(solution)/shard_map/ppermute | solution.py:326
  7.3 4.0 %collective-permute-start.3 = (f32[24,128]{1,0:T(8,128)S(1)}, f32[24,128]{1,0:T(8,128)S(1)}, u32[]{:S(2)}, u32[]{:S(2)}) collective-permute-start(f32[24,128]{1,0:T(8,128)S(1)} %add.12), channel_id=1, source_target_pairs={{0,25},{1,24},{2,27},{3,26},{4,29},{5,28},{6,31},{7,30},{8,17},{9,... | collective-permute-start | bytes 36872 | tf_op jit(solution)/shard_map/ppermute | solution.py:306
  9.9 3.1 %collective-permute-start.2 = (f32[24,128]{1,0:T(8,128)S(1)}, f32[24,128]{1,0:T(8,128)S(1)}, u32[]{:S(2)}, u32[]{:S(2)}) collective-permute-start(f32[24,128]{1,0:T(8,128)S(1)} %add.12), channel_id=1, source_target_pairs={{0,17},{1,16},{2,19},{3,18},{4,21},{5,20},{6,23},{7,22},{8,25},{9,... | collective-permute-start | bytes 36872 | tf_op jit(solution)/shard_map/ppermute | solution.py:306
  10.2 3.1 %collective-permute-start.1 = (f32[24,128]{1,0:T(8,128)S(1)}, f32[24,128]{1,0:T(8,128)S(1)}, u32[]{:S(2)}, u32[]{:S(2)}) collective-permute-start(f32[24,128]{1,0:T(8,128)S(1)} %add.12), channel_id=1, source_target_pairs={{0,9},{1,8},{2,11},{3,10},{4,13},{5,12},{6,15},{7,14},{8,1},{9,0},... | collective-permute-start | bytes 36872 | tf_op jit(solution)/shard_map/ppermute | solution.py:306
  13.3 5.4 %copy-start = (f32[104,128]{1,0:T(8,128)S(1)}, f32[104,128]{1,0:T(8,128)}, u32[]{:S(2)}) copy-start(f32[104,128]{1,0:T(8,128)} %constant.2.clone.table_ref) | copy-start | bytes 159748
  13.3 5.4 %collective-permute-start.7 = (f32[24,128]{1,0:T(8,128)S(1)}, f32[24,128]{1,0:T(8,128)S(1)}, u32[]{:S(2)}, u32[]{:S(2)}) collective-permute-start(f32[24,128]{1,0:T(8,128)S(1)} %add_add_fusion._.band_ref), channel_id=1, source_target_pairs={{0,3},{1,2},{2,5},{3,4},{4,7},{5,6},{6,1},{7,0},{8,11},{9,10},{10,... | collective-permute-start | bytes 36872 | tf_op jit(solution)/shard_map/ppermute | solution.py:306
  13.5 5.2 %collective-permute-start.6 = (f32[24,128]{1,0:T(8,128)S(1)}, f32[24,128]{1,0:T(8,128)S(1)}, u32[]{:S(2)}, u32[]{:S(2)}) collective-permute-start(f32[24,128]{1,0:T(8,128)S(1)} %add_add_fusion._.band_ref), channel_id=1, source_target_pairs={{0,7},{1,6},{2,1},{3,0},{4,3},{5,2},{6,5},{7,4},{8,15},{9,14},{10,... | collective-permute-start | bytes 36872 | tf_op jit(solution)/shard_map/ppermute | solution.py:306
  19.7 4.9 %collective-permute-start.9 = (f32[8,128]{1,0:T(8,128)S(1)}, f32[8,128]{1,0:T(8,128)S(1)}, u32[]{:S(2)}, u32[]{:S(2)}) collective-permute-start(f32[8,128]{1,0:T(8,128)S(1)} %get-tuple-element.9.own_ref), channel_id=1, source_target_pairs={{0,7},{1,2},{2,1},{3,4},{4,3},{5,6},{6,5},{7,0},{8,15},{9,10},{10,... | collective-permute-start | bytes 12296 | tf_op jit(solution)/shard_map/ppermute | solution.py:357
  23.2 1.4 %collective-permute-start.8 = (f32[8,128]{1,0:T(8,128)S(1)}, f32[8,128]{1,0:T(8,128)S(1)}, u32[]{:S(2)}, u32[]{:S(2)}) collective-permute-start(f32[8,128]{1,0:T(8,128)S(1)} %get-tuple-element.9.own_ref), channel_id=1, source_target_pairs={{0,1},{1,0},{2,3},{3,2},{4,5},{5,4},{6,7},{7,6},{8,9},{9,8},{10,11... | collective-permute-start | bytes 12296 | tf_op jit(solution)/shard_map/ppermute | solution.py:358
  23.2 1.4 %copy-start.1 = (s32[1,512]{1,0:T(1,128)S(1)}, s32[1,512]{1,0:T(1,128)}, u32[]{:S(2)}) copy-start(s32[1,512]{1,0:T(1,128)} %coupling_ref.1) | copy-start | bytes 6148

commit v9 on v8

--- a/solution.py
+++ b/solution.py
@@ -138,6 +138,12 @@
     spectrum_sums(own_ref, sums_ref, 0)
 
 
+def halo_kernel(mate_ref, other_ref, sums_ref):
+    sums_ref[...] = jnp.zeros_like(sums_ref)
+    spectrum_sums(other_ref, sums_ref, 0)
+    spectrum_sums(mate_ref, sums_ref, 2)
+
+
 def damping_of(sums_ref, place_row, sea):
     total = sums_ref[place_row : place_row + 1, :] * sea
     moment = sums_ref[place_row + 1 : place_row + 2, :] * sea
@@ -149,13 +155,11 @@
 
 
 def step_kernel(
-    table_ref, own_ref, sums_ref, mate_ref, other_ref, band_ref, after_ref, before_ref, updated_ref, drift_ref,
-    other_sums_ref, scale_ref,
+    table_ref, own_ref, sums_ref, other_sums_ref, mate_ref, other_ref, band_ref, after_ref, before_ref, updated_ref, drift_ref,
+    scale_ref,
 ):
     bins, width = own_ref.shape
     lanes = 8
-    spectrum_sums(mate_ref, other_sums_ref, 2)
-    spectrum_sums(other_ref, other_sums_ref, 0)
     outer_count, inner_count = level_groups(bins // NDIR)
     _, odd, _ = place()
     slot_own, slot_mate, slot_other = 1 + odd, 2 - odd, 3 * odd
@@ -340,19 +344,24 @@
         out_specs=(VMEM, VMEM),
         scratch_shapes=[pltpu.SemaphoreType.DMA],
     )(own, *near(band))
+    halo_sums = pl.pallas_call(
+        halo_kernel,
+        out_shape=pltpu.VMEM((8, width), jnp.float32),
+        in_specs=[VMEM] * 2,
+        out_specs=VMEM,
+    )(*near(mate, other))
     updated, drift = pl.pallas_call(
         step_kernel,
         out_shape=(
             pltpu.VMEM((bins, width), jnp.float32),
             pltpu.VMEM((8, width), jnp.float32),
         ),
-        in_specs=[VMEM] * 8,
+        in_specs=[VMEM] * 9,
         out_specs=(VMEM, VMEM),
         scratch_shapes=[
-            pltpu.VMEM((8, width), jnp.float32),
             pltpu.VMEM((3 * padded(bins // NDIR), width), jnp.float32),
         ],
-    )(*near(direction_table(bins, width), own_near, sums, mate, other, band, after, before))
+    )(*near(direction_table(bins, width), own_near, sums, halo_sums, mate, other, band, after, before))
 
     drift_other = lax.ppermute(drift, "dev", others)
     drift_mate = lax.ppermute(drift, "dev", mates)

time: 25.5 us -> 25.5 us (level)
    ppermute x5, waiting for transfers between devices: 3.48 us -> 2.96 us  [crossed(): return lax.ppermute(value, ('grp', 'dev'), pairs)]
    ppermute x1, waiting for transfers between devices: 0.01 us -> 0.45 us  [body(): other = lax.ppermute(own, 'dev', others)]
  transfers between devices with their start and end apart: 10 -> 10, of which waited for: 6 -> 7; matrix products, arithmetic and copies ran while one was open for 3% -> 3% of each run, Pallas kernels for 7% -> 8%
where the time goes in v9:
time: 25.5 us; the launch traced here: 25.3 us
  starting transfers between devices  15.2 us (60%)
  waiting for transfers between devices  4.97 us (19%)
  Pallas kernels  3.54 us (14%)
  local copies, waits for them, and re-layouts  0.91 us (4%)
  between operations  0.67 us (3%)
    ppermute x5, starting transfers between devices, crossed(): return lax.ppermute(value, ('grp', 'dev'), pairs)  6.7 us
    ppermute x1, starting transfers between devices, body(): other = lax.ppermute(own, 'dev', others)  4.55 us
    ppermute x1, starting transfers between devices, body(): drift_other = lax.ppermute(drift, 'dev', others)  3.35 us
    ppermute x5, waiting for transfers between devices, crossed(): return lax.ppermute(value, ('grp', 'dev'), pairs)  2.96 us
    pallas_call x1, Pallas kernels, body(): pl.pallas_call(fetch_kernel, out_shape=(pltpu.VMEM((bins, width), jnp.flo...  1.13 us
    unnamed x5, local copies, waits for them, and re-layouts  0.91 us
    pallas_call x1, Pallas kernels, body(): pl.pallas_call(step_kernel, out_shape=(pltpu.VMEM((bins, width), jnp.floa...  0.88 us
    ppermute x1, waiting for transfers between devices, body(): band = band + lax.ppermute(band, 'dev', mates)  0.83 us
  transfers between devices with their start and end apart: 10, of which 7 were waited for; matrix products, arithmetic and copies ran while one was open for 3% of the time, Pallas kernels for 8%

profile of v9, /device:TPU:0, one launch (start us, length us, event | category | flops | bytes accessed | tf_op | source)
XLA Modules:
  0.0 25.3 jit_solution(32904284098453032)
XLA Ops:
  0.6 4.6 %collective-permute-start.5 = (f32[1152,128]{1,0:T(8,128)}, f32[1152,128]{1,0:T(8,128)S(1)}, u32[]{:S(2)}, u32[]{:S(2)}) collective-permute-start(f32[1152,128]{1,0:T(8,128)} %bitcast.8), channel_id=1, source_target_pairs={{0,7},{1,2},{2,1},{3,4},{4,3},{5,6},{6,5},{7,0},{8,15},{9,10},{10,... | collective-permute-start | bytes 1769480 | tf_op jit(solution)/shard_map/ppermute | solution.py:313
  5.2 0.0 collective-permute-start.4
  5.2 0.7 %shard_map.77 = f32[24,128]{1,0:T(8,128)S(1)} custom-call(s32[1,512]{1,0:T(1,128)} %coupling_ref.1, f32[2,512]{1,0:T(2,128)} %bitcast.11, s32[1,128]{1,0:T(1,128)} %sea_hbm.1, f32[2,128]{1,0:T(2,128)} %bitcast.13), custom_call_target="tpu_custom_call" | custom-call | tf_op jit(solution)/shard_map/pallas_call | solution.py:317
  5.9 0.6 %collective-permute-start = (f32[24,128]{1,0:T(8,128)S(1)}, f32[24,128]{1,0:T(8,128)S(1)}, u32[]{:S(2)}, u32[]{:S(2)}) collective-permute-start(f32[24,128]{1,0:T(8,128)S(1)} %shard_map.77), channel_id=1, source_target_pairs={{0,1},{1,0},{2,3},{3,2},{4,5},{5,4},{6,7},{7,6},{8,9},{9,8},{10,11... | collective-permute-start | bytes 36872 | tf_op jit(solution)/shard_map/ppermute | solution.py:330
  6.5 0.8 %collective-permute-done = f32[24,128]{1,0:T(8,128)S(1)} collective-permute-done((f32[24,128]{1,0:T(8,128)S(1)}, f32[24,128]{1,0:T(8,128)S(1)}, u32[]{:S(2)}, u32[]{:S(2)}) %collective-permute-start) | collective-permute-done | bytes 12320 | tf_op jit(solution)/shard_map/ppermute | solution.py:330
  7.3 2.6 %collective-permute-start.3 = (f32[24,128]{1,0:T(8,128)S(1)}, f32[24,128]{1,0:T(8,128)S(1)}, u32[]{:S(2)}, u32[]{:S(2)}) collective-permute-start(f32[24,128]{1,0:T(8,128)S(1)} %add.12), channel_id=1, source_target_pairs={{0,25},{1,24},{2,27},{3,26},{4,29},{5,28},{6,31},{7,30},{8,17},{9,... | collective-permute-start | bytes 36872 | tf_op jit(solution)/shard_map/ppermute | solution.py:310
  9.9 0.3 %collective-permute-start.2 = (f32[24,128]{1,0:T(8,128)S(1)}, f32[24,128]{1,0:T(8,128)S(1)}, u32[]{:S(2)}, u32[]{:S(2)}) collective-permute-start(f32[24,128]{1,0:T(8,128)S(1)} %add.12), channel_id=1, source_target_pairs={{0,17},{1,16},{2,19},{3,18},{4,21},{5,20},{6,23},{7,22},{8,25},{9,... | collective-permute-start | bytes 36872 | tf_op jit(solution)/shard_map/ppermute | solution.py:310
  10.2 0.3 %collective-permute-start.1 = (f32[24,128]{1,0:T(8,128)S(1)}, f32[24,128]{1,0:T(8,128)S(1)}, u32[]{:S(2)}, u32[]{:S(2)}) collective-permute-start(f32[24,128]{1,0:T(8,128)S(1)} %add.12), channel_id=1, source_target_pairs={{0,9},{1,8},{2,11},{3,10},{4,13},{5,12},{6,15},{7,14},{8,1},{9,0},... | collective-permute-start | bytes 36872 | tf_op jit(solution)/shard_map/ppermute | solution.py:310
  10.5 0.9 %collective-permute-done.3 = f32[24,128]{1,0:T(8,128)S(1)} collective-permute-done((f32[24,128]{1,0:T(8,128)S(1)}, f32[24,128]{1,0:T(8,128)S(1)}, u32[]{:S(2)}, u32[]{:S(2)}) %collective-permute-start.3) | collective-permute-done | bytes 12320 | tf_op jit(solution)/shard_map/ppermute | solution.py:310
  11.4 1.7 %collective-permute-done.2 = f32[24,128]{1,0:T(8,128)S(1)} collective-permute-done((f32[24,128]{1,0:T(8,128)S(1)}, f32[24,128]{1,0:T(8,128)S(1)}, u32[]{:S(2)}, u32[]{:S(2)}) %collective-permute-start.2) | collective-permute-done | bytes 12320 | tf_op jit(solution)/shard_map/ppermute | solution.py:310
  13.0 0.3 %collective-permute-done.1 = f32[24,128]{1,0:T(8,128)S(1)} collective-permute-done((f32[24,128]{1,0:T(8,128)S(1)}, f32[24,128]{1,0:T(8,128)S(1)}, u32[]{:S(2)}, u32[]{:S(2)}) %collective-permute-start.1) | collective-permute-done | bytes 12320 | tf_op jit(solution)/shard_map/ppermute | solution.py:310
  13.3 0.1 collective-permute-start.7
  13.4 3.4 %collective-permute-start.6 = (f32[24,128]{1,0:T(8,128)S(1)}, f32[24,128]{1,0:T(8,128)S(1)}, u32[]{:S(2)}, u32[]{:S(2)}) collective-permute-start(f32[24,128]{1,0:T(8,128)S(1)} %add_add_fusion._.band_ref), channel_id=1, source_target_pairs={{0,7},{1,6},{2,1},{3,0},{4,3},{5,2},{6,5},{7,4},{8,15},{9,14},{10,... | collective-permute-start | bytes 36872 | tf_op jit(solution)/shard_map/ppermute | solution.py:310
  16.9 1.1 %shard_map.78 = (f32[1152,128]{1,0:T(8,128)S(1)}, f32[8,128]{1,0:T(8,128)S(1)}) custom-call(f32[1152,128]{1,0:T(8,128)} %bitcast.10, f32[24,128]{1,0:T(8,128)S(1)} %add_add_fusion._.band_ref), custom_call_target="tpu_custom_call" | custom-call | tf_op jit(solution)/shard_map/pallas_call | solution.py:337
  18.0 0.0 copy-start
  18.0 0.4 %collective-permute-done.5.other_ref = f32[1152,128]{1,0:T(8,128)S(1)} collective-permute-done((f32[1152,128]{1,0:T(8,128)}, f32[1152,128]{1,0:T(8,128)S(1)}, u32[]{:S(2)}, u32[]{:S(2)}) %collective-permute-start.5) | collective-permute-done | bytes 589856 | tf_op jit(solution)/shard_map/ppermute | solution.py:313
  18.5 0.0 collective-permute-done.4.mate_ref
  18.5 0.1 shard_map.79.other_sums_ref
  18.6 0.2 collective-permute-done.7.before_ref
  18.7 0.0 collective-permute-done.6.after_ref
  18.7 0.1 copy-done
  18.8 0.9 %shard_map.80 = (f32[1152,128]{1,0:T(8,128)S(1)}, f32[8,128]{1,0:T(8,128)S(1)}) custom-call(f32[104,128]{1,0:T(8,128)S(1)} %copy-done, f32[1152,128]{1,0:T(8,128)S(1)} %get-tuple-element.6.own_ref, f32[8,128]{1,0:T(8,128)S(1)} %get-tuple-element.7.sums_ref, f32[8,128]{1,0:T(8,128)S(1)} %shard_map.79.other_sums_ref, ...), custom_call_target="tpu_custom_call" | custom-call | tf_op jit(solution)/shard_map/pallas_call | solution.py:353
  19.7 3.4 %collective-permute-start.9 = (f32[8,128]{1,0:T(8,128)S(1)}, f32[8,128]{1,0:T(8,128)S(1)}, u32[]{:S(2)}, u32[]{:S(2)}) collective-permute-start(f32[8,128]{1,0:T(8,128)S(1)} %get-tuple-element.9.own_ref), channel_id=1, source_target_pairs={{0,7},{1,2},{2,1},{3,4},{4,3},{5,6},{6,5},{7,0},{8,15},{9,10},{10,... | collective-permute-start | bytes 12296 | tf_op jit(solution)/shard_map/ppermute | solution.py:366
  23.0 0.0 collective-permute-start.8
  23.0 0.0 copy-start.1
  23.0 0.8 %copy.9 = f32[1152,1,128]{2,1,0:T(1,128)} copy(f32[1152,1,128]{2,1,0:T(1,128)S(1)} %bitcast.7) | data formatting | bytes 1179648
  23.9 0.7 %collective-permute-done.9.other_ref = f32[8,128]{1,0:T(8,128)S(1)} collective-permute-done((f32[8,128]{1,0:T(8,128)S(1)}, f32[8,128]{1,0:T(8,128)S(1)}, u32[]{:S(2)}, u32[]{:S(2)}) %collective-permute-start.9) | collective-permute-done | bytes 4128 | tf_op jit(solution)/shard_map/ppermute | solution.py:366
  24.6 0.0 collective-permute-done.8.mate_ref
  24.6 0.0 copy-done.1
  24.6 0.7 %shard_map.81 = f32[2,512]{1,0:T(2,128)} custom-call(s32[1,512]{1,0:T(1,128)S(1)} %copy-done.1, f32[8,128]{1,0:T(8,128)S(1)} %get-tuple-element.9.own_ref, f32[8,128]{1,0:T(8,128)S(1)} %collective-permute-done.8.mate_ref, f32[8,128]{1,0:T(8,128)S(1)} %collective-permute-done.9.other_ref), custom_call_target="tpu_custom_call" | custom-call | tf_op jit(solution)/shard_map/pallas_call | solution.py:368
  (2 shorter events, 0.0 us)
Async XLA Ops:
  0.6 17.8 %collective-permute-start.5 = (f32[1152,128]{1,0:T(8,128)}, f32[1152,128]{1,0:T(8,128)S(1)}, u32[]{:S(2)}, u32[]{:S(2)}) collective-permute-start(f32[1152,128]{1,0:T(8,128)} %bitcast.8), channel_id=1, source_target_pairs={{0,7},{1,2},{2,1},{3,4},{4,3},{5,6},{6,5},{7,0},{8,15},{9,10},{10,... | collective-permute-start | bytes 1769480 | tf_op jit(solution)/shard_map/ppermute | solution.py:313
  5.2 13.3 %collective-permute-start.4 = (f32[1152,128]{1,0:T(8,128)}, f32[1152,128]{1,0:T(8,128)S(1)}, u32[]{:S(2)}, u32[]{:S(2)}) collective-permute-start(f32[1152,128]{1,0:T(8,128)} %bitcast.9), channel_id=1, source_target_pairs={{0,1},{1,0},{2,3},{3,2},{4,5},{5,4},{6,7},{7,6},{8,9},{9,8},{10,11... | collective-permute-start | bytes 1769480 | tf_op jit(solution)/shard_map/ppermute | solution.py:314
  5.9 1.4 %collective-permute-start = (f32[24,128]{1,0:T(8,128)S(1)}, f32[24,128]{1,0:T(8,128)S(1)}, u32[]{:S(2)}, u32[]{:S(2)}) collective-permute-start(f32[24,128]{1,0:T(8,128)S(1)} %shard_map.77), channel_id=1, source_target_pairs={{0,1},{1,0},{2,3},{3,2},{4,5},{5,4},{6,7},{7,6},{8,9},{9,8},{10,11... | collective-permute-start | bytes 36872 | tf_op jit(solution)/shard_map/ppermute | solution.py:330
  7.3 4.0 %collective-permute-start.3 = (f32[24,128]{1,0:T(8,128)S(1)}, f32[24,128]{1,0:T(8,128)S(1)}, u32[]{:S(2)}, u32[]{:S(2)}) collective-permute-start(f32[24,128]{1,0:T(8,128)S(1)} %add.12), channel_id=1, source_target_pairs={{0,25},{1,24},{2,27},{3,26},{4,29},{5,28},{6,31},{7,30},{8,17},{9,... | collective-permute-start | bytes 36872 | tf_op jit(solution)/shard_map/ppermute | solution.py:310
  9.9 3.1 %collective-permute-start.2 = (f32[24,128]{1,0:T(8,128)S(1)}, f32[24,128]{1,0:T(8,128)S(1)}, u32[]{:S(2)}, u32[]{:S(2)}) collective-permute-start(f32[24,128]{1,0:T(8,128)S(1)} %add.12), channel_id=1, source_target_pairs={{0,17},{1,16},{2,19},{3,18},{4,21},{5,20},{6,23},{7,22},{8,25},{9,... | collective-permute-start | bytes 36872 | tf_op jit(solution)/shard_map/ppermute | solution.py:310
  10.2 3.1 %collective-permute-start.1 = (f32[24,128]{1,0:T(8,128)S(1)}, f32[24,128]{1,0:T(8,128)S(1)}, u32[]{:S(2)}, u32[]{:S(2)}) collective-permute-start(f32[24,128]{1,0:T(8,128)S(1)} %add.12), channel_id=1, source_target_pairs={{0,9},{1,8},{2,11},{3,10},{4,13},{5,12},{6,15},{7,14},{8,1},{9,0},... | collective-permute-start | bytes 36872 | tf_op jit(solution)/shard_map/ppermute | solution.py:310
  13.3 5.4 %collective-permute-start.7 = (f32[24,128]{1,0:T(8,128)S(1)}, f32[24,128]{1,0:T(8,128)S(1)}, u32[]{:S(2)}, u32[]{:S(2)}) collective-permute-start(f32[24,128]{1,0:T(8,128)S(1)} %add_add_fusion._.band_ref), channel_id=1, source_target_pairs={{0,3},{1,2},{2,5},{3,4},{4,7},{5,6},{6,1},{7,0},{8,11},{9,10},{10,... | collective-permute-start | bytes 36872 | tf_op jit(solution)/shard_map/ppermute | solution.py:310
  13.4 5.3 %collective-permute-start.6 = (f32[24,128]{1,0:T(8,128)S(1)}, f32[24,128]{1,0:T(8,128)S(1)}, u32[]{:S(2)}, u32[]{:S(2)}) collective-permute-start(f32[24,128]{1,0:T(8,128)S(1)} %add_add_fusion._.band_ref), channel_id=1, source_target_pairs={{0,7},{1,6},{2,1},{3,0},{4,3},{5,2},{6,5},{7,4},{8,15},{9,14},{10,... | collective-permute-start | bytes 36872 | tf_op jit(solution)/shard_map/ppermute | solution.py:310
  18.0 0.8 %copy-start = (f32[104,128]{1,0:T(8,128)S(1)}, f32[104,128]{1,0:T(8,128)}, u32[]{:S(2)}) copy-start(f32[104,128]{1,0:T(8,128)} %constant.2.clone.table_ref) | copy-start | bytes 159748
  19.7 4.9 %collective-permute-start.9 = (f32[8,128]{1,0:T(8,128)S(1)}, f32[8,128]{1,0:T(8,128)S(1)}, u32[]{:S(2)}, u32[]{:S(2)}) collective-permute-start(f32[8,128]{1,0:T(8,128)S(1)} %get-tuple-element.9.own_ref), channel_id=1, source_target_pairs={{0,7},{1,2},{2,1},{3,4},{4,3},{5,6},{6,5},{7,0},{8,15},{9,10},{10,... | collective-permute-start | bytes 12296 | tf_op jit(solution)/shard_map/ppermute | solution.py:366
  23.0 1.5 %collective-permute-start.8 = (f32[8,128]{1,0:T(8,128)S(1)}, f32[8,128]{1,0:T(8,128)S(1)}, u32[]{:S(2)}, u32[]{:S(2)}) collective-permute-start(f32[8,128]{1,0:T(8,128)S(1)} %get-tuple-element.9.own_ref), channel_id=1, source_target_pairs={{0,1},{1,0},{2,3},{3,2},{4,5},{5,4},{6,7},{7,6},{8,9},{9,8},{10,11... | collective-permute-start | bytes 12296 | tf_op jit(solution)/shard_map/ppermute | solution.py:367
  23.0 1.5 %copy-start.1 = (s32[1,512]{1,0:T(1,128)S(1)}, s32[1,512]{1,0:T(1,128)}, u32[]{:S(2)}) copy-start(s32[1,512]{1,0:T(1,128)} %coupling_ref.1) | copy-start | bytes 6148
